TPU v7x, 256 devices: a whole 4x4x8 slice. The times are simulated.
256 devices in a mesh: node: 4 (over z_lo), tile: 8 (over x, core), slab: 8 (over y, z_hi).
Axes of the slice: x: 4, y: 4, z: 8 (z_hi: 2, z_lo: 4; z = z_hi * 4 + z_lo), core: 2. Of those that a mesh axis runs over, the one named last changes fastest.
Arguments:
- start_state: float32 [5, 128, 128, 128], P(None, 'tile', 'slab'), may hold values from -1.5 to 3.5, as said below
- iterate: float32 [4, 5, 128, 128, 128], P('node', None, 'tile', 'slab'), may hold values from -1.8 to 3.8
- wall_flags: int32 [2, 128, 128], P(None, 'tile'), may hold values 0 or 1
- reg_index: int32 [1], replicated, may hold values from 0 to 7
Outputs:
- new_iterate: float32 [4, 5, 128, 128, 128], P('node', None, 'tile', 'slab')
Inputs may be any that keep to these rules, and one draw needn't show every extreme that they name: Concentration lies in 0.05 to 0.45 and shear rate is positive in start_state.
All inputs are finite; a program needn't handle non-finite values. No bound on the sum of `wall_flags` on one device may be relied on, other than what follows from the above.
Results may differ from a plain program's by a relative error of at most 0.0001.
Values sent between devices are 32-bit elements; how exact they have to be, the bound alone decides.
No kernel may reach another device: no remote copies, remote signals or barrier semaphores. Data moves between devices by JAX's collectives and lax.ppermute only.
A program may use at most 64 MiB of HBM per device.

v0:
```python
import jax
import jax.numpy as jnp
import numpy as np
from jax import lax
from jax.sharding import PartitionSpec as P

SWEEPS = 2


step_length = 0.2


def padded_2(x, sides, width):
    for axis, dim in sides:
        size, length = (lax.axis_size(axis), x.shape[dim])
        up = [(i, (i + 1) % size) for i in range(size - 1)]
        down = [(j, i) for i, j in up]
        last = lax.slice_in_dim(x, length - width, length, axis=dim)
        first = lax.slice_in_dim(x, 0, width, axis=dim)
        before = lax.ppermute(last, axis, up)
        after = lax.ppermute(first, axis, down)
        x = jnp.concatenate([before, x, after], axis=dim)
    return x


def quadrature_table():
    points = [0.25, 0.5, 0.75, 1.0]
    table = np.zeros((4, 4))
    for column in range(4):
        coeffs = [1.0]
        divisor = 1.0
        for other in range(4):
            if other != column:
                other_point = points[other]
                widened = [0.0] * (len(coeffs) + 1)
                for power, value in enumerate(coeffs):
                    widened[power + 1] += value
                    widened[power] -= other_point * value
                coeffs = widened
                divisor *= points[column] - other_point
        for line_index in range(4):
            position = points[line_index]
            total = 0.0
            for power, value in enumerate(coeffs):
                total += value * position ** (power + 1) / (power + 1)
            table[line_index, column] = total / divisor
    return table


def center(field):
    return field[1:-1, 1:-1, 1:-1]


def ddx(field):
    return 0.5 * (field[2:, 1:-1, 1:-1] - field[:-2, 1:-1, 1:-1])


def ddy(field):
    return 0.5 * (field[1:-1, 2:, 1:-1] - field[1:-1, :-2, 1:-1])


def ddz(field):
    return 0.5 * (field[1:-1, 1:-1, 2:] - field[1:-1, 1:-1, :-2])


def laplace(field):
    middle = center(field)
    return (
        field[2:, 1:-1, 1:-1]
        + field[:-2, 1:-1, 1:-1]
        + field[1:-1, 2:, 1:-1]
        + field[1:-1, :-2, 1:-1]
        + field[1:-1, 1:-1, 2:]
        + field[1:-1, 1:-1, :-2]
        - 6.0 * middle
    )


def gradient_dot(first, second):
    return ddx(first) * ddx(second) + ddy(first) * ddy(second) + ddz(first) * ddz(second)


def tendency(padded, exponent):
    concen = padded[0]
    shear = padded[1]
    stream = padded[2]
    normal = padded[3]
    spanwise = padded[4]
    regular = jnp.power(shear * shear + 0.25, 0.5 * exponent)
    flux_q = concen * regular
    viscous = 0.08 * (1.0 + 2.5 * concen + 6.2 * concen * concen) * regular
    stress = 0.5 * concen * concen * regular
    along = center(stream)
    across = center(normal)
    depth = center(spanwise)

    def carry_term(field):
        return along * ddx(field) + across * ddy(field) + depth * ddz(field)

    def diffuse(field):
        return center(viscous) * laplace(field) + gradient_dot(viscous, field)

    d_concen = -carry_term(concen) + 0.3 * (
        center(concen) * laplace(flux_q) + gradient_dot(concen, flux_q)
    )
    strain = ddy(stream) ** 2 + ddy(spanwise) ** 2 + ddx(normal) ** 2 + ddz(normal) ** 2
    d_shear = 2.0 * (jnp.sqrt(strain + 0.25) - center(shear))
    d_stream = -carry_term(stream) + diffuse(stream) + 0.5
    d_normal = -carry_term(normal) + diffuse(normal) - ddy(stress)
    d_span = -carry_term(spanwise) + diffuse(spanwise)
    return jnp.stack([d_concen, d_shear, d_stream, d_normal, d_span])


def ghost_row(layer, flag):
    slip = 1.0 - 2.0 * flag.astype(jnp.float32)
    return jnp.stack(
        [
            layer[..., 0, :, :],
            layer[..., 1, :, :],
            layer[..., 2, :, :] * slip,
            -layer[..., 3, :, :],
            layer[..., 4, :, :] * slip,
        ],
        axis=-3,
    )


def fix_bounds(padded, flags):
    first_tile = lax.axis_index("tile") == 0
    last_tile = lax.axis_index("tile") == lax.axis_size("tile") - 1
    padded = padded.at[..., 0, :, :].set(
        jnp.where(first_tile, padded[..., 1, :, :], padded[..., 0, :, :])
    )
    padded = padded.at[..., -1, :, :].set(
        jnp.where(last_tile, padded[..., -2, :, :], padded[..., -1, :, :])
    )
    lower_wall = lax.axis_index("slab") == 0
    upper_wall = lax.axis_index("slab") == lax.axis_size("slab") - 1
    lower = ghost_row(padded[..., 1:-1, 1, 1:-1], flags[0])
    upper = ghost_row(padded[..., 1:-1, -2, 1:-1], flags[1])
    padded = padded.at[..., 1:-1, 0, 1:-1].set(
        jnp.where(lower_wall, lower, padded[..., 1:-1, 0, 1:-1])
    )
    return padded.at[..., 1:-1, -1, 1:-1].set(
        jnp.where(upper_wall, upper, padded[..., 1:-1, -1, 1:-1])
    )


def pad_local(state, wall_flags):
    padded = padded_2(state, (("tile", 1), ("slab", 2)), 1)
    padded = jnp.concatenate([padded[..., -1:], padded, padded[..., :1]], axis=-1)
    return fix_bounds(padded, wall_flags)


def shards(start_state, iterate, wall_flags, reg_index):
    exponent = 0.4 + 0.1 * reg_index[0].astype(jnp.float32)
    table = jnp.asarray(quadrature_table(), jnp.float32)
    own_node = lax.axis_index("node")
    own_row = lax.dynamic_slice_in_dim(table, own_node, 1, 0)[0]
    state = iterate[0]
    for sweep in range(SWEEPS):
        rate = tendency(pad_local(state, wall_flags), exponent)
        summed = jnp.tensordot(
            own_row,
            lax.all_gather(rate[None], "node", axis=0, tiled=True),
            axes=1,
            precision=lax.Precision.HIGHEST,
        )
        state = start_state + step_length * summed
    return state[None]


def solution(mesh):
    return jax.shard_map(
        shards,
        mesh=mesh,
        in_specs=(
            P(None, "tile", "slab", None),
            P("node", None, "tile", "slab", None),
            P(None, "tile", None),
            P(),
        ),
        out_specs=P("node", None, "tile", "slab", None),
        check_vma=False,
    )
```

profile of v0, /device:TPU:37, one launch (start us, length us, event | category | flops | bytes accessed | tf_op | source)
XLA Modules:
  0.0 262.5 jit_solution(8337059759537456660)
XLA Ops:
  6.5 1.3 copy.277
  7.9 3.4 %collective-permute-start = (f32[5,1,16,128]{3,1,2,0:T(1,128)S(1)}, f32[5,1,16,128]{3,1,2,0:T(1,128)S(1)}, u32[]{:S(2)}, u32[]{:S(2)}) collective-permute-start(f32[5,1,16,128]{3,1,2,0:T(1,128)S(1)} %get-tuple-element.149), channel_id=1, source_target_pairs={{0,8},{8,16},{16,24},{24,32},{32,40},{40,48},{48,56},{1,9},{9,17},... | collective-permute-start | bytes 122888 | tf_op jit(solution)/shard_map/ppermute | solution.py:20
  11.3 1.9 collective-permute-start.1
  13.2 3.4 %collective-permute-done.1 = f32[5,1,16,128]{3,1,2,0:T(1,128)S(1)} collective-permute-done((f32[5,1,16,128]{3,1,2,0:T(1,128)S(1)}, f32[5,1,16,128]{3,1,2,0:T(1,128)S(1)}, u32[]{:S(2)}, u32[]{:S(2)}) %collective-permute-start.1) | collective-permute-done | bytes 40992 | tf_op jit(solution)/shard_map/ppermute | solution.py:21
  16.6 7.9 %collective-permute-start.2 = (f32[5,18,1,128]{3,1,2,0:T(8,128)S(1)}, f32[5,18,1,128]{3,1,2,0:T(8,128)S(1)}, u32[]{:S(2)}, u32[]{:S(2)}) collective-permute-start(f32[5,18,1,128]{3,1,2,0:T(8,128)S(1)} %get-tuple-element.145), channel_id=1, source_target_pairs={{0,1},{1,2},{2,3},{3,4},{4,5},{5,6},{6,7},{8,9},{9,10},{10,11},{11... | collective-permute-start | bytes 138248 | tf_op jit(solution)/shard_map/ppermute | solution.py:20
  24.6 1.3 collective-permute-start.3
  26.5 9.0 %collective-permute-done.3 = f32[5,18,1,128]{3,1,2,0:T(8,128)S(1)} collective-permute-done((f32[5,18,1,128]{3,1,2,0:T(8,128)S(1)}, f32[5,18,1,128]{3,1,2,0:T(8,128)S(1)}, u32[]{:S(2)}, u32[]{:S(2)}) %collective-permute-start.3) | collective-permute-done | bytes 46112 | tf_op jit(solution)/shard_map/ppermute | solution.py:21
  35.6 0.2 pad_maximum_fusion.2
  35.7 0.4 fusion.97
  36.1 1.3 pad_maximum_fusion
  37.5 3.7 %scatter.26 = f32[5,18,18,130]{3,1,2,0:T(8,128)S(1)} dynamic-update-slice(f32[5,18,18,130]{3,1,2,0:T(8,128)S(1)} %pad_maximum_fusion, f32[5,1,18,130]{3,1,2,0:T(1,128)S(1)} %broadcast_select_fusion.3, s32[]{:T(128)} %constant.237.clone.1, s32[]{:T(128)} %constant.237.clone.1, s32[]{:T(128)} %constant.237.clone.1, s32[]{:T(128)} %constant.237.clone.1) | dynamic-update-slice | bytes 93604 | tf_op jit(solution)/shard_map/scatter | solution.py:131
  41.3 3.7 %scatter.29 = f32[5,18,18,130]{3,1,2,0:T(8,128)S(1)} dynamic-update-slice(f32[5,18,18,130]{3,1,2,0:T(8,128)S(1)} %scatter.26, f32[5,1,18,130]{3,1,2,0:T(1,128)S(1)} %broadcast_select_fusion.1, s32[]{:T(128)} %constant.237.clone.1, s32[]{:T(128)} %constant.241.clone.1, s32[]{:T(128)} %constant.237.clone.1, s32[]{:T(128)} %constant.237.clone.1) | dynamic-update-slice | bytes 93604 | tf_op jit(solution)/shard_map/scatter | solution.py:134
  45.3 2.1 scatter.30
  47.5 2.1 scatter.31
  49.7 0.2 slice_bitcast_fusion.5
  49.9 0.1 copy.278
  50.0 0.6 fusion.10
  50.6 0.1 copy_multiply_fusion.1
  50.7 0.2 fusion.9
  50.9 0.6 slice_subtract_fusion.15
  51.6 0.3 fusion.102
  51.9 0.3 subtract_multiply_fusion.4
  52.2 0.4 multiply_add_fusion
  52.6 0.5 slice_multiply_fusion.2
  53.1 0.2 fusion.101
  53.3 0.1 fusion.42
  53.4 0.4 fusion.38
  53.8 0.4 bitcast_dynamic-update-slice_fusion.2
  54.2 0.8 copy-done.2
  55.0 0.2 all-gather.7.cloned.1.call-start
  55.3 55.4 %all-gather.5.cloned.1.call-done = f32[20,16,16,128]{3,2,1,0:T(8,128)} async-done(((f32[5,16,16,128]{3,2,1,0:T(8,128)}), f32[20,16,16,128]{3,2,1,0:T(8,128)}) %all-gather.5.cloned.1.call-update) | async-done | bytes 2621456 | tf_op jit(solution)/shard_map/all_gather | solution.py:165
  110.7 7.9 %fusion.2 = f32[1,5,16,16,128]{4,0,3,2,1:T(1,128)S(1)} fusion(f32[4,5,16,16,128]{4,3,2,1,0:T(8,128)} %bitcast.162, f32[4,4]{1,0:T(4,128)S(1)} %copy-done.5, s32[]{:T(128)S(6)} %select_n.55), kind=kOutput, calls=%fused_computation.2 | convolution fusion | flops 7864320 | bytes 3277316 | tf_op jit(solution)/shard_map/dot_general | solution.py:163
  118.6 0.4 fusion.6
  119.1 3.4 %collective-permute-start.4 = (f32[5,1,16,128]{3,1,2,0:T(1,128)S(1)}, f32[5,1,16,128]{3,1,2,0:T(1,128)S(1)}, u32[]{:S(2)}, u32[]{:S(2)}) collective-permute-start(f32[5,1,16,128]{3,1,2,0:T(1,128)S(1)} %get-tuple-element.147), channel_id=1, source_target_pairs={{0,8},{8,16},{16,24},{24,32},{32,40},{40,48},{48,56},{1,9},{9,17},... | collective-permute-start | bytes 122888 | tf_op jit(solution)/shard_map/ppermute | solution.py:20
  122.5 1.9 collective-permute-start.5
  124.4 3.4 %collective-permute-done.5 = f32[5,1,16,128]{3,1,2,0:T(1,128)S(1)} collective-permute-done((f32[5,1,16,128]{3,1,2,0:T(1,128)S(1)}, f32[5,1,16,128]{3,1,2,0:T(1,128)S(1)}, u32[]{:S(2)}, u32[]{:S(2)}) %collective-permute-start.5) | collective-permute-done | bytes 40992 | tf_op jit(solution)/shard_map/ppermute | solution.py:21
  127.8 5.3 %collective-permute-start.6 = (f32[5,18,1,128]{3,1,2,0:T(8,128)S(1)}, f32[5,18,1,128]{3,1,2,0:T(8,128)S(1)}, u32[]{:S(2)}, u32[]{:S(2)}) collective-permute-start(f32[5,18,1,128]{3,1,2,0:T(8,128)S(1)} %get-tuple-element.143), channel_id=1, source_target_pairs={{0,1},{1,2},{2,3},{3,4},{4,5},{5,6},{6,7},{8,9},{9,10},{10,11},{11... | collective-permute-start | bytes 138248 | tf_op jit(solution)/shard_map/ppermute | solution.py:20
  133.1 1.5 collective-permute-start.7
  134.6 8.2 %collective-permute-done.7 = f32[5,18,1,128]{3,1,2,0:T(8,128)S(1)} collective-permute-done((f32[5,18,1,128]{3,1,2,0:T(8,128)S(1)}, f32[5,18,1,128]{3,1,2,0:T(8,128)S(1)}, u32[]{:S(2)}, u32[]{:S(2)}) %collective-permute-start.7) | collective-permute-done | bytes 46112 | tf_op jit(solution)/shard_map/ppermute | solution.py:21
  142.9 0.2 pad_maximum_fusion.3
  143.0 0.4 fusion.96
  143.4 1.3 pad_maximum_fusion.1
  144.8 3.7 %scatter.34 = f32[5,18,18,130]{3,1,2,0:T(8,128)S(1)} dynamic-update-slice(f32[5,18,18,130]{3,1,2,0:T(8,128)S(1)} %pad_maximum_fusion.1, f32[5,1,18,130]{3,1,2,0:T(1,128)S(1)} %broadcast_select_fusion.2, s32[]{:T(128)} %constant.237.clone.1, s32[]{:T(128)} %constant.237.clone.1, s32[]{:T(128)} %constant.237.clone.1, s32[]{:T(128)} %constant.237.clone.1) | dynamic-update-slice | bytes 93604 | tf_op jit(solution)/shard_map/scatter | solution.py:131
  148.5 1.4 copy-done
  149.9 2.2 copy.84
  152.1 0.1 fusion.93
  152.3 0.2 fusion.94
  152.4 0.2 broadcast_select_fusion.5
  152.6 14.8 %scatter.36 = f32[5,18,18,130]{3,2,1,0:T(8,128)S(1)} dynamic-update-slice(f32[5,18,18,130]{3,2,1,0:T(8,128)S(1)} %copy_dynamic-update-slice_fusion.3, f32[5,16,1,128]{3,2,1,0:T(1,128)S(1)} %broadcast_select_fusion.5, s32[]{:T(128)} %constant.237.clone.1, s32[]{:T(128)} %constant.244.clone.1, s32[]{:T(128)} %constant.237.clone.1, s32[]{:T(128)} %constant.244.clone.1) | dynamic-update-slice | bytes 81924 | tf_op jit(solution)/shard_map/scatter | solution.py:141
  167.4 0.2 broadcast_select_fusion.4
  167.5 15.0 %scatter.39 = f32[5,18,18,130]{3,2,1,0:T(8,128)S(1)} dynamic-update-slice(f32[5,18,18,130]{3,2,1,0:T(8,128)S(1)} %scatter.36, f32[5,16,1,128]{3,2,1,0:T(1,128)S(1)} %broadcast_select_fusion.4, s32[]{:T(128)} %constant.237.clone.1, s32[]{:T(128)} %constant.244.clone.1, s32[]{:T(128)} %constant.241.clone.1, s32[]{:T(128)} %constant.244.clone.1) | dynamic-update-slice | bytes 81924 | tf_op jit(solution)/shard_map/scatter | solution.py:144
  182.6 0.5 fusion.14
  183.1 0.1 slice_bitcast_fusion
  183.7 0.2 fusion.100
  183.9 0.5 fusion.31
  184.4 0.4 fusion.25
  184.8 0.5 bitcast_dynamic-update-slice_fusion.1
  185.4 0.6 fusion.19
  186.0 0.5 bitcast_dynamic-update-slice_fusion
  186.5 0.8 copy-done.3
  187.4 58.9 %all-gather.7.cloned.1.call-done = f32[20,16,16,128]{3,2,1,0:T(8,128)} async-done(((f32[5,16,16,128]{3,2,1,0:T(8,128)}), f32[20,16,16,128]{3,2,1,0:T(8,128)}) %all-gather.7.cloned.1.call-update) | async-done | bytes 2621456 | tf_op jit(solution)/shard_map/all_gather | solution.py:165
  246.3 7.9 %fusion = f32[1,5,16,16,128]{4,0,3,2,1:T(1,128)S(1)} fusion(f32[4,5,16,16,128]{4,3,2,1,0:T(8,128)} %bitcast.163, f32[4,4]{1,0:T(4,128)S(1)} %copy-done.5, s32[]{:T(128)S(6)} %select_n.55), kind=kOutput, calls=%fused_computation | convolution fusion | flops 7864320 | bytes 3277316 | tf_op jit(solution)/shard_map/dot_general | solution.py:163
  254.2 0.4 fusion.5
  254.6 1.0 copy.117
  (39 shorter events, 1.6 us)
Async XLA Ops:
  6.5 104.1 %all-gather.5.cloned.1.call-start = ((), (), s32[]{:S(2)}) async-start(), calls=%async_computation | async-start | bytes 3276800 | tf_op jit(solution)/shard_map/all_gather | solution.py:165
  7.9 5.3 %collective-permute-start = (f32[5,1,16,128]{3,1,2,0:T(1,128)S(1)}, f32[5,1,16,128]{3,1,2,0:T(1,128)S(1)}, u32[]{:S(2)}, u32[]{:S(2)}) collective-permute-start(f32[5,1,16,128]{3,1,2,0:T(1,128)S(1)} %get-tuple-element.149), channel_id=1, source_target_pairs={{0,8},{8,16},{16,24},{24,32},{32,40},{40,48},{48,56},{1,9},{9,17},... | collective-permute-start | bytes 122888 | tf_op jit(solution)/shard_map/ppermute | solution.py:20
  11.3 5.3 %collective-permute-start.1 = (f32[5,1,16,128]{3,1,2,0:T(1,128)S(1)}, f32[5,1,16,128]{3,1,2,0:T(1,128)S(1)}, u32[]{:S(2)}, u32[]{:S(2)}) collective-permute-start(f32[5,1,16,128]{3,1,2,0:T(1,128)S(1)} %get-tuple-element.150), channel_id=1, source_target_pairs={{8,0},{16,8},{24,16},{32,24},{40,32},{48,40},{56,48},{9,1},{17,9},... | collective-permute-start | bytes 122888 | tf_op jit(solution)/shard_map/ppermute | solution.py:21
  16.6 9.9 %collective-permute-start.2 = (f32[5,18,1,128]{3,1,2,0:T(8,128)S(1)}, f32[5,18,1,128]{3,1,2,0:T(8,128)S(1)}, u32[]{:S(2)}, u32[]{:S(2)}) collective-permute-start(f32[5,18,1,128]{3,1,2,0:T(8,128)S(1)} %get-tuple-element.145), channel_id=1, source_target_pairs={{0,1},{1,2},{2,3},{3,4},{4,5},{5,6},{6,7},{8,9},{9,10},{10,11},{11... | collective-permute-start | bytes 138248 | tf_op jit(solution)/shard_map/ppermute | solution.py:20
  24.6 11.0 %collective-permute-start.3 = (f32[5,18,1,128]{3,1,2,0:T(8,128)S(1)}, f32[5,18,1,128]{3,1,2,0:T(8,128)S(1)}, u32[]{:S(2)}, u32[]{:S(2)}) collective-permute-start(f32[5,18,1,128]{3,1,2,0:T(8,128)S(1)} %get-tuple-element.146), channel_id=1, source_target_pairs={{1,0},{2,1},{3,2},{4,3},{5,4},{6,5},{7,6},{9,8},{10,9},{11,10},{12... | collective-permute-start | bytes 138248 | tf_op jit(solution)/shard_map/ppermute | solution.py:21
  36.1 9.0 %copy-start.4 = (s32[2,16,128]{2,1,0:T(8,128)S(1)}, s32[2,16,128]{2,1,0:T(8,128)}, u32[]{:S(2)}) copy-start(s32[2,16,128]{2,1,0:T(8,128)} %param.23) | copy-start | bytes 49156
  53.2 57.4 %copy-start.5 = (f32[4,4]{1,0:T(4,128)S(1)}, f32[4,4]{1,0:T(4,128)}, u32[]{:S(2)}) copy-start(f32[4,4]{1,0:T(4,128)} %constant.256.clone) | copy-start | bytes 196
  54.2 0.8 copy-start.2
  54.2 64.4 %copy-start.1 = (f32[5,16,16,128]{3,2,1,0:T(8,128)S(1)}, f32[5,16,16,128]{3,2,1,0:T(8,128)}, u32[]{:S(2)}) copy-start(f32[5,16,16,128]{3,2,1,0:T(8,128)} %param.21) | copy-start | bytes 1966084
  55.0 191.2 %all-gather.7.cloned.1.call-start = ((), (), s32[]{:S(2)}) async-start(), calls=%async_computation.1 | async-start | bytes 3276800 | tf_op jit(solution)/shard_map/all_gather | solution.py:165
  119.1 5.3 %collective-permute-start.4 = (f32[5,1,16,128]{3,1,2,0:T(1,128)S(1)}, f32[5,1,16,128]{3,1,2,0:T(1,128)S(1)}, u32[]{:S(2)}, u32[]{:S(2)}) collective-permute-start(f32[5,1,16,128]{3,1,2,0:T(1,128)S(1)} %get-tuple-element.147), channel_id=1, source_target_pairs={{0,8},{8,16},{16,24},{24,32},{32,40},{40,48},{48,56},{1,9},{9,17},... | collective-permute-start | bytes 122888 | tf_op jit(solution)/shard_map/ppermute | solution.py:20
  122.5 5.3 %collective-permute-start.5 = (f32[5,1,16,128]{3,1,2,0:T(1,128)S(1)}, f32[5,1,16,128]{3,1,2,0:T(1,128)S(1)}, u32[]{:S(2)}, u32[]{:S(2)}) collective-permute-start(f32[5,1,16,128]{3,1,2,0:T(1,128)S(1)} %get-tuple-element.148), channel_id=1, source_target_pairs={{8,0},{16,8},{24,16},{32,24},{40,32},{48,40},{56,48},{9,1},{17,9},... | collective-permute-start | bytes 122888 | tf_op jit(solution)/shard_map/ppermute | solution.py:21
  127.8 6.8 %collective-permute-start.6 = (f32[5,18,1,128]{3,1,2,0:T(8,128)S(1)}, f32[5,18,1,128]{3,1,2,0:T(8,128)S(1)}, u32[]{:S(2)}, u32[]{:S(2)}) collective-permute-start(f32[5,18,1,128]{3,1,2,0:T(8,128)S(1)} %get-tuple-element.143), channel_id=1, source_target_pairs={{0,1},{1,2},{2,3},{3,4},{4,5},{5,6},{6,7},{8,9},{9,10},{10,11},{11... | collective-permute-start | bytes 138248 | tf_op jit(solution)/shard_map/ppermute | solution.py:20
  133.1 9.7 %collective-permute-start.7 = (f32[5,18,1,128]{3,1,2,0:T(8,128)S(1)}, f32[5,18,1,128]{3,1,2,0:T(8,128)S(1)}, u32[]{:S(2)}, u32[]{:S(2)}) collective-permute-start(f32[5,18,1,128]{3,1,2,0:T(8,128)S(1)} %get-tuple-element.144), channel_id=1, source_target_pairs={{1,0},{2,1},{3,2},{4,3},{5,4},{6,5},{7,6},{9,8},{10,9},{11,10},{12... | collective-permute-start | bytes 138248 | tf_op jit(solution)/shard_map/ppermute | solution.py:21
  148.5 1.4 copy-start
  186.5 0.8 copy-start.3
Sparse Core Ops, SparseCore 0:
  55.2 55.4 all-gather.4
  187.5 58.6 all-gather.6
where the time goes:
time: 265 us; the launch traced here: 262 us
  waiting for transfers between devices  138 us (52%)
  local copies, waits for them, and re-layouts  54.6 us (21%)
  starting transfers between devices  26.8 us (10%)
  matrix products  15.8 us (6%)
  between operations  14.6 us (6%)
  other arithmetic  12.3 us (5%)
    all_gather x2, waiting for transfers between devices, shards(): lax.all_gather(rate[None], 'node', axis=0, tiled=True)  114 us
    ppermute x4, waiting for transfers between devices, padded_2(): after = lax.ppermute(first, axis, down)  24 us
    ppermute x4, starting transfers between devices, padded_2(): before = lax.ppermute(last, axis, up)  20 us
    scatter x2, local copies, waits for them, and re-layouts, fix_bounds(): padded.at[..., 1:-1, -1, 1:-1]  17.2 us
    scatter x2, local copies, waits for them, and re-layouts, fix_bounds(): padded.at[..., 1:-1, 0, 1:-1]  16.9 us
    dot_general x2, matrix products, shards(): jnp.tensordot(own_row, lax.all_gather(rate[None], 'node', axis=0, tiled=T...  15.8 us
    scatter x3, local copies, waits for them, and re-layouts, fix_bounds(): padded.at[..., 0, :, :]  9.53 us
    ppermute x4, starting transfers between devices, padded_2(): after = lax.ppermute(first, axis, down)  6.65 us
  transfers between devices with their start and end apart: 10, of which 6 were waited for; matrix products, arithmetic and copies ran while one was open for 0% of the time, Pallas kernels for 0%

commit v1 on v0

v1 whole, which is shorter than its diff:
```python
import functools

import jax
import jax.numpy as jnp
import numpy as np
from jax import lax
from jax.experimental import pallas as pl
from jax.experimental.pallas import tpu as pltpu
from jax.sharding import PartitionSpec as P

STEP = 0.2
MAIN = 20
EDGE = 12
VMEM = pl.BlockSpec(memory_space=pltpu.VMEM)
SMEM = pl.BlockSpec(memory_space=pltpu.SMEM)


def quadrature_table():
    points = [0.25, 0.5, 0.75, 1.0]
    table = np.zeros((4, 4))
    for column in range(4):
        coeffs = [1.0]
        divisor = 1.0
        for other in range(4):
            if other != column:
                other_point = points[other]
                widened = [0.0] * (len(coeffs) + 1)
                for power, value in enumerate(coeffs):
                    widened[power + 1] += value
                    widened[power] -= other_point * value
                coeffs = widened
                divisor *= points[column] - other_point
        for line_index in range(4):
            position = points[line_index]
            total = 0.0
            for power, value in enumerate(coeffs):
                total += value * position ** (power + 1) / (power + 1)
            table[line_index, column] = total / divisor
    return table


def relative_table():
    table = np.asarray(quadrature_table(), np.float32) * np.float32(STEP)
    out = np.zeros((4, 4, 4), np.float32)
    for me in range(4):
        for a in range(4):
            for b in range(4):
                out[me, a, b] = table[me ^ a, me ^ b]
    return out.reshape(-1)


def iotas():
    sub = lax.broadcasted_iota(jnp.int32, (16, 128), 0)
    lane = lax.broadcasted_iota(jnp.int32, (16, 128), 1)
    return sub, lane


def derived(c, g, power):
    r = jnp.exp(power * jnp.log(g * g + 0.25))
    q = c * r
    eta = (0.08 + 0.2 * c + 0.496 * (c * c)) * r
    return q, eta, 0.5 * c * q


def rate(cen, lm, lp, sm, sp, zm, zp, lead_x):
    def diffs(f):
        dl = lp(f) - lm(f)
        ds = sp(f) - sm(f)
        return (dl, ds) if lead_x else (ds, dl)

    def grads(f):
        lo, hi, a, b, n, m = lm(f), lp(f), sm(f), sp(f), zm(f), zp(f)
        x, y = (hi - lo, b - a) if lead_x else (b - a, hi - lo)
        return x, y, m - n, (lo + hi) + (a + b) + (n + m)

    c, g, u, v, w, eta = cen(0), cen(1), cen(2), cen(3), cen(4), cen(6)
    hu, hv, hw = 0.5 * u, 0.5 * v, 0.5 * w
    qx, qy, qz, qsum = grads(5)
    cx, cy, cz, _ = grads(0)
    dc = 0.3 * c * (qsum - 6.0 * cen(5)) + (0.075 * qx - hu) * cx + (0.075 * qy - hv) * cy + (0.075 * qz - hw) * cz
    ex, ey, ez, _ = grads(6)
    ax, ay, az = 0.25 * ex - hu, 0.25 * ey - hv, 0.25 * ez - hw
    ux, uy, uz, usum = grads(2)
    du = eta * (usum - 6.0 * u) + ax * ux + ay * uy + az * uz + 0.5
    vx, vy, vz, vsum = grads(3)
    dv = eta * (vsum - 6.0 * v) + ax * vx + ay * vy + az * vz - 0.5 * diffs(7)[1]
    wx, wy, wz, wsum = grads(4)
    dw = eta * (wsum - 6.0 * w) + ax * wx + ay * wy + az * wz
    strain = uy * uy + wy * wy + vx * vx + vz * vz
    dg = jnp.sqrt(strain + 1.0) - 2.0 * g
    return dc, dg, du, dv, dw


def swap_blocks(tiles, axis, block, index):
    size = 4 * block
    low = index < 2 * block
    even = (index // block) % 2 == 0
    roll = lambda t, k: pltpu.roll(t, k, axis)
    a0, a1, a2, a3 = tiles
    lo0 = jnp.where(low, a0, roll(a2, 2 * block))
    hi0 = jnp.where(low, roll(a0, 2 * block), a2)
    lo1 = jnp.where(low, a1, roll(a3, 2 * block))
    hi1 = jnp.where(low, roll(a1, 2 * block), a3)
    out = []
    for p, q in ((lo0, lo1), (hi0, hi1)):
        out.append(jnp.where(even, p, roll(q, block)))
        out.append(jnp.where(even, roll(p, size - block), q))
    return out


def edges():
    me = lax.axis_index("node")
    t, s = lax.axis_index("tile"), lax.axis_index("slab")
    return me, t == 0, t == lax.axis_size("tile") - 1, s == 0, s == lax.axis_size("slab") - 1


def pick(tiles, me):
    out = tiles[3]
    for q in range(3):
        out = jnp.where(me == q, tiles[q], out)
    return out


def pack_z_edge(z_ref, f, xq, rows, lane):
    place = 4 * f + xq
    spot = lane % 32 == place
    for g in range(4):
        z_ref[g] = jnp.where(spot, pltpu.roll(rows[g], place + 1, 1), z_ref[g])
        z_ref[4 + g] = jnp.where(spot, pltpu.roll(rows[g], place + 96, 1), z_ref[4 + g])


def first_kernel(reg, s_ref, w_ref, slip_ref, m0, m1, m2, m3, wq_ref, wz_ref, slipq_ref, der, packed, zs):
    me = lax.axis_index("node")
    sub, lane = iotas()
    power = 0.2 + 0.05 * reg[0].astype(jnp.float32)

    def derive(x, _):
        q, eta, s = derived(s_ref[0, x], s_ref[1, x], power)
        der[0, x], der[1, x], der[2, x] = q, eta, s
        return _

    lax.fori_loop(0, 16, derive, 0)
    zs[...] = jnp.zeros_like(zs)

    def column(xq, _):
        rows = []
        for g in range(4):
            x = 4 * g + xq
            lo = jnp.maximum(x - 1, 0)
            hi = jnp.minimum(x + 1, 15)
            at = lambda f, r: s_ref[f, r] if f < 5 else der[f - 5, r]
            rows.append(rate(
                lambda f: at(f, x), lambda f: at(f, lo), lambda f: at(f, hi),
                lambda f: pltpu.roll(at(f, x), 1, 0), lambda f: pltpu.roll(at(f, x), 15, 0),
                lambda f: pltpu.roll(at(f, x), 1, 1), lambda f: pltpu.roll(at(f, x), 127, 1), True))
        for f in range(5):
            out = swap_blocks([rows[g][f] for g in range(4)], 1, 32, lane)
            for q in range(4):
                packed[q, f * 4 + xq] = out[q]
            own = [w_ref[f, 4 * g + xq] for g in range(4)]
            wq_ref[f * 4 + xq] = pick(swap_blocks(own, 1, 32, lane), me)
            pack_z_edge(zs, f, xq, own, lane)
        return _

    lax.fori_loop(0, 4, column, 0)
    for r, m in enumerate((m0, m1, m2, m3)):
        m[...] = packed[me ^ r]
    for side in range(2):
        wz_ref[side] = pick(swap_blocks([zs[4 * side + g] for g in range(4)], 1, 32, lane), me)
    zero = jnp.zeros((16, 128), jnp.float32)
    tiles = swap_blocks([zero, slip_ref[0], slip_ref[1], zero], 0, 4, sub)
    slipq_ref[...] = pick(swap_blocks(tiles, 1, 32, lane), me)


def slab_kernel(s_ref, lo_ref, hi_ref, wq_ref, up_ref, down_ref):
    _, t0, t7, _, _ = edges()
    for f in range(5):
        for ref, ys, y in ((up_ref, (14, 15), 15), (down_ref, (0, 1), 0)):
            for k in range(2):
                ref[f, pl.ds(16 * k, 16), :] = s_ref[f, pl.ds(ys[k], 16, stride=16), :]
            ref[f, pl.ds(32, 1), :] = jnp.where(
                t0, s_ref[f, pl.ds(y, 1), :], lo_ref[pl.ds((f * 3 + 1) * 16 + y, 1), :])
            ref[f, pl.ds(33, 1), :] = jnp.where(
                t7, s_ref[f, pl.ds(240 + y, 1), :], hi_ref[pl.ds(f * 48 + y, 1), :])
            for xq in range(4):
                ref[f, pl.ds(34 + xq, 1), :] = wq_ref[f * 4 + xq, pl.ds(y, 1), :]
            ref[f, pl.ds(38, 2), :] = jnp.zeros((2, 128), jnp.float32)


def edge_kernel(reg, s_ref, lo_ref, hi_ref, below_ref, above_ref, slip_ref, wq_ref, wz_ref,
                e0, e1, e2, e3, wxy_ref, ext, yh, band, packed, zs, edge):
    me, t0, t7, s0, s7 = edges()
    sub, lane = iotas()
    power = 0.2 + 0.05 * reg[0].astype(jnp.float32)

    for f in range(5):
        lo = lambda r: lo_ref[pl.ds((f * 3 + r) * 16, 16), :]
        hi = lambda r: hi_ref[pl.ds((f * 3 + r) * 16, 16), :]
        first, last = s_ref[f, pl.ds(0, 16), :], s_ref[f, pl.ds(240, 16), :]
        ext[f, 0] = lo(0)
        ext[f, 1] = jnp.where(t0, first, lo(1))
        ext[f, 18] = jnp.where(t7, last, hi(0))
        ext[f, 19] = hi(1)
        for x in range(16):
            ext[f, x + 2] = s_ref[f, pl.ds(16 * x, 16), :]

    def derive(x, _):
        q, eta, s = derived(ext[0, x], ext[1, x], power)
        ext[5, x], ext[6, x], ext[7, x] = q, eta, s
        return _

    lax.fori_loop(0, 20, derive, 0)

    for side in range(2):
        ref = (below_ref, above_ref)[side]
        near = 16 if side == 0 else 0
        y = 0 if side == 0 else 15
        wall = (s0, s7)[side]
        slip = slip_ref[side]
        slip_lo = lo_ref[pl.ds(240 + side, 1), :]
        slip_hi = hi_ref[pl.ds(240 + side, 1), :]
        for f in range(5):
            def ghost(value, flag):
                return -value if f == 3 else value * flag if f in (2, 4) else value

            mine = s_ref[f, pl.ds(y, 16, stride=16), :]
            yh[f, side, pl.ds(0, 16), :] = jnp.where(wall, ghost(mine, slip), ref[f, pl.ds(near, 16), :])
            yh[f, side, pl.ds(16, 1), :] = jnp.where(
                wall, ghost(ext[f, 1, pl.ds(y, 1), :], slip_lo), ref[f, pl.ds(32, 1), :])
            yh[f, side, pl.ds(17, 1), :] = jnp.where(
                wall, ghost(ext[f, 18, pl.ds(y, 1), :], slip_hi), ref[f, pl.ds(33, 1), :])
            yh[f, side, pl.ds(18, 6), :] = jnp.zeros((6, 128), jnp.float32)
            far = 0 if side == 0 else 16
            band[f, side, 0] = ref[f, pl.ds(far, 16), :]
            band[f, side, 1] = ref[f, pl.ds(near, 16), :]
            band[f, side, 2] = mine
        q, eta, s = derived(yh[0, side], yh[1, side], power)
        yh[5, side], yh[6, side], yh[7, side] = q, eta, s
        for k in range(3):
            q, eta, s = derived(band[0, side, k], band[1, side, k], power)
            band[5, side, k], band[6, side, k], band[7, side, k] = q, eta, s

    def row(x, place):
        def below(f):
            return jnp.where(sub == 0, yh[f, 0, pl.ds(place, 1), :], pltpu.roll(ext[f, x], 1, 0))

        def above(f):
            return jnp.where(sub == 15, yh[f, 1, pl.ds(place, 1), :], pltpu.roll(ext[f, x], 15, 0))

        return rate(
            lambda f: ext[f, x], lambda f: ext[f, x - 1], lambda f: ext[f, x + 1], below, above,
            lambda f: pltpu.roll(ext[f, x], 1, 1), lambda f: pltpu.roll(ext[f, x], 127, 1), True)

    zs[...] = jnp.zeros_like(zs)

    def column(xq, _):
        rows = [row(4 * g + xq + 2, 4 * g + xq) for g in range(4)]
        for f in range(5):
            own = [rows[g][f] for g in range(4)]
            out = swap_blocks(own, 1, 32, lane)
            for q in range(4):
                packed[q, f * 4 + xq] = out[q]
            pack_z_edge(zs, f, xq, own, lane)
        return _

    lax.fori_loop(0, 4, column, 0)
    for side in range(2):
        out = swap_blocks([zs[4 * side + g] for g in range(4)], 1, 32, lane)
        for q in range(4):
            edge[q, 10 + side] = out[q]

    lower, upper = row(1, 16), row(18, 17)
    for f in range(5):
        for q in range(4):
            x_edge = jnp.where(
                lane < 32, packed[q, f * 4],
                jnp.where(lane < 64, pltpu.roll(lower[f], (32 * (1 - q)) % 128, 1),
                          jnp.where(lane < 96, pltpu.roll(upper[f], (32 * (2 - q)) % 128, 1), packed[q, f * 4 + 3])))
            edge[q, f] = x_edge

    def band_rate(side):
        def lo(f):
            return jnp.where(sub == 0, yh[f, side, pl.ds(16, 1), :], pltpu.roll(band[f, side, 1], 1, 0))

        def hi(f):
            return jnp.where(sub == 15, yh[f, side, pl.ds(17, 1), :], pltpu.roll(band[f, side, 1], 15, 0))

        before, after = (0, 2) if side == 0 else (2, 0)
        return rate(
            lambda f: band[f, side, 1], lambda f: band[f, side, before], lambda f: band[f, side, after], lo, hi,
            lambda f: pltpu.roll(band[f, side, 1], 1, 1), lambda f: pltpu.roll(band[f, side, 1], 127, 1), False)

    lower, upper = band_rate(0), band_rate(1)
    zero = jnp.zeros((16, 128), jnp.float32)
    for f in range(5):
        tiles = swap_blocks([zero, lower[f], upper[f], zero], 0, 4, sub)
        out = swap_blocks(tiles, 1, 32, lane)
        for q in range(4):
            edge[q, 5 + f] = out[q]
            for xq in range(4):
                edge[q, 5 + f, pl.ds(xq, 1), :] = packed[q, f * 4 + xq, pl.ds(0, 1), :]
                edge[q, 5 + f, pl.ds(12 + xq, 1), :] = packed[q, f * 4 + xq, pl.ds(15, 1), :]
    for r, e in enumerate((e0, e1, e2, e3)):
        e[...] = edge[me ^ r]

    for f in range(5):
        a = pltpu.roll(lo_ref[pl.ds((f * 3 + 2) * 16, 16), :], (5 - me) % 4 * 32, 1)
        b = pltpu.roll(hi_ref[pl.ds((f * 3 + 2) * 16, 16), :], (6 - me) % 4 * 32, 1)
        wxy_ref[f] = jnp.where(
            lane < 32, wq_ref[f * 4], jnp.where(lane < 64, a, jnp.where(lane < 96, b, wq_ref[f * 4 + 3])))
        wxy_ref[5 + f, pl.ds(4, 4), :] = below_ref[f, pl.ds(34, 4), :]
        wxy_ref[5 + f, pl.ds(8, 4), :] = above_ref[f, pl.ds(34, 4), :]
        for xq in range(4):
            wxy_ref[5 + f, pl.ds(xq, 1), :] = wq_ref[f * 4 + xq, pl.ds(0, 1), :]
            wxy_ref[5 + f, pl.ds(12 + xq, 1), :] = wq_ref[f * 4 + xq, pl.ds(15, 1), :]
    for side in range(2):
        wxy_ref[10 + side] = wz_ref[side]


def second_kernel(reg, weights, a0, a1, a2, a3, b0, b1, b2, b3, wq_ref, wxy_ref, slipq_ref,
                  o0, o1, o2, o3, main, xh, yh, zh, rates):
    me, t0, t7, s0, s7 = edges()
    sub, lane = iotas()
    power = 0.2 + 0.05 * reg[0].astype(jnp.float32)
    slip = slipq_ref[...]
    at_lower = jnp.logical_and(jnp.logical_and(sub >= 4, sub < 8), s0)
    at_upper = jnp.logical_and(jnp.logical_and(sub >= 8, sub < 12), s7)
    arrived, edge = (a0, a1, a2, a3), (b0, b1, b2, b3)

    def node(m, _):
        weight = [weights[me * 16 + m * 4 + r] for r in range(4)]

        def mix(start, refs, k):
            out = start
            for r in range(4):
                out = out + weight[r] * refs[r][k]
            return out

        for f in range(5):
            xb = mix(wxy_ref[f], edge, f)
            yb = mix(wxy_ref[5 + f], edge, 5 + f)
            yh[f] = yb
            for xq in range(4):
                tile = mix(wq_ref[f * 4 + xq], arrived, f * 4 + xq)
                if xq == 0:
                    tile = jnp.where(lane < 32, xb, tile)
                if xq == 3:
                    tile = jnp.where(lane >= 96, xb, tile)
                tile = jnp.where(sub == 0, yh[f, pl.ds(xq, 1), :], tile)
                tile = jnp.where(sub == 15, yh[f, pl.ds(12 + xq, 1), :], tile)
                main[f, xq] = tile
            xh[f] = jnp.where(
                lane < 64, jnp.where(t0, xb, pltpu.roll(xb, 96, 1)), jnp.where(t7, xb, pltpu.roll(xb, 32, 1)))
            lower, upper = pltpu.roll(yb, 4, 0), pltpu.roll(yb, 12, 0)
            if f == 3:
                lower, upper = -lower, -upper
            if f in (2, 4):
                lower, upper = lower * slip, upper * slip
            yh[f] = jnp.where(at_lower, lower, jnp.where(at_upper, upper, yb))
        for xq in range(4):
            main[5, xq], main[6, xq], main[7, xq] = derived(main[0, xq], main[1, xq], power)
        xh[5], xh[6], xh[7] = derived(xh[0], xh[1], power)
        yh[5], yh[6], yh[7] = derived(yh[0], yh[1], power)
        for side in range(2):
            z = mix(wxy_ref[10 + side], edge, 10 + side)
            zh[0, side] = z
            q, eta, _s = derived(z, pltpu.roll(z, 124, 1), power)
            zh[1, side], zh[2, side] = q, eta
        for xq in range(4):
            def left(f):
                if xq > 0:
                    return main[f, xq - 1]
                return jnp.where(lane < 32, xh[f], pltpu.roll(main[f, 3], 32, 1))

            def right(f):
                if xq < 3:
                    return main[f, xq + 1]
                return jnp.where(lane >= 96, xh[f], pltpu.roll(main[f, 0], 96, 1))

            def below(f):
                return jnp.where(sub == 0, yh[f, pl.ds(4 + xq, 1), :], pltpu.roll(main[f, xq], 1, 0))

            def above(f):
                return jnp.where(sub == 15, yh[f, pl.ds(8 + xq, 1), :], pltpu.roll(main[f, xq], 15, 0))

            def spot(f):
                return (0, 4 * f + xq) if f < 5 else (f - 4, xq)

            def before(f):
                k, i = spot(f)
                return jnp.where(lane % 32 == 0, pltpu.roll(zh[k, 0], (128 - i) % 128, 1), pltpu.roll(main[f, xq], 1, 1))

            def after(f):
                k, i = spot(f)
                return jnp.where(lane % 32 == 31, pltpu.roll(zh[k, 1], 31 - i, 1), pltpu.roll(main[f, xq], 127, 1))

            out = rate(lambda f: main[f, xq], left, right, below, above, before, after, True)
            for f in range(5):
                rates[m, f * 4 + xq] = out[f]
        return _

    lax.fori_loop(0, 4, node, 0)
    weight = [[weights[me * 16 + m * 4 + r] for r in range(4)] for m in range(4)]

    def combine(k, _):
        have = [rates[r, k] for r in range(4)]
        for m, o in enumerate((o0, o1, o2, o3)):
            out = wq_ref[k]
            for r in range(4):
                out = out + weight[m][r] * have[r]
            o[k] = out
        return _

    lax.fori_loop(0, MAIN, combine, 0)


def last_kernel(r0, r1, r2, r3, out_ref, quarter):
    me = lax.axis_index("node")
    _, lane = iotas()
    for r, ref in enumerate((r0, r1, r2, r3)):
        quarter[me ^ r] = ref[...]

    def column(k, _):
        tiles = swap_blocks([quarter[q, k] for q in range(4)], 1, 32, lane)
        for g in range(4):
            out_ref[k // 4, 4 * g + k % 4] = tiles[g]
        return _

    lax.fori_loop(0, MAIN, column, 0)


def tiles_of(n):
    return jax.ShapeDtypeStruct((n, 16, 128), jnp.float32)


def shards(start_state, iterate, wall_flags, reg_index):
    state = iterate[0]
    flat = state.reshape(5, 256, 128)
    slip = 1.0 - 2.0 * wall_flags.astype(jnp.float32)
    size = lax.axis_size("tile")
    ring_up = [(i, (i + 1) % size) for i in range(size)]
    ring_down = [(j, i) for i, j in ring_up]
    params = pltpu.CompilerParams(vmem_limit_bytes=48 * 1024 * 1024)
    scratch = lambda *shape: pltpu.VMEM(shape + (16, 128), jnp.float32)

    def tile_message(a, b, w):
        rows = jnp.concatenate([state[:, a:b], start_state[:, w:w + 1]], axis=1).reshape(240, 128)
        return jnp.concatenate([rows, slip[:, w], jnp.zeros((6, 128), jnp.float32)], axis=0)

    from_lower = lax.ppermute(tile_message(14, 16, 15), "tile", ring_up)
    from_upper = lax.ppermute(tile_message(0, 2, 0), "tile", ring_down)

    m0, m1, m2, m3, wq, wz, slipq = pl.pallas_call(
        first_kernel,
        out_shape=[tiles_of(MAIN)] * 5 + [tiles_of(2), jax.ShapeDtypeStruct((16, 128), jnp.float32)],
        in_specs=[SMEM] + [VMEM] * 3,
        out_specs=[VMEM] * 7,
        scratch_shapes=[scratch(3, 16), scratch(4, MAIN), scratch(8)],
        compiler_params=params,
    )(reg_index, state, start_state, slip)

    slab_shape = jax.ShapeDtypeStruct((5, 40, 128), jnp.float32)
    up, down = pl.pallas_call(
        slab_kernel,
        out_shape=[slab_shape] * 2,
        in_specs=[VMEM] * 4,
        out_specs=[VMEM] * 2,
        compiler_params=params,
    )(flat, from_lower, from_upper, wq)
    from_below = lax.ppermute(up, "slab", ring_up)
    from_above = lax.ppermute(down, "slab", ring_down)

    xor = lambda r: [(i, i ^ r) for i in range(4)]
    arrived = [m0] + [lax.ppermute(m, "node", xor(r)) for r, m in ((1, m1), (2, m2), (3, m3))]

    e0, e1, e2, e3, wxy = pl.pallas_call(
        edge_kernel,
        out_shape=[tiles_of(EDGE)] * 5,
        in_specs=[SMEM] + [VMEM] * 8,
        out_specs=[VMEM] * 5,
        scratch_shapes=[
            scratch(8, 20), pltpu.VMEM((8, 2, 24, 128), jnp.float32), scratch(8, 2, 3),
            scratch(4, MAIN), scratch(8), scratch(4, EDGE)],
        compiler_params=params,
    )(reg_index, flat, from_lower, from_upper, from_below, from_above, slip, wq, wz)
    edge = [e0] + [lax.ppermute(e, "node", xor(r)) for r, e in ((1, e1), (2, e2), (3, e3))]

    weights = jnp.asarray(relative_table())
    outs = pl.pallas_call(
        second_kernel,
        out_shape=[tiles_of(MAIN)] * 4,
        in_specs=[SMEM] * 2 + [VMEM] * 11,
        out_specs=[VMEM] * 4,
        scratch_shapes=[scratch(8, 4), scratch(8), scratch(8), scratch(3, 2), scratch(4, MAIN)],
        compiler_params=params,
    )(reg_index, weights, *arrived, *edge, wq, wxy, slipq)
    back = [outs[0]] + [lax.ppermute(outs[r], "node", xor(r)) for r in (1, 2, 3)]

    result = pl.pallas_call(
        last_kernel,
        out_shape=jax.ShapeDtypeStruct((5, 16, 16, 128), jnp.float32),
        in_specs=[VMEM] * 4,
        out_specs=VMEM,
        scratch_shapes=[scratch(4, MAIN)],
        compiler_params=params,
    )(*back)
    return result[None]


def solution(mesh):
    return jax.shard_map(
        shards,
        mesh=mesh,
        in_specs=(
            P(None, "tile", "slab", None),
            P("node", None, "tile", "slab", None),
            P(None, "tile", None),
            P(),
        ),
        out_specs=P("node", None, "tile", "slab", None),
        check_vma=False,
    )
```

time: 265 us -> 75.5 us (0.28)
  waiting for transfers between devices: 138 us -> 37.1 us
  local copies, waits for them, and re-layouts: 54.6 us -> 2.61 us
  matrix products: 15.8 us -> 0 us
  Pallas kernels: 0 us -> 14.3 us
  between operations: 14.6 us -> 0.77 us
  other arithmetic: 12.3 us -> 0.84 us
  starting transfers between devices: 26.8 us -> 18.6 us
    all_gather x2 -> x0, waiting for transfers between devices: 114 us -> none  [shards(): lax.all_gather(rate[None], 'node', axis=0, tiled=True)]
    scatter x9 -> x0, local copies, waits for them, and re-layouts: 47.3 us -> none  [the longest x2 17.2 us: fix_bounds(): padded.at[..., 1:-1, -1, 1:-1]]
    dot_general x2 -> x0, matrix products: 15.8 us -> none  [shards(): jnp.tensordot(own_row, lax.all_gather(rate[None], 'node', axis=0, tiled=T...]
    pallas_call x0 -> x5, Pallas kernels: none -> 14.3 us  [the longest x1 4.38 us: shards(): pl.pallas_call(first_kernel, out_shape=[tiles_of(MAIN)] * 5 + [tiles_of(2...]
    ppermute x8 -> x13, waiting for transfers between devices: 24 us -> 37.1 us  [the longest x3 14.2 us: shards(): lax.ppermute(outs[r], 'node', xor(r))]
    ppermute x8 -> x13, starting transfers between devices: 26.6 us -> 18.6 us  [the longest x1 6.79 us: shards(): from_below = lax.ppermute(up, 'slab', ring_up)]
    unnamed x16 -> x6, local copies, waits for them, and re-layouts: 4.45 us -> 0.66 us
    concatenate x4 -> x2, other arithmetic: 2.92 us -> 0.12 us  [the longest x1 0.1 us: tile_message(): jnp.concatenate([rows, slip[:, w], jnp.zeros((6, 128), jnp.float32)], axi...]
  transfers between devices with their start and end apart: 10 -> 13, of which waited for: 6 -> 9; matrix products, arithmetic and copies ran while one was open for 0% -> 0% of each run, Pallas kernels for 0% -> 11%
where the time goes in v1:
time: 75.5 us; the launch traced here: 74.2 us
  waiting for transfers between devices  37.1 us (49%)
  starting transfers between devices  18.6 us (25%)
  Pallas kernels  14.3 us (19%)
  local copies, waits for them, and re-layouts  2.61 us (3%)
  other arithmetic  0.84 us (1%)
  between operations  0.77 us (1%)
    ppermute x3, waiting for transfers between devices, shards(): lax.ppermute(outs[r], 'node', xor(r))  14.2 us
    ppermute x3, waiting for transfers between devices, shards(): lax.ppermute(m, 'node', xor(r))  9.94 us
    ppermute x1, waiting for transfers between devices, shards(): from_below = lax.ppermute(up, 'slab', ring_up)  7.82 us
    ppermute x1, starting transfers between devices, shards(): from_below = lax.ppermute(up, 'slab', ring_up)  6.79 us
    pallas_call x1, Pallas kernels, shards(): pl.pallas_call(first_kernel, out_shape=[tiles_of(MAIN)] * 5 + [tiles_of(2...  4.38 us
    ppermute x3, waiting for transfers between devices, shards(): lax.ppermute(e, 'node', xor(r))  4.21 us
    pallas_call x1, Pallas kernels, shards(): pl.pallas_call(last_kernel, out_shape=jax.ShapeDtypeStruct((5, 16, 16, 12...  3.91 us
    pallas_call x1, Pallas kernels, shards(): pl.pallas_call(edge_kernel, out_shape=[tiles_of(EDGE)] * 5, in_specs=[SME...  3.6 us
  transfers between devices with their start and end apart: 13, of which 9 were waited for; matrix products, arithmetic and copies ran while one was open for 0% of the time, Pallas kernels for 11%

profile of v1, /device:TPU:37, one launch (start us, length us, event | category | flops | bytes accessed | tf_op | source)
XLA Modules:
  0.0 74.2 jit_solution(7097834578038375102)
XLA Ops:
  0.0 0.7 multiply_subtract_fusion.slip_ref
  0.7 0.8 %fusion.1 = (f32[5,1,16,128]{3,2,1,0:T(8,128)S(1)}, f32[5,1,16,128]{3,2,1,0:T(8,128)S(1)}) fusion(f32[5,16,16,128]{3,2,1,0:T(8,128)} %w_ref.1), kind=kLoop, calls=%fused_computation.6 | loop fusion | bytes 163840 | tf_op jit(solution)/shard_map/slice | solution.py:447
  1.5 0.0 copy-start
  1.5 0.0 copy-start.1
  1.6 1.0 %fusion = (f32[5,2,16,128]{3,2,1,0:T(8,128)S(1)}, f32[5,2,16,128]{3,2,1,0:T(8,128)S(1)}) fusion(f32[5,16,16,128]{3,2,1,0:T(8,128)} %bitcast.7), kind=kLoop, calls=%fused_computation.5 | loop fusion | bytes 327680 | tf_op jit(solution)/shard_map/slice | solution.py:447
  2.6 0.1 pad.7.clone
  2.7 0.1 maximum_maximum_fusion.1
  2.8 0.7 collective-permute-start.4
  3.5 1.1 %collective-permute-start.3 = (f32[248,128]{1,0:T(8,128)S(1)}, f32[248,128]{1,0:T(8,128)S(1)}, u32[]{:S(2)}, u32[]{:S(2)}) collective-permute-start(f32[248,128]{1,0:T(8,128)S(1)} %get-tuple-element.48), channel_id=1, source_target_pairs={{0,8},{8,16},{16,24},{24,32},{32,40},{40,48},{48,56},{56,0},{1,9},... | collective-permute-start | bytes 380936 | tf_op jit(solution)/shard_map/ppermute | solution.py:450
  5.2 0.0 copy-done
  5.2 0.0 copy-done.1
  5.2 4.4 %shard_map.55 = (f32[20,16,128]{2,1,0:T(8,128)S(1)}, f32[20,16,128]{2,1,0:T(8,128)S(1)}, f32[20,16,128]{2,1,0:T(8,128)S(1)}, f32[20,16,128]{2,1,0:T(8,128)S(1)},...) custom-call(s32[1]{0:T(128)S(6)} %copy.6.reg, f32[5,16,16,128]{3,2,1,0:T(8,128)S(1)} %bitcast.8, ...), custom_call_target="tpu_custom_call" | custom-call | tf_op jit(solution)/shard_map/pallas_call | solution.py:453
  9.6 0.1 collective-permute-start
  9.7 0.0 collective-permute-done.4.hi_ref
  9.7 0.0 collective-permute-done.3.lo_ref
  9.8 0.1 shard_map.56
  9.8 6.8 %collective-permute-start.5 = (f32[5,40,128]{2,1,0:T(8,128)S(1)}, f32[5,40,128]{2,1,0:T(8,128)S(1)}, u32[]{:S(2)}, u32[]{:S(2)}) collective-permute-start(f32[5,40,128]{2,1,0:T(8,128)S(1)} %get-tuple-element.28), channel_id=1, source_target_pairs={{0,1},{1,2},{2,3},{3,4},{4,5},{5,6},{6,7},{7,0},{8,9},{9,10},{10,1... | collective-permute-start | bytes 307208 | tf_op jit(solution)/shard_map/ppermute | solution.py:470
  16.6 2.5 %collective-permute-start.6 = (f32[5,40,128]{2,1,0:T(8,128)S(1)}, f32[5,40,128]{2,1,0:T(8,128)S(1)}, u32[]{:S(2)}, u32[]{:S(2)}) collective-permute-start(f32[5,40,128]{2,1,0:T(8,128)S(1)} %get-tuple-element.29), channel_id=1, source_target_pairs={{1,0},{2,1},{3,2},{4,3},{5,4},{6,5},{7,6},{0,7},{9,8},{10,9},{11,1... | collective-permute-start | bytes 307208 | tf_op jit(solution)/shard_map/ppermute | solution.py:471
  19.2 1.2 %collective-permute-start.1 = (f32[20,16,128]{2,1,0:T(8,128)S(1)}, f32[20,16,128]{2,1,0:T(8,128)S(1)}, u32[]{:S(2)}, u32[]{:S(2)}) collective-permute-start(f32[20,16,128]{2,1,0:T(8,128)S(1)} %get-tuple-element.25), channel_id=1, source_target_pairs={{0,128},{64,192},{128,0},{192,64},{1,129},{65,193},{129,1},{193,65... | collective-permute-start | bytes 491528 | tf_op jit(solution)/shard_map/ppermute | solution.py:474
  20.4 0.7 collective-permute-start.2
  21.1 7.8 %collective-permute-done.5.below_ref = f32[5,40,128]{2,1,0:T(8,128)S(1)} collective-permute-done((f32[5,40,128]{2,1,0:T(8,128)S(1)}, f32[5,40,128]{2,1,0:T(8,128)S(1)}, u32[]{:S(2)}, u32[]{:S(2)}) %collective-permute-start.5) | collective-permute-done | bytes 102432 | tf_op jit(solution)/shard_map/ppermute | solution.py:470
  28.9 1.0 %collective-permute-done.6.above_ref = f32[5,40,128]{2,1,0:T(8,128)S(1)} collective-permute-done((f32[5,40,128]{2,1,0:T(8,128)S(1)}, f32[5,40,128]{2,1,0:T(8,128)S(1)}, u32[]{:S(2)}, u32[]{:S(2)}) %collective-permute-start.6) | collective-permute-done | bytes 102432 | tf_op jit(solution)/shard_map/ppermute | solution.py:471
  29.9 3.6 %shard_map.57 = (f32[12,16,128]{2,1,0:T(8,128)S(1)}, f32[12,16,128]{2,1,0:T(8,128)S(1)}, f32[12,16,128]{2,1,0:T(8,128)S(1)}, f32[12,16,128]{2,1,0:T(8,128)S(1)}, f32[12,16,128]{2,1,0:T(8,128)S(1)}) custom-call(s32[1]{0:T(128)S(6)} %copy.6.reg, f32[5,256,128]{2,1,0:T(8,128)S(1)} %bitcast.10, f32[248,128]{1,0:T(8,128)S(1)} %collective-permute-done.3.lo_ref, ...), custom_call_target="tpu_custom_call" | custom-call | tf_op jit(solution)/shard_map/pallas_call | solution.py:476
  33.5 0.1 collective-permute-start.7
  33.6 1.9 %collective-permute-start.8 = (f32[12,16,128]{2,1,0:T(8,128)S(1)}, f32[12,16,128]{2,1,0:T(8,128)S(1)}, u32[]{:S(2)}, u32[]{:S(2)}) collective-permute-start(f32[12,16,128]{2,1,0:T(8,128)S(1)} %get-tuple-element.33), channel_id=1, source_target_pairs={{0,128},{64,192},{128,0},{192,64},{1,129},{65,193},{129,1},{193,65... | collective-permute-start | bytes 294920 | tf_op jit(solution)/shard_map/ppermute | solution.py:486
  35.5 0.0 collective-permute-done.a1
  35.5 0.7 collective-permute-start.9
  36.2 0.8 %collective-permute-done.1.a2 = f32[20,16,128]{2,1,0:T(8,128)S(1)} collective-permute-done((f32[20,16,128]{2,1,0:T(8,128)S(1)}, f32[20,16,128]{2,1,0:T(8,128)S(1)}, u32[]{:S(2)}, u32[]{:S(2)}) %collective-permute-start.1) | collective-permute-done | bytes 163872 | tf_op jit(solution)/shard_map/ppermute | solution.py:474
  37.0 9.2 %collective-permute-done.2.a3 = f32[20,16,128]{2,1,0:T(8,128)S(1)} collective-permute-done((f32[20,16,128]{2,1,0:T(8,128)S(1)}, f32[20,16,128]{2,1,0:T(8,128)S(1)}, u32[]{:S(2)}, u32[]{:S(2)}) %collective-permute-start.2) | collective-permute-done | bytes 163872 | tf_op jit(solution)/shard_map/ppermute | solution.py:474
  46.2 0.0 collective-permute-done.7.b1
  46.2 0.6 collective-permute-done.8.b2
  46.8 3.6 %collective-permute-done.9.b3 = f32[12,16,128]{2,1,0:T(8,128)S(1)} collective-permute-done((f32[12,16,128]{2,1,0:T(8,128)S(1)}, f32[12,16,128]{2,1,0:T(8,128)S(1)}, u32[]{:S(2)}, u32[]{:S(2)}) %collective-permute-start.9) | collective-permute-done | bytes 98336 | tf_op jit(solution)/shard_map/ppermute | solution.py:486
  50.4 0.0 copy-start.2
  50.4 0.7 copy-done.2
  51.0 2.4 %shard_map.58 = (f32[20,16,128]{2,1,0:T(8,128)S(1)}, f32[20,16,128]{2,1,0:T(8,128)S(1)}, f32[20,16,128]{2,1,0:T(8,128)S(1)}, f32[20,16,128]{2,1,0:T(8,128)S(1)}) custom-call(s32[1]{0:T(128)S(6)} %copy.6.reg, f32[64]{0:T(128)S(1)} %copy-done.2, f32[20,16,128]{2,1,0:T(8,128)S(1)} %get-tuple-element.23.a0, f32[20,16,128]{2,1,0:T(8,128)S(1)} %collective-permute-done.a1, ...), custom_call_target="tpu_custom_call" | custom-call | tf_op jit(solution)/shard_map/pallas_call | solution.py:489
  53.4 0.1 collective-permute-start.10
  53.5 1.9 %collective-permute-start.11 = (f32[20,16,128]{2,1,0:T(8,128)S(1)}, f32[20,16,128]{2,1,0:T(8,128)S(1)}, u32[]{:S(2)}, u32[]{:S(2)}) collective-permute-start(f32[20,16,128]{2,1,0:T(8,128)S(1)} %get-tuple-element.39), channel_id=1, source_target_pairs={{0,128},{64,192},{128,0},{192,64},{1,129},{65,193},{129,1},{193,65... | collective-permute-start | bytes 491528 | tf_op jit(solution)/shard_map/ppermute | solution.py:497
  55.4 0.7 collective-permute-start.12
  56.2 2.7 %collective-permute-done.10.r1 = f32[20,16,128]{2,1,0:T(8,128)S(1)} collective-permute-done((f32[20,16,128]{2,1,0:T(8,128)S(1)}, f32[20,16,128]{2,1,0:T(8,128)S(1)}, u32[]{:S(2)}, u32[]{:S(2)}) %collective-permute-start.10) | collective-permute-done | bytes 163872 | tf_op jit(solution)/shard_map/ppermute | solution.py:497
  58.9 4.0 %collective-permute-done.11.r2 = f32[20,16,128]{2,1,0:T(8,128)S(1)} collective-permute-done((f32[20,16,128]{2,1,0:T(8,128)S(1)}, f32[20,16,128]{2,1,0:T(8,128)S(1)}, u32[]{:S(2)}, u32[]{:S(2)}) %collective-permute-start.11) | collective-permute-done | bytes 163872 | tf_op jit(solution)/shard_map/ppermute | solution.py:497
  62.9 7.5 %collective-permute-done.12.r3 = f32[20,16,128]{2,1,0:T(8,128)S(1)} collective-permute-done((f32[20,16,128]{2,1,0:T(8,128)S(1)}, f32[20,16,128]{2,1,0:T(8,128)S(1)}, u32[]{:S(2)}, u32[]{:S(2)}) %collective-permute-start.12) | collective-permute-done | bytes 163872 | tf_op jit(solution)/shard_map/ppermute | solution.py:497
  70.3 3.9 %shard_map.59 = f32[5,16,16,128]{3,2,1,0:T(8,128)} custom-call(f32[20,16,128]{2,1,0:T(8,128)S(1)} %get-tuple-element.37.r0, f32[20,16,128]{2,1,0:T(8,128)S(1)} %collective-permute-done.10.r1, f32[20,16,128]{2,1,0:T(8,128)S(1)} %collective-permute-done.11.r2, f32[20,16,128]{2,1,0:T(8,128)S(1)} %collective-permute-done.12.r3), custom_call_target="tpu_custom_call" | custom-call | tf_op jit(solution)/shard_map/pallas_call | solution.py:499
  (3 shorter events, 0.0 us)
Async XLA Ops:
  1.5 3.7 %copy-start = (f32[1,5,16,16,128]{4,3,2,1,0:T(8,128)S(1)}, f32[1,5,16,16,128]{4,3,2,1,0:T(8,128)}, u32[]{:S(2)}) copy-start(f32[1,5,16,16,128]{4,3,2,1,0:T(8,128)} %param.6) | copy-start | bytes 1966084
  1.5 3.7 %copy-start.1 = (f32[5,16,16,128]{3,2,1,0:T(8,128)S(1)}, f32[5,16,16,128]{3,2,1,0:T(8,128)}, u32[]{:S(2)}) copy-start(f32[5,16,16,128]{3,2,1,0:T(8,128)} %w_ref.1) | copy-start | bytes 1966084
  2.8 6.9 %collective-permute-start.4 = (f32[248,128]{1,0:T(8,128)S(1)}, f32[248,128]{1,0:T(8,128)S(1)}, u32[]{:S(2)}, u32[]{:S(2)}) collective-permute-start(f32[248,128]{1,0:T(8,128)S(1)} %get-tuple-element.47), channel_id=1, source_target_pairs={{8,0},{16,8},{24,16},{32,24},{40,32},{48,40},{56,48},{0,56},{9,1},... | collective-permute-start | bytes 380936 | tf_op jit(solution)/shard_map/ppermute | solution.py:451
  3.5 6.2 %collective-permute-start.3 = (f32[248,128]{1,0:T(8,128)S(1)}, f32[248,128]{1,0:T(8,128)S(1)}, u32[]{:S(2)}, u32[]{:S(2)}) collective-permute-start(f32[248,128]{1,0:T(8,128)S(1)} %get-tuple-element.48), channel_id=1, source_target_pairs={{0,8},{8,16},{16,24},{24,32},{32,40},{40,48},{48,56},{56,0},{1,9},... | collective-permute-start | bytes 380936 | tf_op jit(solution)/shard_map/ppermute | solution.py:450
  9.6 25.9 %collective-permute-start = (f32[20,16,128]{2,1,0:T(8,128)S(1)}, f32[20,16,128]{2,1,0:T(8,128)S(1)}, u32[]{:S(2)}, u32[]{:S(2)}) collective-permute-start(f32[20,16,128]{2,1,0:T(8,128)S(1)} %get-tuple-element.24), channel_id=1, source_target_pairs={{0,64},{64,0},{128,192},{192,128},{1,65},{65,1},{129,193},{193,129... | collective-permute-start | bytes 491528 | tf_op jit(solution)/shard_map/ppermute | solution.py:474
  9.8 19.1 %collective-permute-start.5 = (f32[5,40,128]{2,1,0:T(8,128)S(1)}, f32[5,40,128]{2,1,0:T(8,128)S(1)}, u32[]{:S(2)}, u32[]{:S(2)}) collective-permute-start(f32[5,40,128]{2,1,0:T(8,128)S(1)} %get-tuple-element.28), channel_id=1, source_target_pairs={{0,1},{1,2},{2,3},{3,4},{4,5},{5,6},{6,7},{7,0},{8,9},{9,10},{10,1... | collective-permute-start | bytes 307208 | tf_op jit(solution)/shard_map/ppermute | solution.py:470
  16.6 13.3 %collective-permute-start.6 = (f32[5,40,128]{2,1,0:T(8,128)S(1)}, f32[5,40,128]{2,1,0:T(8,128)S(1)}, u32[]{:S(2)}, u32[]{:S(2)}) collective-permute-start(f32[5,40,128]{2,1,0:T(8,128)S(1)} %get-tuple-element.29), channel_id=1, source_target_pairs={{1,0},{2,1},{3,2},{4,3},{5,4},{6,5},{7,6},{0,7},{9,8},{10,9},{11,1... | collective-permute-start | bytes 307208 | tf_op jit(solution)/shard_map/ppermute | solution.py:471
  19.2 17.8 %collective-permute-start.1 = (f32[20,16,128]{2,1,0:T(8,128)S(1)}, f32[20,16,128]{2,1,0:T(8,128)S(1)}, u32[]{:S(2)}, u32[]{:S(2)}) collective-permute-start(f32[20,16,128]{2,1,0:T(8,128)S(1)} %get-tuple-element.25), channel_id=1, source_target_pairs={{0,128},{64,192},{128,0},{192,64},{1,129},{65,193},{129,1},{193,65... | collective-permute-start | bytes 491528 | tf_op jit(solution)/shard_map/ppermute | solution.py:474
  20.4 25.8 %collective-permute-start.2 = (f32[20,16,128]{2,1,0:T(8,128)S(1)}, f32[20,16,128]{2,1,0:T(8,128)S(1)}, u32[]{:S(2)}, u32[]{:S(2)}) collective-permute-start(f32[20,16,128]{2,1,0:T(8,128)S(1)} %get-tuple-element.26), channel_id=1, source_target_pairs={{0,192},{64,128},{128,64},{192,0},{1,193},{65,129},{129,65},{193,1... | collective-permute-start | bytes 491528 | tf_op jit(solution)/shard_map/ppermute | solution.py:474
  33.5 12.7 %collective-permute-start.7 = (f32[12,16,128]{2,1,0:T(8,128)S(1)}, f32[12,16,128]{2,1,0:T(8,128)S(1)}, u32[]{:S(2)}, u32[]{:S(2)}) collective-permute-start(f32[12,16,128]{2,1,0:T(8,128)S(1)} %get-tuple-element.32), channel_id=1, source_target_pairs={{0,64},{64,0},{128,192},{192,128},{1,65},{65,1},{129,193},{193,129... | collective-permute-start | bytes 294920 | tf_op jit(solution)/shard_map/ppermute | solution.py:486
  33.6 13.2 %collective-permute-start.8 = (f32[12,16,128]{2,1,0:T(8,128)S(1)}, f32[12,16,128]{2,1,0:T(8,128)S(1)}, u32[]{:S(2)}, u32[]{:S(2)}) collective-permute-start(f32[12,16,128]{2,1,0:T(8,128)S(1)} %get-tuple-element.33), channel_id=1, source_target_pairs={{0,128},{64,192},{128,0},{192,64},{1,129},{65,193},{129,1},{193,65... | collective-permute-start | bytes 294920 | tf_op jit(solution)/shard_map/ppermute | solution.py:486
  35.5 14.9 %collective-permute-start.9 = (f32[12,16,128]{2,1,0:T(8,128)S(1)}, f32[12,16,128]{2,1,0:T(8,128)S(1)}, u32[]{:S(2)}, u32[]{:S(2)}) collective-permute-start(f32[12,16,128]{2,1,0:T(8,128)S(1)} %get-tuple-element.34), channel_id=1, source_target_pairs={{0,192},{64,128},{128,64},{192,0},{1,193},{65,129},{129,65},{193,1... | collective-permute-start | bytes 294920 | tf_op jit(solution)/shard_map/ppermute | solution.py:486
  50.4 0.7 copy-start.2
  53.4 5.4 %collective-permute-start.10 = (f32[20,16,128]{2,1,0:T(8,128)S(1)}, f32[20,16,128]{2,1,0:T(8,128)S(1)}, u32[]{:S(2)}, u32[]{:S(2)}) collective-permute-start(f32[20,16,128]{2,1,0:T(8,128)S(1)} %get-tuple-element.38), channel_id=1, source_target_pairs={{0,64},{64,0},{128,192},{192,128},{1,65},{65,1},{129,193},{193,129... | collective-permute-start | bytes 491528 | tf_op jit(solution)/shard_map/ppermute | solution.py:497
  53.5 9.3 %collective-permute-start.11 = (f32[20,16,128]{2,1,0:T(8,128)S(1)}, f32[20,16,128]{2,1,0:T(8,128)S(1)}, u32[]{:S(2)}, u32[]{:S(2)}) collective-permute-start(f32[20,16,128]{2,1,0:T(8,128)S(1)} %get-tuple-element.39), channel_id=1, source_target_pairs={{0,128},{64,192},{128,0},{192,64},{1,129},{65,193},{129,1},{193,65... | collective-permute-start | bytes 491528 | tf_op jit(solution)/shard_map/ppermute | solution.py:497
  55.4 14.9 %collective-permute-start.12 = (f32[20,16,128]{2,1,0:T(8,128)S(1)}, f32[20,16,128]{2,1,0:T(8,128)S(1)}, u32[]{:S(2)}, u32[]{:S(2)}) collective-permute-start(f32[20,16,128]{2,1,0:T(8,128)S(1)} %get-tuple-element.40), channel_id=1, source_target_pairs={{0,192},{64,128},{128,64},{192,0},{1,193},{65,129},{129,65},{193,1... | collective-permute-start | bytes 491528 | tf_op jit(solution)/shard_map/ppermute | solution.py:497

commit v2 on v1

v2 whole, which is shorter than its diff:
```python
import jax
import jax.numpy as jnp
import numpy as np
from jax import lax
from jax.experimental import pallas as pl
from jax.experimental.pallas import tpu as pltpu
from jax.sharding import PartitionSpec as P

STEP = 0.2
MAIN = 20
EDGE = 12
VMEM = pl.BlockSpec(memory_space=pltpu.VMEM)
SMEM = pl.BlockSpec(memory_space=pltpu.SMEM)
ANY = pl.BlockSpec(memory_space=pl.ANY)
HBM = pl.BlockSpec(memory_space=pltpu.HBM)


def quadrature_table():
    points = [0.25, 0.5, 0.75, 1.0]
    table = np.zeros((4, 4))
    for column in range(4):
        coeffs = [1.0]
        divisor = 1.0
        for other in range(4):
            if other != column:
                other_point = points[other]
                widened = [0.0] * (len(coeffs) + 1)
                for power, value in enumerate(coeffs):
                    widened[power + 1] += value
                    widened[power] -= other_point * value
                coeffs = widened
                divisor *= points[column] - other_point
        for line_index in range(4):
            position = points[line_index]
            total = 0.0
            for power, value in enumerate(coeffs):
                total += value * position ** (power + 1) / (power + 1)
            table[line_index, column] = total / divisor
    return table


def relative_weights(me):
    table = np.asarray(quadrature_table(), np.float32) * np.float32(STEP)

    def entry(a, b):
        value = jnp.float32(table[3 ^ a, 3 ^ b])
        for node in range(3):
            value = jnp.where(me == node, jnp.float32(table[node ^ a, node ^ b]), value)
        return value

    return [[entry(a, b) for b in range(4)] for a in range(4)]


def iotas():
    sub = lax.broadcasted_iota(jnp.int32, (16, 128), 0)
    lane = lax.broadcasted_iota(jnp.int32, (16, 128), 1)
    return sub, lane


def derived(c, g, power):
    r = jnp.exp(power * jnp.log(g * g + 0.25))
    q = c * r
    eta = (0.08 + 0.2 * c + 0.496 * (c * c)) * r
    return q, eta, 0.5 * c * q


def rate(cen, lm, lp, sm, sp, zm, zp, lead_x):
    def diffs(f):
        dl = lp(f) - lm(f)
        ds = sp(f) - sm(f)
        return (dl, ds) if lead_x else (ds, dl)

    def grads(f):
        lo, hi, a, b, n, m = lm(f), lp(f), sm(f), sp(f), zm(f), zp(f)
        x, y = (hi - lo, b - a) if lead_x else (b - a, hi - lo)
        return x, y, m - n, (lo + hi) + (a + b) + (n + m)

    c, g, u, v, w, eta = cen(0), cen(1), cen(2), cen(3), cen(4), cen(6)
    hu, hv, hw = 0.5 * u, 0.5 * v, 0.5 * w
    qx, qy, qz, qsum = grads(5)
    cx, cy, cz, _ = grads(0)
    dc = 0.3 * c * (qsum - 6.0 * cen(5)) + (0.075 * qx - hu) * cx + (0.075 * qy - hv) * cy + (0.075 * qz - hw) * cz
    ex, ey, ez, _ = grads(6)
    ax, ay, az = 0.25 * ex - hu, 0.25 * ey - hv, 0.25 * ez - hw
    ux, uy, uz, usum = grads(2)
    du = eta * (usum - 6.0 * u) + ax * ux + ay * uy + az * uz + 0.5
    vx, vy, vz, vsum = grads(3)
    dv = eta * (vsum - 6.0 * v) + ax * vx + ay * vy + az * vz - 0.5 * diffs(7)[1]
    wx, wy, wz, wsum = grads(4)
    dw = eta * (wsum - 6.0 * w) + ax * wx + ay * wy + az * wz
    strain = uy * uy + wy * wy + vx * vx + vz * vz
    dg = jnp.sqrt(strain + 1.0) - 2.0 * g
    return dc, dg, du, dv, dw


def swap_blocks(tiles, axis, block, index):
    size = 4 * block
    low = index < 2 * block
    even = (index // block) % 2 == 0
    roll = lambda t, k: pltpu.roll(t, k, axis)
    a0, a1, a2, a3 = tiles
    lo0 = jnp.where(low, a0, roll(a2, 2 * block))
    hi0 = jnp.where(low, roll(a0, 2 * block), a2)
    lo1 = jnp.where(low, a1, roll(a3, 2 * block))
    hi1 = jnp.where(low, roll(a1, 2 * block), a3)
    out = []
    for p, q in ((lo0, lo1), (hi0, hi1)):
        out.append(jnp.where(even, p, roll(q, block)))
        out.append(jnp.where(even, roll(p, size - block), q))
    return out


def edges():
    me = lax.axis_index("node")
    t, s = lax.axis_index("tile"), lax.axis_index("slab")
    return me, t == 0, t == lax.axis_size("tile") - 1, s == 0, s == lax.axis_size("slab") - 1


def pick(tiles, me):
    out = tiles[3]
    for q in range(3):
        out = jnp.where(me == q, tiles[q], out)
    return out


def pack_z_edge(z_ref, f, xq, rows, lane):
    place = 4 * f + xq
    spot = lane % 32 == place
    for g in range(4):
        z_ref[g] = jnp.where(spot, pltpu.roll(rows[g], place + 1, 1), z_ref[g])
        z_ref[4 + g] = jnp.where(spot, pltpu.roll(rows[g], place + 96, 1), z_ref[4 + g])


def slip_of(flags):
    return 1.0 - 2.0 * flags.astype(jnp.float32)


def tile_kernel(s_ref, w_ref, flag_ref, _after, up_ref, down_ref):
    for ref, rows, edge in ((up_ref, (14, 15), 15), (down_ref, (0, 1), 0)):
        for f in range(5):
            ref[f] = s_ref[f, rows[0]]
            ref[5 + f] = s_ref[f, rows[1]]
            ref[10 + f] = w_ref[f, edge]
        ref[15] = jnp.zeros((16, 128), jnp.float32)
        for side in range(2):
            ref[15, pl.ds(side, 1), :] = slip_of(flag_ref[side, pl.ds(edge, 1), :])


def first_kernel(reg, s_ref, _after, m0, m1, m2, m3, der, packed):
    me = lax.axis_index("node")
    sub, lane = iotas()
    power = 0.2 + 0.05 * reg[0].astype(jnp.float32)

    def derive(k, _):
        x = pl.ds(4 * k, 4)
        der[0, x], der[1, x], der[2, x] = derived(s_ref[0, x], s_ref[1, x], power)
        return _

    lax.fori_loop(0, 4, derive, 0)

    def column(xq, _):
        rows = []
        for g in range(4):
            x = 4 * g + xq
            lo = jnp.maximum(x - 1, 0)
            hi = jnp.minimum(x + 1, 15)
            at = lambda f, r: s_ref[f, r] if f < 5 else der[f - 5, r]
            rows.append(rate(
                lambda f: at(f, x), lambda f: at(f, lo), lambda f: at(f, hi),
                lambda f: pltpu.roll(at(f, x), 1, 0), lambda f: pltpu.roll(at(f, x), 15, 0),
                lambda f: pltpu.roll(at(f, x), 1, 1), lambda f: pltpu.roll(at(f, x), 127, 1), True))
        for f in range(5):
            out = swap_blocks([rows[g][f] for g in range(4)], 1, 32, lane)
            for q in range(4):
                packed[q, f * 4 + xq] = out[q]
        return _

    lax.fori_loop(0, 4, column, 0)
    for r, m in enumerate((m0, m1, m2, m3)):
        m[...] = packed[me ^ r]


def start_kernel(w_ref, flag_ref, _after, wq_ref, wz_ref, slipq_ref, zs):
    me = lax.axis_index("node")
    sub, lane = iotas()
    zs[...] = jnp.zeros_like(zs)
    for xq in range(4):
        for f in range(5):
            own = [w_ref[f, 4 * g + xq] for g in range(4)]
            wq_ref[f * 4 + xq] = pick(swap_blocks(own, 1, 32, lane), me)
            pack_z_edge(zs, f, xq, own, lane)
    for side in range(2):
        wz_ref[side] = pick(swap_blocks([zs[4 * side + g] for g in range(4)], 1, 32, lane), me)
    slipq_ref[...] = pack_y_edge(slip_of(flag_ref[0]), slip_of(flag_ref[1]), me, sub, lane)


def pack_y_edge(lower, upper, me, sub, lane):
    zero = jnp.zeros((16, 128), jnp.float32)
    tiles = swap_blocks([zero, lower, upper, zero], 0, 4, sub)
    return pick(swap_blocks(tiles, 1, 32, lane), me)


def slab_kernel(s_hbm, w_hbm, up_ref, down_ref, rows, sems):
    me = lax.axis_index("node")
    sub, lane = iotas()
    copies = []
    for k, (ref, ys) in enumerate(((up_ref, (14, 15)), (down_ref, (0, 1)))):
        for r in range(2):
            copies.append(pltpu.make_async_copy(
                s_hbm.at[:, :, ys[r], :], ref.at[:, pl.ds(16 * r, 16), :], sems.at[2 * k + r]))
        copies.append(pltpu.make_async_copy(w_hbm.at[:, :, (15, 0)[k], :], rows.at[k], sems.at[4 + k]))
    for copy in copies:
        copy.start()
    copies[2].wait()
    copies[5].wait()
    for f in range(5):
        start = pack_y_edge(rows[1, f], rows[0, f], me, sub, lane)
        for ref, place in ((up_ref, 8), (down_ref, 4)):
            ref[f, pl.ds(32, 4), :] = start[place:place + 4]
            ref[f, pl.ds(36, 4), :] = jnp.zeros((4, 128), jnp.float32)
    for k in (0, 1, 3, 4):
        copies[k].wait()


def corner_kernel(below_ref, above_ref, up_ref, down_ref):
    for ref, x in ((up_ref, 15), (down_ref, 0)):
        ref[pl.ds(10, 6), :] = jnp.zeros((6, 128), jnp.float32)
        for f in range(5):
            ref[pl.ds(f, 1), :] = below_ref[f, pl.ds(16 + x, 1), :]
            ref[pl.ds(5 + f, 1), :] = above_ref[f, pl.ds(x, 1), :]


def fill_ext(ext, s_ref, lo_ref, hi_ref, rows, t0, t7):
    for f in range(5):
        ext[f, 0] = lo_ref[f]
        ext[f, 1] = jnp.where(t0, s_ref[f, pl.ds(0, 16), :], lo_ref[5 + f])
        ext[f, 18] = jnp.where(t7, s_ref[f, pl.ds(240, 16), :], hi_ref[f])
        ext[f, 19] = hi_ref[5 + f]
        for x in rows:
            ext[f, x + 2] = s_ref[f, pl.ds(16 * x, 16), :]


def inner_kernel(reg, s_ref, lo_ref, hi_ref, out_ref, ext, zs):
    _, t0, t7, _, _ = edges()
    sub, lane = iotas()
    power = 0.2 + 0.05 * reg[0].astype(jnp.float32)
    fill_ext(ext, s_ref, lo_ref, hi_ref, range(16), t0, t7)

    def derive(k, _):
        x = pl.ds(4 * k, 4)
        ext[5, x], ext[6, x], ext[7, x] = derived(ext[0, x], ext[1, x], power)
        return _

    lax.fori_loop(0, 5, derive, 0)
    zs[...] = jnp.zeros_like(zs)

    def column(xq, _):
        rows = []
        for g in range(4):
            x = 4 * g + xq + 2
            rows.append(rate(
                lambda f: ext[f, x], lambda f: ext[f, x - 1], lambda f: ext[f, x + 1],
                lambda f: pltpu.roll(ext[f, x], 1, 0), lambda f: pltpu.roll(ext[f, x], 15, 0),
                lambda f: pltpu.roll(ext[f, x], 1, 1), lambda f: pltpu.roll(ext[f, x], 127, 1), True))
        for f in range(5):
            own = [rows[g][f] for g in range(4)]
            pack_z_edge(zs, f, xq, own, lane)
            first, last = own[0], own[3]

            @pl.when(xq == 0)
            def _first():
                for q in range(4):
                    out_ref[q, f] = pltpu.roll(first, 32 * (4 - q) % 128, 1)

            @pl.when(xq == 3)
            def _last():
                for q in range(4):
                    out_ref[q, f] = jnp.where(lane < 32, out_ref[q, f], pltpu.roll(last, 32 * (3 - q), 1))
        return _

    lax.fori_loop(0, 4, column, 0)
    for side in range(2):
        out = swap_blocks([zs[4 * side + g] for g in range(4)], 1, 32, lane)
        for q in range(4):
            out_ref[q, 5 + side] = out[q]


def edge_kernel(reg, s_ref, lo_ref, hi_ref, below_ref, above_ref, clo_ref, chi_ref, flag_ref, inner_ref,
                e0, e1, e2, e3, ext, yh, band, edge):
    me, t0, t7, s0, s7 = edges()
    sub, lane = iotas()
    power = 0.2 + 0.05 * reg[0].astype(jnp.float32)
    fill_ext(ext, s_ref, lo_ref, hi_ref, (0, 15), t0, t7)
    for x in (pl.ds(0, 3), pl.ds(17, 3)):
        ext[5, x], ext[6, x], ext[7, x] = derived(ext[0, x], ext[1, x], power)

    for side in range(2):
        ref = (below_ref, above_ref)[side]
        near, far = ((16, 0), (0, 16))[side]
        y, inward = ((0, 1), (15, 14))[side]
        wall = (s0, s7)[side]
        slip = slip_of(flag_ref[side])
        slip_lo = lo_ref[15, pl.ds(side, 1), :]
        slip_hi = hi_ref[15, pl.ds(side, 1), :]
        for f in range(5):
            def ghost(value, flag):
                return -value if f == 3 else value * flag if f in (2, 4) else value

            mine = s_ref[f, pl.ds(y, 16, stride=16), :]
            yh[f, side, pl.ds(0, 16), :] = jnp.where(wall, ghost(mine, slip), ref[f, pl.ds(near, 16), :])
            yh[f, side, pl.ds(16, 1), :] = jnp.where(
                wall, ghost(ext[f, 1, pl.ds(y, 1), :], slip_lo),
                jnp.where(t0, ref[f, pl.ds(near, 1), :], clo_ref[pl.ds(5 * side + f, 1), :]))
            yh[f, side, pl.ds(17, 1), :] = jnp.where(
                wall, ghost(ext[f, 18, pl.ds(y, 1), :], slip_hi),
                jnp.where(t7, ref[f, pl.ds(near + 15, 1), :], chi_ref[pl.ds(5 * side + f, 1), :]))
            yh[f, side, pl.ds(18, 6), :] = jnp.zeros((6, 128), jnp.float32)
            band[f, side, 0] = ref[f, pl.ds(far, 16), :]
            band[f, side, 1] = ref[f, pl.ds(near, 16), :]
            band[f, side, 2] = mine
            band[f, side, 3] = s_ref[f, pl.ds(inward, 16, stride=16), :]
        yh[5, side], yh[6, side], yh[7, side] = derived(yh[0, side], yh[1, side], power)
        band[5, side], band[6, side], band[7, side] = derived(band[0, side], band[1, side], power)

    def row(x, place):
        def below(f):
            return jnp.where(sub == 0, yh[f, 0, pl.ds(place, 1), :], pltpu.roll(ext[f, x], 1, 0))

        def above(f):
            return jnp.where(sub == 15, yh[f, 1, pl.ds(place, 1), :], pltpu.roll(ext[f, x], 15, 0))

        return rate(
            lambda f: ext[f, x], lambda f: ext[f, x - 1], lambda f: ext[f, x + 1], below, above,
            lambda f: pltpu.roll(ext[f, x], 1, 1), lambda f: pltpu.roll(ext[f, x], 127, 1), True)

    lower, upper = row(1, 16), row(18, 17)
    for f in range(5):
        for q in range(4):
            edge[q, f] = jnp.where(
                jnp.logical_or(lane < 32, lane >= 96), inner_ref[q, f],
                jnp.where(lane < 64, pltpu.roll(lower[f], (32 * (1 - q)) % 128, 1),
                          pltpu.roll(upper[f], (32 * (2 - q)) % 128, 1)))

    def band_rate(side, k):
        y = 0 if side == 0 else 15
        left = (lambda f: yh[f, side, pl.ds(16, 1), :]) if k == 1 else (lambda f: ext[f, 1, pl.ds(y, 1), :])
        right = (lambda f: yh[f, side, pl.ds(17, 1), :]) if k == 1 else (lambda f: ext[f, 18, pl.ds(y, 1), :])

        def lo(f):
            return jnp.where(sub == 0, left(f), pltpu.roll(band[f, side, k], 1, 0))

        def hi(f):
            return jnp.where(sub == 15, right(f), pltpu.roll(band[f, side, k], 15, 0))

        outer = (lambda f: band[f, side, 0]) if k == 1 else (lambda f: yh[f, side, pl.ds(0, 16), :])
        inner = lambda f: band[f, side, k + 1]
        before, after = (outer, inner) if side == 0 else (inner, outer)
        return rate(
            lambda f: band[f, side, k], before, after, lo, hi,
            lambda f: pltpu.roll(band[f, side, k], 1, 1), lambda f: pltpu.roll(band[f, side, k], 127, 1), False)

    rows = [band_rate(0, 2), band_rate(0, 1), band_rate(1, 1), band_rate(1, 2)]
    zero = jnp.zeros((16, 128), jnp.float32)
    beside = [[zero, zero] for q in range(4)]
    for f in range(5):
        out = swap_blocks(swap_blocks([r[f] for r in rows], 0, 4, sub), 1, 32, lane)
        for q in range(4):
            edge[q, 5 + f] = out[q]
            for xq in range(4):
                place = 4 * f + xq
                spot = jnp.logical_and(lane % 32 == place, sub % 4 == xq)
                for side, to, shift in ((0, (q + 1) % 4, (place + 97) % 128), (1, (q + 3) % 4, place)):
                    beside[to][side] = jnp.where(spot, pltpu.roll(out[q], shift, 1), beside[to][side])
    for q in range(4):
        for side in range(2):
            b = beside[q][side]
            low = b + pltpu.roll(b, 15, 0)
            low = low + pltpu.roll(low, 14, 0)
            high = b + pltpu.roll(b, 1, 0)
            high = high + pltpu.roll(high, 2, 0)
            edge[q, 10 + side] = jnp.where(sub == 0, low, jnp.where(sub == 15, high, inner_ref[q, 5 + side]))
    for r, e in enumerate((e0, e1, e2, e3)):
        e[...] = edge[me ^ r]


def start_tiles_kernel(lo_ref, hi_ref, below_ref, above_ref, wq_ref, wz_ref, _after, wxy_ref):
    me = lax.axis_index("node")
    sub, lane = iotas()
    for f in range(5):
        a = pltpu.roll(lo_ref[10 + f], (5 - me) % 4 * 32, 1)
        b = pltpu.roll(hi_ref[10 + f], (6 - me) % 4 * 32, 1)
        wxy_ref[f] = jnp.where(
            lane < 32, wq_ref[f * 4], jnp.where(lane < 64, a, jnp.where(lane < 96, b, wq_ref[f * 4 + 3])))
        wxy_ref[5 + f, pl.ds(4, 4), :] = below_ref[f, pl.ds(32, 4), :]
        wxy_ref[5 + f, pl.ds(8, 4), :] = above_ref[f, pl.ds(32, 4), :]
        for xq in range(4):
            wxy_ref[5 + f, pl.ds(xq, 1), :] = wq_ref[f * 4 + xq, pl.ds(0, 1), :]
            wxy_ref[5 + f, pl.ds(12 + xq, 1), :] = wq_ref[f * 4 + xq, pl.ds(15, 1), :]
    for side in range(2):
        wxy_ref[10 + side] = wz_ref[side]


def second_kernel(reg, a0, a1, a2, a3, b0, b1, b2, b3, wq_ref, wxy_ref, slipq_ref,
                  o0, o1, o2, o3, main, xh, yh, zh, rates, table):
    me, t0, t7, s0, s7 = edges()
    sub, lane = iotas()
    power = 0.2 + 0.05 * reg[0].astype(jnp.float32)
    slip = slipq_ref[...]
    at_lower = jnp.logical_and(jnp.logical_and(sub >= 4, sub < 8), s0)
    at_upper = jnp.logical_and(jnp.logical_and(sub >= 8, sub < 12), s7)
    arrived, edge = (a0, a1, a2, a3), (b0, b1, b2, b3)
    weights = relative_weights(me)
    for m in range(4):
        for r in range(4):
            table[m * 4 + r] = weights[m][r]

    def node(m, _):
        weight = [table[m * 4 + r] for r in range(4)]

        def mix(start, refs, k):
            out = start
            for r in range(4):
                out = out + weight[r] * refs[r][k]
            return out

        for f in range(5):
            xb = mix(wxy_ref[f], edge, f)
            yb = mix(wxy_ref[5 + f], edge, 5 + f)
            yh[f] = yb
            for xq in range(4):
                tile = mix(wq_ref[f * 4 + xq], arrived, f * 4 + xq)
                if xq == 0:
                    tile = jnp.where(lane < 32, xb, tile)
                if xq == 3:
                    tile = jnp.where(lane >= 96, xb, tile)
                tile = jnp.where(sub == 0, yh[f, pl.ds(xq, 1), :], tile)
                tile = jnp.where(sub == 15, yh[f, pl.ds(12 + xq, 1), :], tile)
                main[f, xq] = tile
            xh[f] = jnp.where(
                lane < 64, jnp.where(t0, main[f, 0], pltpu.roll(xb, 96, 1)),
                jnp.where(t7, main[f, 3], pltpu.roll(xb, 32, 1)))
            lower, upper = pltpu.roll(yb, 4, 0), pltpu.roll(yb, 12, 0)
            if f == 3:
                lower, upper = -lower, -upper
            if f in (2, 4):
                lower, upper = lower * slip, upper * slip
            yh[f] = jnp.where(at_lower, lower, jnp.where(at_upper, upper, yb))
        for xq in range(4):
            main[5, xq], main[6, xq], main[7, xq] = derived(main[0, xq], main[1, xq], power)
        xh[5], xh[6], xh[7] = derived(xh[0], xh[1], power)
        yh[5], yh[6], yh[7] = derived(yh[0], yh[1], power)
        for side in range(2):
            z = mix(wxy_ref[10 + side], edge, 10 + side)
            zh[0, side] = z
            q, eta, _s = derived(z, pltpu.roll(z, 124, 1), power)
            zh[1, side], zh[2, side] = q, eta
        for xq in range(4):
            def left(f):
                if xq > 0:
                    return main[f, xq - 1]
                return jnp.where(lane < 32, xh[f], pltpu.roll(main[f, 3], 32, 1))

            def right(f):
                if xq < 3:
                    return main[f, xq + 1]
                return jnp.where(lane >= 96, xh[f], pltpu.roll(main[f, 0], 96, 1))

            def below(f):
                return jnp.where(sub == 0, yh[f, pl.ds(4 + xq, 1), :], pltpu.roll(main[f, xq], 1, 0))

            def above(f):
                return jnp.where(sub == 15, yh[f, pl.ds(8 + xq, 1), :], pltpu.roll(main[f, xq], 15, 0))

            def spot(f):
                return (0, 4 * f + xq) if f < 5 else (f - 4, xq)

            def before(f):
                k, i = spot(f)
                return jnp.where(lane % 32 == 0, pltpu.roll(zh[k, 0], (128 - i) % 128, 1), pltpu.roll(main[f, xq], 1, 1))

            def after(f):
                k, i = spot(f)
                return jnp.where(lane % 32 == 31, pltpu.roll(zh[k, 1], 31 - i, 1), pltpu.roll(main[f, xq], 127, 1))

            out = rate(lambda f: main[f, xq], left, right, below, above, before, after, True)
            for f in range(5):
                rates[m, f * 4 + xq] = out[f]
        return _

    lax.fori_loop(0, 4, node, 0)

    def combine(k, _):
        have = [rates[r, k] for r in range(4)]
        for m, o in enumerate((o0, o1, o2, o3)):
            out = wq_ref[k]
            for r in range(4):
                out = out + weights[m][r] * have[r]
            o[k] = out
        return _

    lax.fori_loop(0, MAIN, combine, 0)


def last_kernel(r0, r1, r2, r3, out_hbm, quarter, out, sems):
    me = lax.axis_index("node")
    _, lane = iotas()
    copies = []
    for f in range(5):
        for r, ref in enumerate((r0, r1, r2, r3)):
            quarter[me ^ r, pl.ds(4 * f, 4)] = ref[pl.ds(4 * f, 4)]
        for xq in range(4):
            tiles = swap_blocks([quarter[q, 4 * f + xq] for q in range(4)], 1, 32, lane)
            for g in range(4):
                out[f, 4 * g + xq] = tiles[g]
        copies.append(pltpu.make_async_copy(out.at[f], out_hbm.at[f], sems.at[f]))
        copies[f].start()
    for copy in copies:
        copy.wait()


def tiles_of(n):
    return jax.ShapeDtypeStruct((n, 16, 128), jnp.float32)


def shards(start_state, iterate, wall_flags, reg_index):
    state = iterate[0]
    flat = state.reshape(5, 256, 128)
    size = lax.axis_size("tile")
    ring_up = [(i, (i + 1) % size) for i in range(size)]
    ring_down = [(j, i) for i, j in ring_up]
    params = pltpu.CompilerParams(vmem_limit_bytes=32 * 1024 * 1024)
    scratch = lambda *shape: pltpu.VMEM(shape + (16, 128), jnp.float32)

    def call(kernel, ins, outs, scratch_shapes=(), place=VMEM):
        return pl.pallas_call(
            kernel, out_shape=outs, in_specs=ins, out_specs=[place] * len(outs),
            scratch_shapes=scratch_shapes, compiler_params=params)

    def exchange(tiles):
        out = [tiles[0]] + [None] * 3
        for r in (2, 3, 1):
            out[r] = lax.ppermute(tiles[r], "node", [(i, i ^ r) for i in range(4)])
        return out

    far = pltpu.with_memory_space_constraint
    slab_shape = jax.ShapeDtypeStruct((5, 40, 128), jnp.float32)
    slab_up, slab_down = call(
        slab_kernel, [HBM] * 2, [slab_shape] * 2, [scratch(2, 5), pltpu.SemaphoreType.DMA((6,))])(
        far(state, pltpu.HBM), far(start_state, pltpu.HBM))
    from_above = lax.ppermute(slab_down, "slab", ring_down)
    from_below = lax.ppermute(slab_up, "slab", ring_up)

    tile_up, tile_down = call(tile_kernel, [VMEM] * 3 + [ANY], [tiles_of(16)] * 2)(
        state, start_state, wall_flags, slab_up)
    from_lower = lax.ppermute(tile_up, "tile", ring_up)
    from_upper = lax.ppermute(tile_down, "tile", ring_down)

    rates = call(first_kernel, [SMEM, VMEM, ANY], [tiles_of(MAIN)] * 4, [scratch(3, 16), scratch(4, MAIN)])(
        reg_index, state, tile_up)
    arrived = exchange(rates)

    wq, wz, slipq = call(
        start_kernel, [VMEM, VMEM, ANY], [tiles_of(MAIN), tiles_of(2), jax.ShapeDtypeStruct((16, 128), jnp.float32)],
        [scratch(8)])(start_state, wall_flags, rates[1])

    inner, = call(
        inner_kernel, [SMEM] + [VMEM] * 3, [jax.ShapeDtypeStruct((4, 7, 16, 128), jnp.float32)],
        [scratch(8, 20), scratch(8)])(reg_index, flat, from_lower, from_upper)

    corner_shape = jax.ShapeDtypeStruct((16, 128), jnp.float32)
    corner_up, corner_down = call(corner_kernel, [VMEM] * 2, [corner_shape] * 2)(from_below, from_above)
    corner_lower = lax.ppermute(corner_up, "tile", ring_up)
    corner_upper = lax.ppermute(corner_down, "tile", ring_down)

    edge = call(
        edge_kernel, [SMEM] + [VMEM] * 9, [tiles_of(EDGE)] * 4,
        [scratch(8, 20), pltpu.VMEM((8, 2, 24, 128), jnp.float32), scratch(8, 2, 4), scratch(4, EDGE)])(
        reg_index, flat, from_lower, from_upper, from_below, from_above, corner_lower, corner_upper, wall_flags, inner)
    wxy, = call(start_tiles_kernel, [VMEM] * 6 + [ANY], [tiles_of(EDGE)])(
        from_lower, from_upper, from_below, from_above, wq, wz, edge[1])
    edge = exchange(edge)

    outs = call(
        second_kernel, [SMEM] + [VMEM] * 11, [tiles_of(MAIN)] * 4,
        [scratch(8, 4), scratch(8), scratch(8), scratch(3, 2), scratch(4, MAIN), pltpu.SMEM((16,), jnp.float32)])(
        reg_index, *arrived, *edge, wq, wxy, slipq)
    back = exchange(outs)

    result, = call(
        last_kernel, [VMEM] * 4, [jax.ShapeDtypeStruct((5, 16, 16, 128), jnp.float32)],
        [scratch(4, MAIN), scratch(5, 16), pltpu.SemaphoreType.DMA((5,))], HBM)(*back)
    return result[None]


def solution(mesh):
    return jax.shard_map(
        shards,
        mesh=mesh,
        in_specs=(
            P(None, "tile", "slab", None),
            P("node", None, "tile", "slab", None),
            P(None, "tile", None),
            P(),
        ),
        out_specs=P("node", None, "tile", "slab", None),
        check_vma=False,
    )
```

time: 75.5 us -> 63.2 us (0.84)
  waiting for transfers between devices: 37.1 us -> 21.9 us
  starting transfers between devices: 18.6 us -> 25 us
  local copies, waits for them, and re-layouts: 2.61 us -> 0.72 us
  other arithmetic: 0.84 us -> 0 us
  Pallas kernels: 14.3 us -> 13.5 us
    ppermute x13 -> x15, waiting for transfers between devices: 37.1 us -> 21.9 us  [the longest x9 18 us: exchange(): out[r] = lax.ppermute(tiles[r], 'node', [(i, i ^ r) for i in range(4)])]
    ppermute x13 -> x15, starting transfers between devices: 18.6 us -> 25 us  [the longest x9 11.7 us: exchange(): out[r] = lax.ppermute(tiles[r], 'node', [(i, i ^ r) for i in range(4)])]
    slice x3 -> x0, local copies, waits for them, and re-layouts: 1.87 us -> none  [the longest x1 1.05 us: tile_message(): state[:, a:b]]
    pallas_call x5 -> x10, Pallas kernels: 14.3 us -> 13.5 us  [the longest x1 3.11 us: shards(): call(inner_kernel, [SMEM] + [VMEM] * 3, [jax.ShapeDtypeStruct((4, 7, 16,...]
  transfers between devices with their start and end apart: 13 -> 15, of which waited for: 9 -> 7; matrix products, arithmetic and copies ran while one was open for 0% -> 0% of each run, Pallas kernels for 11% -> 14%
where the time goes in v2:
time: 63.2 us; the launch traced here: 62 us
  starting transfers between devices  25 us (40%)
  waiting for transfers between devices  21.9 us (35%)
  Pallas kernels  13.5 us (21%)
  between operations  0.8 us (1%)
  local copies, waits for them, and re-layouts  0.72 us (1%)
    ppermute x9, waiting for transfers between devices, exchange(): out[r] = lax.ppermute(tiles[r], 'node', [(i, i ^ r) for i in range(4)])  18 us
    ppermute x9, starting transfers between devices, exchange(): out[r] = lax.ppermute(tiles[r], 'node', [(i, i ^ r) for i in range(4)])  11.7 us
    ppermute x1, starting transfers between devices, shards(): from_above = lax.ppermute(slab_down, 'slab', ring_down)  8.54 us
    ppermute x1, waiting for transfers between devices, shards(): from_below = lax.ppermute(slab_up, 'slab', ring_up)  3.72 us
    pallas_call x1, Pallas kernels, shards(): call(inner_kernel, [SMEM] + [VMEM] * 3, [jax.ShapeDtypeStruct((4, 7, 16,...  3.11 us
    ppermute x1, starting transfers between devices, shards(): corner_lower = lax.ppermute(corner_up, 'tile', ring_up)  2.73 us
    pallas_call x1, Pallas kernels, shards(): call(start_kernel, [VMEM, VMEM, ANY], [tiles_of(MAIN), tiles_of(2), jax.S...  1.99 us
    pallas_call x1, Pallas kernels, shards(): call(second_kernel, [SMEM] + [VMEM] * 11, [tiles_of(MAIN)] * 4, [scratch(...  1.94 us
  transfers between devices with their start and end apart: 15, of which 7 were waited for; matrix products, arithmetic and copies ran while one was open for 0% of the time, Pallas kernels for 14%

profile of v2, /device:TPU:37, one launch (start us, length us, event | category | flops | bytes accessed | tf_op | source)
XLA Modules:
  0.0 62.0 jit_solution(781353036368565062)
XLA Ops:
  0.0 0.0 copy-start
  0.0 0.0 copy-start.1
  0.0 1.3 %shard_map.46 = (f32[5,40,128]{2,1,0:T(8,128)S(1)}, f32[5,40,128]{2,1,0:T(8,128)S(1)}) custom-call(f32[5,16,16,128]{3,2,1,0:T(8,128)} %bitcast.3, f32[5,16,16,128]{3,2,1,0:T(8,128)} %w_ref.3), custom_call_target="tpu_custom_call" | custom-call | tf_op jit(solution)/shard_map/pallas_call | solution.py:547
  1.3 8.5 %collective-permute-start.6 = (f32[5,40,128]{2,1,0:T(8,128)S(1)}, f32[5,40,128]{2,1,0:T(8,128)S(1)}, u32[]{:S(2)}, u32[]{:S(2)}) collective-permute-start(f32[5,40,128]{2,1,0:T(8,128)S(1)} %get-tuple-element.33), channel_id=1, source_target_pairs={{1,0},{2,1},{3,2},{4,3},{5,4},{6,5},{7,6},{0,7},{9,8},{10,9},{11,1... | collective-permute-start | bytes 307208 | tf_op jit(solution)/shard_map/ppermute | solution.py:550
  9.8 0.0 collective-permute-start.5
  10.5 0.0 copy-done
  10.5 0.0 copy-done.1
  10.5 0.0 copy-start.2
  10.5 0.7 %copy-done.2 = s32[2,16,128]{2,1,0:T(8,128)S(1)} copy-done((s32[2,16,128]{2,1,0:T(8,128)S(1)}, s32[2,16,128]{2,1,0:T(8,128)}, u32[]{:S(2)}) %copy-start.2) | copy-done | bytes 16408
  11.2 1.8 %shard_map.48 = (f32[20,16,128]{2,1,0:T(8,128)S(1)}, f32[20,16,128]{2,1,0:T(8,128)S(1)}, f32[20,16,128]{2,1,0:T(8,128)S(1)}, f32[20,16,128]{2,1,0:T(8,128)S(1)}) custom-call(s32[1]{0:T(128)S(6)} %copy.5.reg, f32[5,16,16,128]{3,2,1,0:T(8,128)S(1)} %bitcast.5, f32[16,16,128]{2,1,0:T(8,128)S(1)} %get-tuple-element.27._after), custom_call_target="tpu_custom_call" | custom-call | tf_op jit(solution)/shard_map/pallas_call | solution.py:558
  13.0 1.3 %collective-permute-start.1 = (f32[20,16,128]{2,1,0:T(8,128)S(1)}, f32[20,16,128]{2,1,0:T(8,128)S(1)}, u32[]{:S(2)}, u32[]{:S(2)}) collective-permute-start(f32[20,16,128]{2,1,0:T(8,128)S(1)} %get-tuple-element.30), channel_id=1, source_target_pairs={{0,128},{64,192},{128,0},{192,64},{1,129},{65,193},{129,1},{193,65... | collective-permute-start | bytes 491528 | tf_op jit(solution)/shard_map/ppermute | solution.py:542
  14.3 1.2 %collective-permute-start.4 = (f32[16,16,128]{2,1,0:T(8,128)S(1)}, f32[16,16,128]{2,1,0:T(8,128)S(1)}, u32[]{:S(2)}, u32[]{:S(2)}) collective-permute-start(f32[16,16,128]{2,1,0:T(8,128)S(1)} %get-tuple-element.32), channel_id=1, source_target_pairs={{8,0},{16,8},{24,16},{32,24},{40,32},{48,40},{56,48},{0,56},{9,1},... | collective-permute-start | bytes 393224 | tf_op jit(solution)/shard_map/ppermute | solution.py:556
  15.5 0.8 %collective-permute-start.3 = (f32[16,16,128]{2,1,0:T(8,128)S(1)}, f32[16,16,128]{2,1,0:T(8,128)S(1)}, u32[]{:S(2)}, u32[]{:S(2)}) collective-permute-start(f32[16,16,128]{2,1,0:T(8,128)S(1)} %get-tuple-element.27._after), channel_id=1, source_target_pairs={{0,8},{8,16},{16,24},{24,32},{32,40},{40,48},{48,56},{56,0},{1,9},... | collective-permute-start | bytes 393224 | tf_op jit(solution)/shard_map/ppermute | solution.py:555
  16.3 0.0 collective-permute-done.6.above_ref
  16.3 0.7 %collective-permute-start.2 = (f32[20,16,128]{2,1,0:T(8,128)S(1)}, f32[20,16,128]{2,1,0:T(8,128)S(1)}, u32[]{:S(2)}, u32[]{:S(2)}) collective-permute-start(f32[20,16,128]{2,1,0:T(8,128)S(1)} %get-tuple-element.31), channel_id=1, source_target_pairs={{0,192},{64,128},{128,64},{192,0},{1,193},{65,129},{129,65},{193,1... | collective-permute-start | bytes 491528 | tf_op jit(solution)/shard_map/ppermute | solution.py:542
  17.0 3.7 %collective-permute-done.5.below_ref = f32[5,40,128]{2,1,0:T(8,128)S(1)} collective-permute-done((f32[5,40,128]{2,1,0:T(8,128)S(1)}, f32[5,40,128]{2,1,0:T(8,128)S(1)}, u32[]{:S(2)}, u32[]{:S(2)}) %collective-permute-start.5) | collective-permute-done | bytes 102432 | tf_op jit(solution)/shard_map/ppermute | solution.py:551
  20.8 2.6 %collective-permute-start = (f32[20,16,128]{2,1,0:T(8,128)S(1)}, f32[20,16,128]{2,1,0:T(8,128)S(1)}, u32[]{:S(2)}, u32[]{:S(2)}) collective-permute-start(f32[20,16,128]{2,1,0:T(8,128)S(1)} %get-tuple-element.29._after), channel_id=1, source_target_pairs={{0,64},{64,0},{128,192},{192,128},{1,65},{65,1},{129,193},{193,129... | collective-permute-start | bytes 491528 | tf_op jit(solution)/shard_map/ppermute | solution.py:542
  23.3 0.0 collective-permute-done.4.hi_ref
  23.4 2.7 %collective-permute-start.7 = (f32[16,128]{1,0:T(8,128)S(1)}, f32[16,128]{1,0:T(8,128)S(1)}, u32[]{:S(2)}, u32[]{:S(2)}) collective-permute-start(f32[16,128]{1,0:T(8,128)S(1)} %get-tuple-element.34), channel_id=1, source_target_pairs={{0,8},{8,16},{16,24},{24,32},{32,40},{40,48},{48,56},{56,0},{1,9},... | collective-permute-start | bytes 24584 | tf_op jit(solution)/shard_map/ppermute | solution.py:572
  26.1 0.0 collective-permute-done.3.lo_ref
  26.1 0.0 collective-permute-start.8
  26.1 0.0 copy-start.3
  26.1 3.1 %shard_map.50.inner_ref = f32[4,7,16,128]{3,2,1,0:T(8,128)S(1)} custom-call(s32[1]{0:T(128)S(6)} %copy.5.reg, f32[5,256,128]{2,1,0:T(8,128)S(1)} %bitcast.6, f32[16,16,128]{2,1,0:T(8,128)S(1)} %collective-permute-done.3.lo_ref, f32[16,16,128]{2,1,0:T(8,128)S(1)} %collective-permute-done.4.hi_ref), custom_call_target="tpu_custom_call" | custom-call | tf_op jit(solution)/shard_map/pallas_call | solution.py:566
  29.2 0.0 collective-permute-done.7.clo_ref
  29.2 0.2 collective-permute-done.8.chi_ref
  29.5 0.0 copy-done.3
  29.5 1.5 %shard_map.51 = (f32[12,16,128]{2,1,0:T(8,128)S(1)}, f32[12,16,128]{2,1,0:T(8,128)S(1)}, f32[12,16,128]{2,1,0:T(8,128)S(1)}, f32[12,16,128]{2,1,0:T(8,128)S(1)}) custom-call(s32[1]{0:T(128)S(6)} %copy.5.reg, f32[5,256,128]{2,1,0:T(8,128)S(1)} %bitcast.7, f32[16,16,128]{2,1,0:T(8,128)S(1)} %collective-permute-done.3.lo_ref, ...), custom_call_target="tpu_custom_call" | custom-call | tf_op jit(solution)/shard_map/pallas_call | solution.py:575
  31.0 0.1 collective-permute-start.10
  31.1 1.1 %collective-permute-start.11 = (f32[12,16,128]{2,1,0:T(8,128)S(1)}, f32[12,16,128]{2,1,0:T(8,128)S(1)}, u32[]{:S(2)}, u32[]{:S(2)}) collective-permute-start(f32[12,16,128]{2,1,0:T(8,128)S(1)} %get-tuple-element.39), channel_id=1, source_target_pairs={{0,192},{64,128},{128,64},{192,0},{1,193},{65,129},{129,65},{193,1... | collective-permute-start | bytes 294920 | tf_op jit(solution)/shard_map/ppermute | solution.py:542
  32.2 0.0 collective-permute-done.1.a2
  32.2 2.4 %collective-permute-start.9 = (f32[12,16,128]{2,1,0:T(8,128)S(1)}, f32[12,16,128]{2,1,0:T(8,128)S(1)}, u32[]{:S(2)}, u32[]{:S(2)}) collective-permute-start(f32[12,16,128]{2,1,0:T(8,128)S(1)} %get-tuple-element.37._after), channel_id=1, source_target_pairs={{0,64},{64,0},{128,192},{192,128},{1,65},{65,1},{129,193},{193,129... | collective-permute-start | bytes 294920 | tf_op jit(solution)/shard_map/ppermute | solution.py:542
  34.6 2.0 %shard_map.52 = (f32[20,16,128]{2,1,0:T(8,128)S(1)}, f32[2,16,128]{2,1,0:T(8,128)S(1)}, f32[16,128]{1,0:T(8,128)S(1)}) custom-call(f32[5,16,16,128]{3,2,1,0:T(8,128)S(1)} %copy-done.1, s32[2,16,128]{2,1,0:T(8,128)S(1)} %copy-done.3, f32[20,16,128]{2,1,0:T(8,128)S(1)} %get-tuple-element.29._after), custom_call_target="tpu_custom_call" | custom-call | tf_op jit(solution)/shard_map/pallas_call | solution.py:562
  36.6 0.1 shard_map.53.wxy_ref
  36.7 0.0 collective-permute-done.2.a3
  36.8 0.0 collective-permute-done.a1
  36.8 1.9 %collective-permute-done.10.b2 = f32[12,16,128]{2,1,0:T(8,128)S(1)} collective-permute-done((f32[12,16,128]{2,1,0:T(8,128)S(1)}, f32[12,16,128]{2,1,0:T(8,128)S(1)}, u32[]{:S(2)}, u32[]{:S(2)}) %collective-permute-start.10) | collective-permute-done | bytes 98336 | tf_op jit(solution)/shard_map/ppermute | solution.py:542
  38.7 2.2 %collective-permute-done.11.b3 = f32[12,16,128]{2,1,0:T(8,128)S(1)} collective-permute-done((f32[12,16,128]{2,1,0:T(8,128)S(1)}, f32[12,16,128]{2,1,0:T(8,128)S(1)}, u32[]{:S(2)}, u32[]{:S(2)}) %collective-permute-start.11) | collective-permute-done | bytes 98336 | tf_op jit(solution)/shard_map/ppermute | solution.py:542
  40.9 0.0 collective-permute-done.9.b1
  40.9 1.9 %shard_map.54 = (f32[20,16,128]{2,1,0:T(8,128)S(1)}, f32[20,16,128]{2,1,0:T(8,128)S(1)}, f32[20,16,128]{2,1,0:T(8,128)S(1)}, f32[20,16,128]{2,1,0:T(8,128)S(1)}) custom-call(s32[1]{0:T(128)S(6)} %copy.5.reg, f32[20,16,128]{2,1,0:T(8,128)S(1)} %get-tuple-element.28.a0, f32[20,16,128]{2,1,0:T(8,128)S(1)} %collective-permute-done.a1, ...), custom_call_target="tpu_custom_call" | custom-call | tf_op jit(solution)/shard_map/pallas_call | solution.py:583
  42.9 0.1 collective-permute-start.12
  43.0 3.4 %collective-permute-start.13 = (f32[20,16,128]{2,1,0:T(8,128)S(1)}, f32[20,16,128]{2,1,0:T(8,128)S(1)}, u32[]{:S(2)}, u32[]{:S(2)}) collective-permute-start(f32[20,16,128]{2,1,0:T(8,128)S(1)} %get-tuple-element.45), channel_id=1, source_target_pairs={{0,128},{64,192},{128,0},{192,64},{1,129},{65,193},{129,1},{193,65... | collective-permute-start | bytes 491528 | tf_op jit(solution)/shard_map/ppermute | solution.py:542
  46.4 0.0 collective-permute-start.14
  46.4 0.8 %collective-permute-done.12.r1 = f32[20,16,128]{2,1,0:T(8,128)S(1)} collective-permute-done((f32[20,16,128]{2,1,0:T(8,128)S(1)}, f32[20,16,128]{2,1,0:T(8,128)S(1)}, u32[]{:S(2)}, u32[]{:S(2)}) %collective-permute-start.12) | collective-permute-done | bytes 163872 | tf_op jit(solution)/shard_map/ppermute | solution.py:542
  47.1 9.5 %collective-permute-done.13.r2 = f32[20,16,128]{2,1,0:T(8,128)S(1)} collective-permute-done((f32[20,16,128]{2,1,0:T(8,128)S(1)}, f32[20,16,128]{2,1,0:T(8,128)S(1)}, u32[]{:S(2)}, u32[]{:S(2)}) %collective-permute-start.13) | collective-permute-done | bytes 163872 | tf_op jit(solution)/shard_map/ppermute | solution.py:542
  56.7 3.5 %collective-permute-done.14.r3 = f32[20,16,128]{2,1,0:T(8,128)S(1)} collective-permute-done((f32[20,16,128]{2,1,0:T(8,128)S(1)}, f32[20,16,128]{2,1,0:T(8,128)S(1)}, u32[]{:S(2)}, u32[]{:S(2)}) %collective-permute-start.14) | collective-permute-done | bytes 163872 | tf_op jit(solution)/shard_map/ppermute | solution.py:542
  60.2 1.8 %shard_map.55 = f32[5,16,16,128]{3,2,1,0:T(8,128)} custom-call(f32[20,16,128]{2,1,0:T(8,128)S(1)} %get-tuple-element.43.r0, f32[20,16,128]{2,1,0:T(8,128)S(1)} %collective-permute-done.12.r1, f32[20,16,128]{2,1,0:T(8,128)S(1)} %collective-permute-done.13.r2, f32[20,16,128]{2,1,0:T(8,128)S(1)} %collective-permute-done.14.r3), custom_call_target="tpu_custom_call" | custom-call | tf_op jit(solution)/shard_map/pallas_call | solution.py:589
  (2 shorter events, 0.0 us)
Async XLA Ops:
  0.0 10.5 %copy-start = (f32[1,5,16,16,128]{4,3,2,1,0:T(8,128)S(1)}, f32[1,5,16,16,128]{4,3,2,1,0:T(8,128)}, u32[]{:S(2)}) copy-start(f32[1,5,16,16,128]{4,3,2,1,0:T(8,128)} %param.5) | copy-start | bytes 1966084
  0.0 10.5 %copy-start.1 = (f32[5,16,16,128]{3,2,1,0:T(8,128)S(1)}, f32[5,16,16,128]{3,2,1,0:T(8,128)}, u32[]{:S(2)}) copy-start(f32[5,16,16,128]{3,2,1,0:T(8,128)} %w_ref.3) | copy-start | bytes 1966084
  1.3 15.0 %collective-permute-start.6 = (f32[5,40,128]{2,1,0:T(8,128)S(1)}, f32[5,40,128]{2,1,0:T(8,128)S(1)}, u32[]{:S(2)}, u32[]{:S(2)}) collective-permute-start(f32[5,40,128]{2,1,0:T(8,128)S(1)} %get-tuple-element.33), channel_id=1, source_target_pairs={{1,0},{2,1},{3,2},{4,3},{5,4},{6,5},{7,6},{0,7},{9,8},{10,9},{11,1... | collective-permute-start | bytes 307208 | tf_op jit(solution)/shard_map/ppermute | solution.py:550
  9.8 11.0 %collective-permute-start.5 = (f32[5,40,128]{2,1,0:T(8,128)S(1)}, f32[5,40,128]{2,1,0:T(8,128)S(1)}, u32[]{:S(2)}, u32[]{:S(2)}) collective-permute-start(f32[5,40,128]{2,1,0:T(8,128)S(1)} %get-tuple-element.26._after), channel_id=1, source_target_pairs={{0,1},{1,2},{2,3},{3,4},{4,5},{5,6},{6,7},{7,0},{8,9},{9,10},{10,1... | collective-permute-start | bytes 307208 | tf_op jit(solution)/shard_map/ppermute | solution.py:551
  10.5 0.7 %copy-start.2 = (s32[2,16,128]{2,1,0:T(8,128)S(1)}, s32[2,16,128]{2,1,0:T(8,128)}, u32[]{:S(2)}) copy-start(s32[2,16,128]{2,1,0:T(8,128)} %flag_ref.5) | copy-start | bytes 49156
  13.0 19.2 %collective-permute-start.1 = (f32[20,16,128]{2,1,0:T(8,128)S(1)}, f32[20,16,128]{2,1,0:T(8,128)S(1)}, u32[]{:S(2)}, u32[]{:S(2)}) collective-permute-start(f32[20,16,128]{2,1,0:T(8,128)S(1)} %get-tuple-element.30), channel_id=1, source_target_pairs={{0,128},{64,192},{128,0},{192,64},{1,129},{65,193},{129,1},{193,65... | collective-permute-start | bytes 491528 | tf_op jit(solution)/shard_map/ppermute | solution.py:542
  14.3 9.1 %collective-permute-start.4 = (f32[16,16,128]{2,1,0:T(8,128)S(1)}, f32[16,16,128]{2,1,0:T(8,128)S(1)}, u32[]{:S(2)}, u32[]{:S(2)}) collective-permute-start(f32[16,16,128]{2,1,0:T(8,128)S(1)} %get-tuple-element.32), channel_id=1, source_target_pairs={{8,0},{16,8},{24,16},{32,24},{40,32},{48,40},{56,48},{0,56},{9,1},... | collective-permute-start | bytes 393224 | tf_op jit(solution)/shard_map/ppermute | solution.py:556
  15.5 10.6 %collective-permute-start.3 = (f32[16,16,128]{2,1,0:T(8,128)S(1)}, f32[16,16,128]{2,1,0:T(8,128)S(1)}, u32[]{:S(2)}, u32[]{:S(2)}) collective-permute-start(f32[16,16,128]{2,1,0:T(8,128)S(1)} %get-tuple-element.27._after), channel_id=1, source_target_pairs={{0,8},{8,16},{16,24},{24,32},{32,40},{40,48},{48,56},{56,0},{1,9},... | collective-permute-start | bytes 393224 | tf_op jit(solution)/shard_map/ppermute | solution.py:555
  16.3 20.4 %collective-permute-start.2 = (f32[20,16,128]{2,1,0:T(8,128)S(1)}, f32[20,16,128]{2,1,0:T(8,128)S(1)}, u32[]{:S(2)}, u32[]{:S(2)}) collective-permute-start(f32[20,16,128]{2,1,0:T(8,128)S(1)} %get-tuple-element.31), channel_id=1, source_target_pairs={{0,192},{64,128},{128,64},{192,0},{1,193},{65,129},{129,65},{193,1... | collective-permute-start | bytes 491528 | tf_op jit(solution)/shard_map/ppermute | solution.py:542
  20.8 16.0 %collective-permute-start = (f32[20,16,128]{2,1,0:T(8,128)S(1)}, f32[20,16,128]{2,1,0:T(8,128)S(1)}, u32[]{:S(2)}, u32[]{:S(2)}) collective-permute-start(f32[20,16,128]{2,1,0:T(8,128)S(1)} %get-tuple-element.29._after), channel_id=1, source_target_pairs={{0,64},{64,0},{128,192},{192,128},{1,65},{65,1},{129,193},{193,129... | collective-permute-start | bytes 491528 | tf_op jit(solution)/shard_map/ppermute | solution.py:542
  23.4 5.9 %collective-permute-start.7 = (f32[16,128]{1,0:T(8,128)S(1)}, f32[16,128]{1,0:T(8,128)S(1)}, u32[]{:S(2)}, u32[]{:S(2)}) collective-permute-start(f32[16,128]{1,0:T(8,128)S(1)} %get-tuple-element.34), channel_id=1, source_target_pairs={{0,8},{8,16},{16,24},{24,32},{32,40},{40,48},{48,56},{56,0},{1,9},... | collective-permute-start | bytes 24584 | tf_op jit(solution)/shard_map/ppermute | solution.py:572
  26.1 3.4 %collective-permute-start.8 = (f32[16,128]{1,0:T(8,128)S(1)}, f32[16,128]{1,0:T(8,128)S(1)}, u32[]{:S(2)}, u32[]{:S(2)}) collective-permute-start(f32[16,128]{1,0:T(8,128)S(1)} %get-tuple-element.35), channel_id=1, source_target_pairs={{8,0},{16,8},{24,16},{32,24},{40,32},{48,40},{56,48},{0,56},{9,1},... | collective-permute-start | bytes 24584 | tf_op jit(solution)/shard_map/ppermute | solution.py:573
  26.1 3.4 %copy-start.3 = (s32[2,16,128]{2,1,0:T(8,128)S(1)}, s32[2,16,128]{2,1,0:T(8,128)}, u32[]{:S(2)}) copy-start(s32[2,16,128]{2,1,0:T(8,128)} %flag_ref.5) | copy-start | bytes 49156
  31.0 7.7 %collective-permute-start.10 = (f32[12,16,128]{2,1,0:T(8,128)S(1)}, f32[12,16,128]{2,1,0:T(8,128)S(1)}, u32[]{:S(2)}, u32[]{:S(2)}) collective-permute-start(f32[12,16,128]{2,1,0:T(8,128)S(1)} %get-tuple-element.38), channel_id=1, source_target_pairs={{0,128},{64,192},{128,0},{192,64},{1,129},{65,193},{129,1},{193,65... | collective-permute-start | bytes 294920 | tf_op jit(solution)/shard_map/ppermute | solution.py:542
  31.1 9.8 %collective-permute-start.11 = (f32[12,16,128]{2,1,0:T(8,128)S(1)}, f32[12,16,128]{2,1,0:T(8,128)S(1)}, u32[]{:S(2)}, u32[]{:S(2)}) collective-permute-start(f32[12,16,128]{2,1,0:T(8,128)S(1)} %get-tuple-element.39), channel_id=1, source_target_pairs={{0,192},{64,128},{128,64},{192,0},{1,193},{65,129},{129,65},{193,1... | collective-permute-start | bytes 294920 | tf_op jit(solution)/shard_map/ppermute | solution.py:542
  32.2 8.7 %collective-permute-start.9 = (f32[12,16,128]{2,1,0:T(8,128)S(1)}, f32[12,16,128]{2,1,0:T(8,128)S(1)}, u32[]{:S(2)}, u32[]{:S(2)}) collective-permute-start(f32[12,16,128]{2,1,0:T(8,128)S(1)} %get-tuple-element.37._after), channel_id=1, source_target_pairs={{0,64},{64,0},{128,192},{192,128},{1,65},{65,1},{129,193},{193,129... | collective-permute-start | bytes 294920 | tf_op jit(solution)/shard_map/ppermute | solution.py:542
  42.9 4.3 %collective-permute-start.12 = (f32[20,16,128]{2,1,0:T(8,128)S(1)}, f32[20,16,128]{2,1,0:T(8,128)S(1)}, u32[]{:S(2)}, u32[]{:S(2)}) collective-permute-start(f32[20,16,128]{2,1,0:T(8,128)S(1)} %get-tuple-element.44), channel_id=1, source_target_pairs={{0,64},{64,0},{128,192},{192,128},{1,65},{65,1},{129,193},{193,129... | collective-permute-start | bytes 491528 | tf_op jit(solution)/shard_map/ppermute | solution.py:542
  43.0 13.7 %collective-permute-start.13 = (f32[20,16,128]{2,1,0:T(8,128)S(1)}, f32[20,16,128]{2,1,0:T(8,128)S(1)}, u32[]{:S(2)}, u32[]{:S(2)}) collective-permute-start(f32[20,16,128]{2,1,0:T(8,128)S(1)} %get-tuple-element.45), channel_id=1, source_target_pairs={{0,128},{64,192},{128,0},{192,64},{1,129},{65,193},{129,1},{193,65... | collective-permute-start | bytes 491528 | tf_op jit(solution)/shard_map/ppermute | solution.py:542
  46.4 13.8 %collective-permute-start.14 = (f32[20,16,128]{2,1,0:T(8,128)S(1)}, f32[20,16,128]{2,1,0:T(8,128)S(1)}, u32[]{:S(2)}, u32[]{:S(2)}) collective-permute-start(f32[20,16,128]{2,1,0:T(8,128)S(1)} %get-tuple-element.46), channel_id=1, source_target_pairs={{0,192},{64,128},{128,64},{192,0},{1,193},{65,129},{129,65},{193,1... | collective-permute-start | bytes 491528 | tf_op jit(solution)/shard_map/ppermute | solution.py:542

commit v3 on v2

v3 whole, which is shorter than its diff:
```python
import jax
import jax.numpy as jnp
import numpy as np
from jax import lax
from jax.experimental import pallas as pl
from jax.experimental.pallas import tpu as pltpu
from jax.sharding import PartitionSpec as P

STEP = 0.2
MAIN = 18
EDGE = 12
VMEM = pl.BlockSpec(memory_space=pltpu.VMEM)
SMEM = pl.BlockSpec(memory_space=pltpu.SMEM)
ANY = pl.BlockSpec(memory_space=pl.ANY)
HBM = pl.BlockSpec(memory_space=pltpu.HBM)


def quadrature_table():
    points = [0.25, 0.5, 0.75, 1.0]
    table = np.zeros((4, 4))
    for column in range(4):
        coeffs = [1.0]
        divisor = 1.0
        for other in range(4):
            if other != column:
                other_point = points[other]
                widened = [0.0] * (len(coeffs) + 1)
                for power, value in enumerate(coeffs):
                    widened[power + 1] += value
                    widened[power] -= other_point * value
                coeffs = widened
                divisor *= points[column] - other_point
        for line_index in range(4):
            position = points[line_index]
            total = 0.0
            for power, value in enumerate(coeffs):
                total += value * position ** (power + 1) / (power + 1)
            table[line_index, column] = total / divisor
    return table


def relative_weights(me):
    table = np.asarray(quadrature_table(), np.float32) * np.float32(STEP)

    def entry(a, b):
        value = jnp.float32(table[3 ^ a, 3 ^ b])
        for node in range(3):
            value = jnp.where(me == node, jnp.float32(table[node ^ a, node ^ b]), value)
        return value

    return [[entry(a, b) for b in range(4)] for a in range(4)]


def iotas():
    sub = lax.broadcasted_iota(jnp.int32, (16, 128), 0)
    lane = lax.broadcasted_iota(jnp.int32, (16, 128), 1)
    return sub, lane


def derived(c, g, power):
    r = jnp.exp(power * jnp.log(g * g + 0.25))
    q = c * r
    eta = (0.08 + 0.2 * c + 0.496 * (c * c)) * r
    return q, eta, 0.5 * c * q


def rate(cen, lm, lp, sm, sp, zm, zp, lead_x):
    def diffs(f):
        dl = lp(f) - lm(f)
        ds = sp(f) - sm(f)
        return (dl, ds) if lead_x else (ds, dl)

    def grads(f):
        lo, hi, a, b, n, m = lm(f), lp(f), sm(f), sp(f), zm(f), zp(f)
        x, y = (hi - lo, b - a) if lead_x else (b - a, hi - lo)
        return x, y, m - n, (lo + hi) + (a + b) + (n + m)

    c, g, u, v, w, eta = cen(0), cen(1), cen(2), cen(3), cen(4), cen(6)
    hu, hv, hw = 0.5 * u, 0.5 * v, 0.5 * w
    qx, qy, qz, qsum = grads(5)
    cx, cy, cz, _ = grads(0)
    dc = 0.3 * c * (qsum - 6.0 * cen(5)) + (0.075 * qx - hu) * cx + (0.075 * qy - hv) * cy + (0.075 * qz - hw) * cz
    ex, ey, ez, _ = grads(6)
    ax, ay, az = 0.25 * ex - hu, 0.25 * ey - hv, 0.25 * ez - hw
    ux, uy, uz, usum = grads(2)
    du = eta * (usum - 6.0 * u) + ax * ux + ay * uy + az * uz + 0.5
    vx, vy, vz, vsum = grads(3)
    dv = eta * (vsum - 6.0 * v) + ax * vx + ay * vy + az * vz - 0.5 * diffs(7)[1]
    wx, wy, wz, wsum = grads(4)
    dw = eta * (wsum - 6.0 * w) + ax * wx + ay * wy + az * wz
    strain = uy * uy + wy * wy + vx * vx + vz * vz
    dg = jnp.sqrt(strain + 1.0) - 2.0 * g
    return dc, dg, du, dv, dw


def swap_blocks(tiles, axis, block, index):
    size = 4 * block
    low = index < 2 * block
    even = (index // block) % 2 == 0
    roll = lambda t, k: pltpu.roll(t, k, axis)
    a0, a1, a2, a3 = tiles
    lo0 = jnp.where(low, a0, roll(a2, 2 * block))
    hi0 = jnp.where(low, roll(a0, 2 * block), a2)
    lo1 = jnp.where(low, a1, roll(a3, 2 * block))
    hi1 = jnp.where(low, roll(a1, 2 * block), a3)
    out = []
    for p, q in ((lo0, lo1), (hi0, hi1)):
        out.append(jnp.where(even, p, roll(q, block)))
        out.append(jnp.where(even, roll(p, size - block), q))
    return out


def edges():
    me = lax.axis_index("node")
    t, s = lax.axis_index("tile"), lax.axis_index("slab")
    return me, t == 0, t == lax.axis_size("tile") - 1, s == 0, s == lax.axis_size("slab") - 1


def pick(tiles, me):
    out = tiles[3]
    for q in range(3):
        out = jnp.where(me == q, tiles[q], out)
    return out


def reads(*refs):
    return [lambda *at, ref=ref: ref[at] for ref in refs]


def pack_z_edge(row, sides, lane):
    left = right = jnp.zeros((16, 128), jnp.float32)
    for xq in range(4):
        for f in range(5):
            place = 4 * f + xq
            spot = lane % 32 == place
            tile = row(f, xq)
            left = jnp.where(spot, pltpu.roll(tile, place + 1, 1), left)
            right = jnp.where(spot, pltpu.roll(tile, (place + 96) % 128, 1), right)
    return left, right


def slip_of(flags):
    return 1.0 - 2.0 * flags.astype(jnp.float32)


def tile_kernel(s_ref, w_ref, slip_ref, _after, up_ref, down_ref):
    for ref, up in ((up_ref, True), (down_ref, False)):
        for f in range(5):
            ref[f] = ((s_ref[f, 14]) if up else s_ref[f, 0])
            ref[5 + f] = ((s_ref[f, 15]) if up else s_ref[f, 1])
            ref[10 + f] = ((w_ref[f, 15]) if up else w_ref[f, 0])
        ref[15] = jnp.zeros((16, 128), jnp.float32)
        for side in range(2):
            ref[15, pl.ds(side, 1), :] = ((slip_ref[side, pl.ds(15, 1), :]) if up else slip_ref[side, pl.ds(0, 1), :])


def first_kernel(power_ref, s_ref, m0, m1, m2, m3, rates, der, packed):
    me = lax.axis_index("node")
    sub, lane = iotas()
    power = power_ref[0:1, :]

    def derive(k, _):
        x = pl.ds(4 * k, 4)
        der[0, x], der[1, x], der[2, x] = derived(s_ref[0, x], s_ref[1, x], power)
        return _

    lax.fori_loop(0, 4, derive, 0)

    def column(xq, _):
        rows = []
        for g in range(4):
            x = 4 * g + xq
            lo = jnp.maximum(x - 1, 0)
            hi = jnp.minimum(x + 1, 15)
            at = lambda f, r: s_ref[f, r] if f < 5 else der[f - 5, r]
            rows.append(rate(
                lambda f: at(f, x), lambda f: at(f, lo), lambda f: at(f, hi),
                lambda f: pltpu.roll(at(f, x), 1, 0), lambda f: pltpu.roll(at(f, x), 15, 0),
                lambda f: pltpu.roll(at(f, x), 1, 1), lambda f: pltpu.roll(at(f, x), 127, 1), True))
        for f in range(5):
            for g in range(4):
                rates[f, 4 * g + xq] = rows[g][f]
            out = swap_blocks([rows[g][f] for g in range(4)], 1, 32, lane)
            for q in range(4):
                packed[q, f * 4 + xq] = out[q]
        return _

    lax.fori_loop(0, 4, column, 0)
    for r, m in enumerate((m0, m1, m2, m3)):
        q = me ^ r
        for f in range(5):
            for xq in (1, 2):
                m[2 * f + xq - 1] = packed[q, f * 4 + xq]
        for p in range(2):
            a0, a3 = packed[q, 8 * p], packed[q, 8 * p + 3]
            b0, b3 = packed[q, 8 * p + 4], packed[q, 8 * p + 7]
            m[10 + 3 * p] = jnp.where(lane < 32, b3, a0)
            m[11 + 3 * p] = jnp.where(lane >= 96, b0, a3)
            m[12 + 3 * p] = jnp.where(
                lane < 32, pltpu.roll(b3, 96, 1), jnp.where(lane < 96, b0, pltpu.roll(b3, 32, 1)))
        m[16] = packed[q, 16]
        m[17] = packed[q, 19]


def start_kernel(w_ref, slip_ref, _after, wq_ref, wz_ref, slipq_ref):
    me = lax.axis_index("node")
    sub, lane = iotas()
    for xq in range(4):
        for f in range(5):
            own = [w_ref[f, 4 * g + xq] for g in range(4)]
            wq_ref[f * 4 + xq] = pick(swap_blocks(own, 1, 32, lane), me)
    packs = [pack_z_edge(lambda f, xq: w_ref[f, 4 * g + xq], 2, lane) for g in range(4)]
    for side in range(2):
        wz_ref[side] = pick(swap_blocks([packs[g][side] for g in range(4)], 1, 32, lane), me)
    slipq_ref[...] = pack_y_edge(slip_ref[0], slip_ref[1], me, sub, lane)


def pack_y_edge(lower, upper, me, sub, lane):
    zero = jnp.zeros((16, 128), jnp.float32)
    tiles = swap_blocks([zero, lower, upper, zero], 0, 4, sub)
    return pick(swap_blocks(tiles, 1, 32, lane), me)


def slab_kernel(reg_hbm, flag_hbm, s_hbm, w_hbm, up_ref, down_ref, slip_ref, power_ref, rows, flags, reg, sems):
    me = lax.axis_index("node")
    sub, lane = iotas()

    def run(up_ref, down_ref):
        copies = []
        for k, (ref, ys) in enumerate(((up_ref, (14, 15)), (down_ref, (0, 1)))):
            for r in range(2):
                copies.append(pltpu.make_async_copy(
                    s_hbm.at[:, :, ys[r], :], ref.at[:, pl.ds(16 * r, 16), :], sems.at[2 * k + r]))
            copies.append(pltpu.make_async_copy(w_hbm.at[:, :, (15, 0)[k], :], rows.at[k], sems.at[4 + k]))
        copies.append(pltpu.make_async_copy(flag_hbm, flags, sems.at[6]))
        copies.append(pltpu.make_async_copy(reg_hbm, reg, sems.at[7]))
        for copy in copies:
            copy.start()
        copies[2].wait()
        copies[5].wait()
        for f in range(5):
            start = pack_y_edge(rows[1, f], rows[0, f], me, sub, lane)
            for ref, place in ((up_ref, 8), (down_ref, 4)):
                ref[f, pl.ds(32, 4), :] = start[place:place + 4]
                ref[f, pl.ds(36, 4), :] = jnp.zeros((4, 128), jnp.float32)
        for k in (0, 1, 3, 4, 6, 7):
            copies[k].wait()

    run(up_ref, down_ref)

    slip_ref[...] = slip_of(flags[...])
    power_ref[...] = jnp.full((8, 128), 0.2 + 0.05 * reg[0].astype(jnp.float32))


def corner_kernel(slow_ref, shigh_ref, up_ref, down_ref):
    below, above = reads(slow_ref, shigh_ref)
    for ref, up in ((up_ref, True), (down_ref, False)):
        ref[pl.ds(10, 6), :] = jnp.zeros((6, 128), jnp.float32)
        for f in range(5):
            ref[pl.ds(f, 1), :] = ((below(f, pl.ds(31, 1))) if up else below(f, pl.ds(16, 1)))
            ref[pl.ds(5 + f, 1), :] = ((above(f, pl.ds(15, 1))) if up else above(f, pl.ds(0, 1)))


def fill_ext(ext, s_ref, tlow_ref, thigh_ref, t0, t7):
    lo, hi = reads(tlow_ref, thigh_ref)
    for f in range(5):
        first, last = s_ref[f, pl.ds(0, 16), :], s_ref[f, pl.ds(240, 16), :]
        ext[f, 0] = lo(f)
        ext[f, 1] = jnp.where(t0, first, lo(5 + f))
        ext[f, 2] = first
        ext[f, 3] = s_ref[f, pl.ds(16, 16), :]
        ext[f, 4] = s_ref[f, pl.ds(224, 16), :]
        ext[f, 5] = last
        ext[f, 6] = jnp.where(t7, last, hi(f))
        ext[f, 7] = hi(5 + f)


def inner_kernel(power_ref, s_ref, tlow_ref, thigh_ref, rates, out_ref, ext):
    _, t0, t7, _, _ = edges()
    sub, lane = iotas()
    fill_ext(ext, s_ref, tlow_ref, thigh_ref, t0, t7)
    ext[5], ext[6], ext[7] = derived(ext[0], ext[1], power_ref[0:1, :])

    def row(x):
        return rate(
            lambda f: ext[f, x], lambda f: ext[f, x - 1], lambda f: ext[f, x + 1],
            lambda f: pltpu.roll(ext[f, x], 1, 0), lambda f: pltpu.roll(ext[f, x], 15, 0),
            lambda f: pltpu.roll(ext[f, x], 1, 1), lambda f: pltpu.roll(ext[f, x], 127, 1), True)

    first, last = row(2), row(5)
    for f in range(5):
        for q in range(4):
            out_ref[q, f] = jnp.where(
                lane < 32, pltpu.roll(first[f], 32 * (4 - q) % 128, 1), pltpu.roll(last[f], 32 * (3 - q), 1))

    def at(g):
        def tile(f, xq):
            return first[f] if g + xq == 0 else last[f] if g + xq == 6 else rates[f, 4 * g + xq]

        return tile

    packs = [pack_z_edge(at(g), 2, lane) for g in range(4)]
    for side in range(2):
        out = swap_blocks([packs[g][side] for g in range(4)], 1, 32, lane)
        for q in range(4):
            out_ref[q, 5 + side] = out[q]


def edge_kernel(power_ref, s_ref, tlow_ref, thigh_ref, slow_ref, shigh_ref, clow_ref, chigh_ref, slip_ref,
                inner_ref, e0, e1, e2, e3, ext, yh, band, edge):
    me, t0, t7, s0, s7 = edges()
    sub, lane = iotas()
    power = power_ref[0:1, :]
    lo, hi = reads(tlow_ref, thigh_ref)
    corner_lo, corner_hi = reads(clow_ref, chigh_ref)
    below_row, above_row = reads(slow_ref, shigh_ref)
    fill_ext(ext, s_ref, tlow_ref, thigh_ref, t0, t7)
    ext[5], ext[6], ext[7] = derived(ext[0], ext[1], power)

    for side in range(2):
        ref = (below_row, above_row)[side]
        near, far = ((16, 0), (0, 16))[side]
        y, inward = ((0, 1), (15, 14))[side]
        wall = (s0, s7)[side]
        slip = slip_ref[side]
        slip_lo = lo(15, pl.ds(side, 1))
        slip_hi = hi(15, pl.ds(side, 1))
        for f in range(5):
            def ghost(value, flag):
                return -value if f == 3 else value * flag if f in (2, 4) else value

            mine = s_ref[f, pl.ds(y, 16, stride=16), :]
            yh[f, side, pl.ds(0, 16), :] = jnp.where(wall, ghost(mine, slip), ref(f, pl.ds(near, 16)))
            yh[f, side, pl.ds(16, 1), :] = jnp.where(
                wall, ghost(ext[f, 1, pl.ds(y, 1), :], slip_lo),
                jnp.where(t0, ref(f, pl.ds(near, 1)), corner_lo(pl.ds(5 * side + f, 1))))
            yh[f, side, pl.ds(17, 1), :] = jnp.where(
                wall, ghost(ext[f, 6, pl.ds(y, 1), :], slip_hi),
                jnp.where(t7, ref(f, pl.ds(near + 15, 1)), corner_hi(pl.ds(5 * side + f, 1))))
            yh[f, side, pl.ds(18, 6), :] = jnp.zeros((6, 128), jnp.float32)
            band[f, side, 0] = ref(f, pl.ds(far, 16))
            band[f, side, 1] = ref(f, pl.ds(near, 16))
            band[f, side, 2] = mine
            band[f, side, 3] = s_ref[f, pl.ds(inward, 16, stride=16), :]
        yh[5, side], yh[6, side], yh[7, side] = derived(yh[0, side], yh[1, side], power)
        band[5, side], band[6, side], band[7, side] = derived(band[0, side], band[1, side], power)

    def row(x, place):
        def below(f):
            return jnp.where(sub == 0, yh[f, 0, pl.ds(place, 1), :], pltpu.roll(ext[f, x], 1, 0))

        def above(f):
            return jnp.where(sub == 15, yh[f, 1, pl.ds(place, 1), :], pltpu.roll(ext[f, x], 15, 0))

        return rate(
            lambda f: ext[f, x], lambda f: ext[f, x - 1], lambda f: ext[f, x + 1], below, above,
            lambda f: pltpu.roll(ext[f, x], 1, 1), lambda f: pltpu.roll(ext[f, x], 127, 1), True)

    lower, upper = row(1, 16), row(6, 17)
    for f in range(5):
        for q in range(4):
            edge[q, f] = jnp.where(
                jnp.logical_or(lane < 32, lane >= 96), inner_ref[q, f],
                jnp.where(lane < 64, pltpu.roll(lower[f], (32 * (1 - q)) % 128, 1),
                          pltpu.roll(upper[f], (32 * (2 - q)) % 128, 1)))

    def band_rate(side, k):
        y = 0 if side == 0 else 15
        left = (lambda f: yh[f, side, pl.ds(16, 1), :]) if k == 1 else (lambda f: ext[f, 1, pl.ds(y, 1), :])
        right = (lambda f: yh[f, side, pl.ds(17, 1), :]) if k == 1 else (lambda f: ext[f, 6, pl.ds(y, 1), :])

        def before_x(f):
            return jnp.where(sub == 0, left(f), pltpu.roll(band[f, side, k], 1, 0))

        def after_x(f):
            return jnp.where(sub == 15, right(f), pltpu.roll(band[f, side, k], 15, 0))

        outer = (lambda f: band[f, side, 0]) if k == 1 else (lambda f: yh[f, side, pl.ds(0, 16), :])
        inner = lambda f: band[f, side, k + 1]
        before, after = (outer, inner) if side == 0 else (inner, outer)
        return rate(
            lambda f: band[f, side, k], before, after, before_x, after_x,
            lambda f: pltpu.roll(band[f, side, k], 1, 1), lambda f: pltpu.roll(band[f, side, k], 127, 1), False)

    rows = [band_rate(0, 2), band_rate(0, 1), band_rate(1, 1), band_rate(1, 2)]
    zero = jnp.zeros((16, 128), jnp.float32)
    beside = [[zero, zero] for q in range(4)]
    for f in range(5):
        out = swap_blocks(swap_blocks([r[f] for r in rows], 0, 4, sub), 1, 32, lane)
        for q in range(4):
            edge[q, 5 + f] = out[q]
            for xq in range(4):
                place = 4 * f + xq
                spot = jnp.logical_and(lane % 32 == place, sub % 4 == xq)
                for side, to, shift in ((0, (q + 1) % 4, (place + 97) % 128), (1, (q + 3) % 4, place)):
                    beside[to][side] = jnp.where(spot, pltpu.roll(out[q], shift, 1), beside[to][side])
    for q in range(4):
        for side in range(2):
            b = beside[q][side]
            low = b + pltpu.roll(b, 15, 0)
            low = low + pltpu.roll(low, 14, 0)
            high = b + pltpu.roll(b, 1, 0)
            high = high + pltpu.roll(high, 2, 0)
            edge[q, 10 + side] = jnp.where(sub == 0, low, jnp.where(sub == 15, high, inner_ref[q, 5 + side]))
    for r, e in enumerate((e0, e1, e2, e3)):
        e[...] = edge[me ^ r]


def start_tiles_kernel(tlow_ref, thigh_ref, slow_ref, shigh_ref, wq_ref, wz_ref, _after, wxy_ref):
    me = lax.axis_index("node")
    sub, lane = iotas()
    lo, hi = reads(tlow_ref, thigh_ref)
    below, above = reads(slow_ref, shigh_ref)
    for f in range(5):
        a = pltpu.roll(lo(10 + f), (5 - me) % 4 * 32, 1)
        b = pltpu.roll(hi(10 + f), (6 - me) % 4 * 32, 1)
        wxy_ref[f] = jnp.where(
            lane < 32, wq_ref[f * 4], jnp.where(lane < 64, a, jnp.where(lane < 96, b, wq_ref[f * 4 + 3])))
        wxy_ref[5 + f, pl.ds(4, 4), :] = below(f, pl.ds(32, 4))
        wxy_ref[5 + f, pl.ds(8, 4), :] = above(f, pl.ds(32, 4))
        for xq in range(4):
            wxy_ref[5 + f, pl.ds(xq, 1), :] = wq_ref[f * 4 + xq, pl.ds(0, 1), :]
            wxy_ref[5 + f, pl.ds(12 + xq, 1), :] = wq_ref[f * 4 + xq, pl.ds(15, 1), :]
    for side in range(2):
        wxy_ref[10 + side] = wz_ref[side]


def second_kernel(a2, a3, power_ref, a0, a1, b0, b1, b2, b3, wq_ref, wxy_ref, slipq_ref,
                  o0, o1, o2, o3, main, xh, yh, zh, rates, table):
    me, t0, t7, s0, s7 = edges()
    sub, lane = iotas()
    power = power_ref[0:1, :]
    slip = slipq_ref[...]
    at_lower = jnp.logical_and(jnp.logical_and(sub >= 4, sub < 8), s0)
    at_upper = jnp.logical_and(jnp.logical_and(sub >= 8, sub < 12), s7)
    arrived = ((a0, 0), (a1, 0), (a2, 0), (a3, 0))
    edge = ((b0, 0), (b1, 0), (b2, 0), (b3, 0))
    weights = relative_weights(me)
    for m in range(4):
        for r in range(4):
            table[m * 4 + r] = weights[m][r]

    def node(m, _):
        weight = [table[m * 4 + r] for r in range(4)]

        def mix(refs, k):
            out = None
            for r, (ref, base) in enumerate(refs):
                term = weight[r] * ref[base + k]
                out = term if out is None else out + term
            return out

        outer = {}
        for p in range(2):
            a0, a3, b = (mix(arrived, 10 + 3 * p + k) for k in range(3))
            outer[2 * p] = a0, a3
            outer[2 * p + 1] = jnp.where(lane < 96, b, a3), jnp.where(
                lane < 32, a0, jnp.where(lane < 64, pltpu.roll(b, 32, 1), pltpu.roll(b, 96, 1)))
        outer[4] = mix(arrived, 16), mix(arrived, 17)

        for f in range(5):
            xb = wxy_ref[f] + mix(edge, f)
            yb = wxy_ref[5 + f] + mix(edge, 5 + f)
            yh[f] = yb
            for xq in range(4):
                tile = wq_ref[f * 4 + xq] + (mix(arrived, 2 * f + xq - 1) if xq in (1, 2) else outer[f][xq // 3])
                if xq == 0:
                    tile = jnp.where(lane < 32, xb, tile)
                if xq == 3:
                    tile = jnp.where(lane >= 96, xb, tile)
                tile = jnp.where(sub == 0, yh[f, pl.ds(xq, 1), :], tile)
                tile = jnp.where(sub == 15, yh[f, pl.ds(12 + xq, 1), :], tile)
                main[f, xq] = tile
            xh[f] = jnp.where(
                lane < 64, jnp.where(t0, main[f, 0], pltpu.roll(xb, 96, 1)),
                jnp.where(t7, main[f, 3], pltpu.roll(xb, 32, 1)))
            lower, upper = pltpu.roll(yb, 4, 0), pltpu.roll(yb, 12, 0)
            if f == 3:
                lower, upper = -lower, -upper
            if f in (2, 4):
                lower, upper = lower * slip, upper * slip
            yh[f] = jnp.where(at_lower, lower, jnp.where(at_upper, upper, yb))
        for xq in range(4):
            main[5, xq], main[6, xq], main[7, xq] = derived(main[0, xq], main[1, xq], power)
        xh[5], xh[6], xh[7] = derived(xh[0], xh[1], power)
        yh[5], yh[6], yh[7] = derived(yh[0], yh[1], power)
        for side in range(2):
            z = wxy_ref[10 + side] + mix(edge, 10 + side)
            zh[0, side] = z
            q, eta, _s = derived(z, pltpu.roll(z, 124, 1), power)
            zh[1, side], zh[2, side] = q, eta
        for xq in range(4):
            def left(f):
                if xq > 0:
                    return main[f, xq - 1]
                return jnp.where(lane < 32, xh[f], pltpu.roll(main[f, 3], 32, 1))

            def right(f):
                if xq < 3:
                    return main[f, xq + 1]
                return jnp.where(lane >= 96, xh[f], pltpu.roll(main[f, 0], 96, 1))

            def below(f):
                return jnp.where(sub == 0, yh[f, pl.ds(4 + xq, 1), :], pltpu.roll(main[f, xq], 1, 0))

            def above(f):
                return jnp.where(sub == 15, yh[f, pl.ds(8 + xq, 1), :], pltpu.roll(main[f, xq], 15, 0))

            def spot(f):
                return (0, 4 * f + xq) if f < 5 else (f - 4, xq)

            def before(f):
                k, i = spot(f)
                return jnp.where(lane % 32 == 0, pltpu.roll(zh[k, 0], (128 - i) % 128, 1), pltpu.roll(main[f, xq], 1, 1))

            def after(f):
                k, i = spot(f)
                return jnp.where(lane % 32 == 31, pltpu.roll(zh[k, 1], 31 - i, 1), pltpu.roll(main[f, xq], 127, 1))

            out = rate(lambda f: main[f, xq], left, right, below, above, before, after, True)
            for f in range(5):
                rates[m, f * 4 + xq] = out[f]
        return _

    lax.fori_loop(0, 4, node, 0)

    def combine(k, _):
        have = [rates[r, k] for r in range(4)]
        for m, o in enumerate((o0, o1, o2, o3)):
            out = wq_ref[k]
            for r in range(4):
                out = out + weights[m][r] * have[r]
            o[k] = out
        return _

    lax.fori_loop(0, 20, combine, 0)


def last_kernel(r0, r1, r2, r3, out_hbm, quarter, out, sems):
    me = lax.axis_index("node")
    _, lane = iotas()
    copies = []
    for f in range(5):
        for r, ref in enumerate((r0, r1, r2, r3)):
            quarter[me ^ r, pl.ds(4 * f, 4)] = ref[pl.ds(4 * f, 4)]
        for xq in range(4):
            tiles = swap_blocks([quarter[q, 4 * f + xq] for q in range(4)], 1, 32, lane)
            for g in range(4):
                out[f, 4 * g + xq] = tiles[g]
        copies.append(pltpu.make_async_copy(out.at[f], out_hbm.at[f], sems.at[f]))
        copies[f].start()
    for copy in copies:
        copy.wait()


def tiles_of(n):
    return jax.ShapeDtypeStruct((n, 16, 128), jnp.float32)


def shards(start_state, iterate, wall_flags, reg_index):
    state = iterate[0]
    flat = state.reshape(5, 256, 128)
    params = pltpu.CompilerParams(vmem_limit_bytes=32 * 1024 * 1024)
    scratch = lambda *shape: pltpu.VMEM(shape + (16, 128), jnp.float32)
    shape = lambda *dims: jax.ShapeDtypeStruct(dims, jnp.float32)
    dma = lambda n: pltpu.SemaphoreType.DMA((n,))

    def call(kernel, ins, outs, scratch_shapes=(), place=VMEM):
        return pl.pallas_call(
            kernel, out_shape=outs, in_specs=ins, out_specs=[place] * len(outs),
            scratch_shapes=scratch_shapes, compiler_params=params,
            cost_estimate=pl.CostEstimate(flops=1, bytes_accessed=1, transcendentals=0))

    def neighbours(up, down, axis):
        size = lax.axis_size(axis)
        from_lower = lax.ppermute(up, axis, [(i, (i + 1) % size) for i in range(size)])
        from_upper = lax.ppermute(down, axis, [((i + 1) % size, i) for i in range(size)])
        return from_lower, from_upper

    def send(tiles, r):
        return lax.ppermute(tiles, "node", [(i, i ^ r) for i in range(4)])

    far = lambda x: pltpu.with_memory_space_constraint(x, pltpu.HBM)
    slab_near, slab_next, slip, power = call(
        slab_kernel, [ANY] + [HBM] * 3, [shape(5, 40, 128)] * 2 + [shape(2, 16, 128), shape(8, 128)],
        [scratch(2, 5), pltpu.VMEM((2, 16, 128), jnp.int32), pltpu.SMEM((1,), jnp.int32), dma(8)])(
        reg_index, far(wall_flags), far(state), far(start_state))
    slab = neighbours(slab_near, slab_next, "slab")

    m0, m1, m2, m3, rates = call(
        first_kernel, [VMEM, VMEM], [tiles_of(MAIN)] * 4 + [shape(5, 16, 16, 128)],
        [scratch(3, 16), scratch(4, 20)])(power, state)
    a2, a3, a1 = send(m2, 2), send(m3, 3), send(m1, 1)

    tile = neighbours(*call(tile_kernel, [VMEM] * 3 + [ANY], [tiles_of(16)] * 2)(
        state, start_state, slip, m2), "tile")

    inner, = call(
        inner_kernel, [VMEM] * 5, [shape(4, 7, 16, 128)], [scratch(8, 8)])(power, flat, *tile, rates)

    corner = neighbours(*call(corner_kernel, [VMEM] * 2, [shape(16, 128)] * 2)(*slab), "tile")

    e0, e1, e2, e3 = call(
        edge_kernel, [VMEM] * 10, [tiles_of(EDGE)] * 4,
        [scratch(8, 8), pltpu.VMEM((8, 2, 24, 128), jnp.float32), scratch(8, 2, 4), scratch(4, EDGE)])(
        power, flat, *tile, *slab, *corner, slip, inner)
    b2, b3, b1 = send(e2, 2), send(e3, 3), send(e1, 1)

    wq, wz, slipq = call(
        start_kernel, [VMEM, VMEM, ANY], [tiles_of(20), tiles_of(2), shape(16, 128)])(start_state, slip, e2)
    wxy, = call(start_tiles_kernel, [VMEM] * 6 + [ANY], [tiles_of(EDGE)])(*tile, *slab, wq, wz, e2)

    outs = call(
        second_kernel, [VMEM] * 12, [tiles_of(20)] * 4,
        [scratch(8, 4), scratch(8), scratch(8), scratch(3, 2), scratch(4, 20), pltpu.SMEM((16,), jnp.float32)])(
        a2, a3, power, m0, a1, e0, b1, b2, b3, wq, wxy, slipq)
    back = {r: send(outs[r], r) for r in (2, 3, 1)}

    result, = call(
        last_kernel, [VMEM] * 4, [shape(5, 16, 16, 128)], [scratch(4, 20), scratch(5, 16), dma(5)], HBM)(
        outs[0], back[1], back[2], back[3])
    return result[None]


def solution(mesh):
    return jax.shard_map(
        shards,
        mesh=mesh,
        in_specs=(
            P(None, "tile", "slab", None),
            P("node", None, "tile", "slab", None),
            P(None, "tile", None),
            P(),
        ),
        out_specs=P("node", None, "tile", "slab", None),
        check_vma=False,
    )
```

time: 63.2 us -> 61.3 us (0.970)
  Pallas kernels: 13.5 us -> 11.3 us
  waiting for transfers between devices: 21.9 us -> 22.8 us
  local copies, waits for them, and re-layouts: 0.72 us -> 0.01 us
    pallas_call x8, Pallas kernels: 13.4 us -> 11.2 us  [the longest x1 2.01 us: shards(): call(second_kernel, [VMEM] * 12, [tiles_of(20)] * 4, [scratch(8, 4), scra...]
    ppermute x15, waiting for transfers between devices: 21.9 us -> 22.8 us  [the longest x9 19.6 us: send(): return lax.ppermute(tiles, 'node', [(i, i ^ r) for i in range(4)])]
    unnamed x8 -> x4, local copies, waits for them, and re-layouts: 0.72 us -> 0.01 us
  transfers between devices with their start and end apart: 15 -> 15, of which waited for: 7 -> 8; matrix products, arithmetic and copies ran while one was open for 0% -> 0% of each run, Pallas kernels for 14% -> 10%
where the time goes in v3:
time: 61.3 us; the launch traced here: 60.2 us
  starting transfers between devices  25.2 us (41%)
  waiting for transfers between devices  22.8 us (37%)
  Pallas kernels  11.3 us (18%)
  between operations  0.76 us (1%)
    ppermute x9, waiting for transfers between devices, send(): return lax.ppermute(tiles, 'node', [(i, i ^ r) for i in range(4)])  19.6 us
    ppermute x3, starting transfers between devices, neighbours(): lax.ppermute(up, axis, [(i, (i + 1) % size) for i in range(size)])  13 us
    ppermute x9, starting transfers between devices, send(): return lax.ppermute(tiles, 'node', [(i, i ^ r) for i in range(4)])  9.73 us
    ppermute x3, waiting for transfers between devices, neighbours(): lax.ppermute(down, axis, [((i + 1) % size, i) for i in range(size)])  2.59 us
    ppermute x3, starting transfers between devices, neighbours(): lax.ppermute(down, axis, [((i + 1) % size, i) for i in range(size)])  2.55 us
    pallas_call x1, Pallas kernels, shards(): call(second_kernel, [VMEM] * 12, [tiles_of(20)] * 4, [scratch(8, 4), scra...  2.01 us
    pallas_call x1, Pallas kernels, shards(): call(start_kernel, [VMEM, VMEM, ANY], [tiles_of(20), tiles_of(2), shape(1...  1.95 us
    pallas_call x1, Pallas kernels, shards(): call(first_kernel, [VMEM, VMEM], [tiles_of(MAIN)] * 4 + [shape(5, 16, 16,...  1.89 us
  transfers between devices with their start and end apart: 15, of which 8 were waited for; matrix products, arithmetic and copies ran while one was open for 0% of the time, Pallas kernels for 10%

profile of v3, /device:TPU:37, one launch (start us, length us, event | category | flops | bytes accessed | tf_op | source)
XLA Modules:
  0.0 60.2 jit_solution(8687110879603227501)
XLA Ops:
  0.7 0.0 copy-start
  0.7 1.3 %shard_map.46 = (f32[5,40,128]{2,1,0:T(8,128)S(1)}, f32[5,40,128]{2,1,0:T(8,128)S(1)}, f32[2,16,128]{2,1,0:T(8,128)S(1)}, f32[8,128]{1,0:T(8,128)S(1)}) custom-call(s32[1]{0:T(128)S(6)} %copy.5.reg_hbm, s32[2,16,128]{2,1,0:T(8,128)} %flag_hbm.1, f32[5,16,16,128]{3,2,1,0:T(8,128)} %bitcast.3, f32[5,16,16,128]{3,2,1,0:T(8,128)} %w_ref.3), custom_call_target="tpu_custom_call" | custom-call | flops 1 | bytes 1 | tf_op jit(solution)/shard_map/pallas_call | solution.py:584
  1.9 0.0 copy-start.1
  1.9 6.1 %collective-permute-start.5 = (f32[5,40,128]{2,1,0:T(8,128)S(1)}, f32[5,40,128]{2,1,0:T(8,128)S(1)}, u32[]{:S(2)}, u32[]{:S(2)}) collective-permute-start(f32[5,40,128]{2,1,0:T(8,128)S(1)} %get-tuple-element.37), channel_id=1, source_target_pairs={{0,1},{1,2},{2,3},{3,4},{4,5},{5,6},{6,7},{7,0},{8,9},{9,10},{10,1... | collective-permute-start | bytes 307208 | tf_op jit(solution)/shard_map/ppermute | solution.py:576
  8.0 2.5 %collective-permute-start.6 = (f32[5,40,128]{2,1,0:T(8,128)S(1)}, f32[5,40,128]{2,1,0:T(8,128)S(1)}, u32[]{:S(2)}, u32[]{:S(2)}) collective-permute-start(f32[5,40,128]{2,1,0:T(8,128)S(1)} %get-tuple-element.38), channel_id=1, source_target_pairs={{1,0},{2,1},{3,2},{4,3},{5,4},{6,5},{7,6},{0,7},{9,8},{10,9},{11,1... | collective-permute-start | bytes 307208 | tf_op jit(solution)/shard_map/ppermute | solution.py:577
  10.6 0.0 copy-done
  10.6 1.9 %shard_map.47 = (f32[18,16,128]{2,1,0:T(8,128)S(1)}, f32[18,16,128]{2,1,0:T(8,128)S(1)}, f32[18,16,128]{2,1,0:T(8,128)S(1)}, f32[18,16,128]{2,1,0:T(8,128)S(1)}, f32[5,16,16,128]{3,2,1,0:T(8,128)S(1)}) custom-call(f32[8,128]{1,0:T(8,128)S(1)} %get-tuple-element.29.power_ref, f32[5,16,16,128]{3,2,1,0:T(8,128)S(1)} %bitcast.4), custom_call_target="tpu_custom_call" | custom-call | flops 1 | bytes 1 | tf_op jit(solution)/shard_map/pallas_call | solution.py:590
  12.5 2.0 %collective-permute-start = (f32[18,16,128]{2,1,0:T(8,128)S(1)}, f32[18,16,128]{2,1,0:T(8,128)S(1)}, u32[]{:S(2)}, u32[]{:S(2)}) collective-permute-start(f32[18,16,128]{2,1,0:T(8,128)S(1)} %get-tuple-element.30._after), channel_id=1, source_target_pairs={{0,128},{64,192},{128,0},{192,64},{1,129},{65,193},{129,1},{193,65... | collective-permute-start | bytes 442376 | tf_op jit(solution)/shard_map/ppermute | solution.py:581
  14.5 0.0 copy-done.1
  14.5 2.3 %collective-permute-start.3 = (f32[16,16,128]{2,1,0:T(8,128)S(1)}, f32[16,16,128]{2,1,0:T(8,128)S(1)}, u32[]{:S(2)}, u32[]{:S(2)}) collective-permute-start(f32[16,16,128]{2,1,0:T(8,128)S(1)} %get-tuple-element.35), channel_id=1, source_target_pairs={{0,8},{8,16},{16,24},{24,32},{32,40},{40,48},{48,56},{56,0},{1,9},... | collective-permute-start | bytes 393224 | tf_op jit(solution)/shard_map/ppermute | solution.py:576
  16.8 0.0 collective-permute-start.4
  16.8 0.0 collective-permute-done.5.slow_ref
  16.8 0.0 collective-permute-start.1
  16.9 0.0 collective-permute-done.6.shigh_ref
  16.9 1.3 %collective-permute-start.2 = (f32[18,16,128]{2,1,0:T(8,128)S(1)}, f32[18,16,128]{2,1,0:T(8,128)S(1)}, u32[]{:S(2)}, u32[]{:S(2)}) collective-permute-start(f32[18,16,128]{2,1,0:T(8,128)S(1)} %get-tuple-element.33), channel_id=1, source_target_pairs={{0,64},{64,0},{128,192},{192,128},{1,65},{65,1},{129,193},{193,129... | collective-permute-start | bytes 442376 | tf_op jit(solution)/shard_map/ppermute | solution.py:581
  18.2 0.6 collective-permute-done.3.tlow_ref
  18.8 4.6 %collective-permute-start.7 = (f32[16,128]{1,0:T(8,128)S(1)}, f32[16,128]{1,0:T(8,128)S(1)}, u32[]{:S(2)}, u32[]{:S(2)}) collective-permute-start(f32[16,128]{1,0:T(8,128)S(1)} %get-tuple-element.39), channel_id=1, source_target_pairs={{0,8},{8,16},{16,24},{24,32},{32,40},{40,48},{48,56},{56,0},{1,9},... | collective-permute-start | bytes 24584 | tf_op jit(solution)/shard_map/ppermute | solution.py:576
  23.3 0.0 collective-permute-done.4.thigh_ref
  23.3 0.0 collective-permute-start.8
  23.3 0.7 %shard_map.50.inner_ref = f32[4,7,16,128]{3,2,1,0:T(8,128)S(1)} custom-call(f32[8,128]{1,0:T(8,128)S(1)} %get-tuple-element.29.power_ref, f32[5,256,128]{2,1,0:T(8,128)S(1)} %bitcast.6, f32[16,16,128]{2,1,0:T(8,128)S(1)} %collective-permute-done.3.tlow_ref, f32[16,16,128]{2,1,0:T(8,128)S(1)} %collective-permute-done.4.thigh_ref, ...), custom_call_target="tpu_custom_call" | custom-call | flops 1 | bytes 1 | tf_op jit(solution)/shard_map/pallas_call | solution.py:598
  24.1 0.0 collective-permute-done.7.clow_ref
  24.1 2.6 %collective-permute-done.8.chigh_ref = f32[16,128]{1,0:T(8,128)S(1)} collective-permute-done((f32[16,128]{1,0:T(8,128)S(1)}, f32[16,128]{1,0:T(8,128)S(1)}, u32[]{:S(2)}, u32[]{:S(2)}) %collective-permute-start.8) | collective-permute-done | bytes 8224 | tf_op jit(solution)/shard_map/ppermute | solution.py:577
  26.7 1.5 %shard_map.51 = (f32[12,16,128]{2,1,0:T(8,128)S(1)}, f32[12,16,128]{2,1,0:T(8,128)S(1)}, f32[12,16,128]{2,1,0:T(8,128)S(1)}, f32[12,16,128]{2,1,0:T(8,128)S(1)}) custom-call(f32[8,128]{1,0:T(8,128)S(1)} %get-tuple-element.29.power_ref, f32[5,256,128]{2,1,0:T(8,128)S(1)} %bitcast.7, f32[16,16,128]{2,1,0:T(8,128)S(1)} %collective-permute-done.3.tlow_ref, ...), custom_call_target="tpu_custom_call" | custom-call | flops 1 | bytes 1 | tf_op jit(solution)/shard_map/pallas_call | solution.py:603
  28.3 0.1 collective-permute-start.10
  28.4 0.9 %collective-permute-start.11 = (f32[12,16,128]{2,1,0:T(8,128)S(1)}, f32[12,16,128]{2,1,0:T(8,128)S(1)}, u32[]{:S(2)}, u32[]{:S(2)}) collective-permute-start(f32[12,16,128]{2,1,0:T(8,128)S(1)} %get-tuple-element.45), channel_id=1, source_target_pairs={{0,192},{64,128},{128,64},{192,0},{1,193},{65,129},{129,65},{193,1... | collective-permute-start | bytes 294920 | tf_op jit(solution)/shard_map/ppermute | solution.py:581
  29.3 0.0 collective-permute-done.a2
  29.3 2.6 %collective-permute-start.9 = (f32[12,16,128]{2,1,0:T(8,128)S(1)}, f32[12,16,128]{2,1,0:T(8,128)S(1)}, u32[]{:S(2)}, u32[]{:S(2)}) collective-permute-start(f32[12,16,128]{2,1,0:T(8,128)S(1)} %get-tuple-element.43), channel_id=1, source_target_pairs={{0,64},{64,0},{128,192},{192,128},{1,65},{65,1},{129,193},{193,129... | collective-permute-start | bytes 294920 | tf_op jit(solution)/shard_map/ppermute | solution.py:581
  31.9 2.0 %shard_map.52 = (f32[20,16,128]{2,1,0:T(8,128)S(1)}, f32[2,16,128]{2,1,0:T(8,128)S(1)}, f32[16,128]{1,0:T(8,128)S(1)}) custom-call(f32[5,16,16,128]{3,2,1,0:T(8,128)S(1)} %copy-done.1, f32[2,16,128]{2,1,0:T(8,128)S(1)} %get-tuple-element.34.slip_ref, f32[12,16,128]{2,1,0:T(8,128)S(1)} %get-tuple-element.44._after), custom_call_target="tpu_custom_call" | custom-call | flops 1 | bytes 1 | tf_op jit(solution)/shard_map/pallas_call | solution.py:609
  33.9 0.1 shard_map.53.wxy_ref
  34.0 0.5 collective-permute-done.1.a3
  34.4 0.0 collective-permute-done.2.a1
  34.4 2.3 %collective-permute-done.10.b2 = f32[12,16,128]{2,1,0:T(8,128)S(1)} collective-permute-done((f32[12,16,128]{2,1,0:T(8,128)S(1)}, f32[12,16,128]{2,1,0:T(8,128)S(1)}, u32[]{:S(2)}, u32[]{:S(2)}) %collective-permute-start.10) | collective-permute-done | bytes 98336 | tf_op jit(solution)/shard_map/ppermute | solution.py:581
  36.7 2.8 %collective-permute-done.11.b3 = f32[12,16,128]{2,1,0:T(8,128)S(1)} collective-permute-done((f32[12,16,128]{2,1,0:T(8,128)S(1)}, f32[12,16,128]{2,1,0:T(8,128)S(1)}, u32[]{:S(2)}, u32[]{:S(2)}) %collective-permute-start.11) | collective-permute-done | bytes 98336 | tf_op jit(solution)/shard_map/ppermute | solution.py:581
  39.5 0.0 collective-permute-done.9.b1
  39.5 2.0 %shard_map.54 = (f32[20,16,128]{2,1,0:T(8,128)S(1)}, f32[20,16,128]{2,1,0:T(8,128)S(1)}, f32[20,16,128]{2,1,0:T(8,128)S(1)}, f32[20,16,128]{2,1,0:T(8,128)S(1)}) custom-call(f32[18,16,128]{2,1,0:T(8,128)S(1)} %collective-permute-done.a2, f32[18,16,128]{2,1,0:T(8,128)S(1)} %collective-permute-done.1.a3, f32[8,128]{1,0:T(8,128)S(1)} %get-tuple-element.29.power_ref, ...), custom_call_target="tpu_custom_call" | custom-call | flops 1 | bytes 1 | tf_op jit(solution)/shard_map/pallas_call | solution.py:613
  41.5 0.9 %collective-permute-start.12 = (f32[20,16,128]{2,1,0:T(8,128)S(1)}, f32[20,16,128]{2,1,0:T(8,128)S(1)}, u32[]{:S(2)}, u32[]{:S(2)}) collective-permute-start(f32[20,16,128]{2,1,0:T(8,128)S(1)} %get-tuple-element.50), channel_id=1, source_target_pairs={{0,64},{64,0},{128,192},{192,128},{1,65},{65,1},{129,193},{193,129... | collective-permute-start | bytes 491528 | tf_op jit(solution)/shard_map/ppermute | solution.py:581
  42.5 1.8 %collective-permute-start.13 = (f32[20,16,128]{2,1,0:T(8,128)S(1)}, f32[20,16,128]{2,1,0:T(8,128)S(1)}, u32[]{:S(2)}, u32[]{:S(2)}) collective-permute-start(f32[20,16,128]{2,1,0:T(8,128)S(1)} %get-tuple-element.51), channel_id=1, source_target_pairs={{0,128},{64,192},{128,0},{192,64},{1,129},{65,193},{129,1},{193,65... | collective-permute-start | bytes 491528 | tf_op jit(solution)/shard_map/ppermute | solution.py:581
  44.3 0.0 collective-permute-start.14
  44.3 3.8 %collective-permute-done.12.r1 = f32[20,16,128]{2,1,0:T(8,128)S(1)} collective-permute-done((f32[20,16,128]{2,1,0:T(8,128)S(1)}, f32[20,16,128]{2,1,0:T(8,128)S(1)}, u32[]{:S(2)}, u32[]{:S(2)}) %collective-permute-start.12) | collective-permute-done | bytes 163872 | tf_op jit(solution)/shard_map/ppermute | solution.py:581
  48.1 3.5 %collective-permute-done.13.r2 = f32[20,16,128]{2,1,0:T(8,128)S(1)} collective-permute-done((f32[20,16,128]{2,1,0:T(8,128)S(1)}, f32[20,16,128]{2,1,0:T(8,128)S(1)}, u32[]{:S(2)}, u32[]{:S(2)}) %collective-permute-start.13) | collective-permute-done | bytes 163872 | tf_op jit(solution)/shard_map/ppermute | solution.py:581
  51.7 6.7 %collective-permute-done.14.r3 = f32[20,16,128]{2,1,0:T(8,128)S(1)} collective-permute-done((f32[20,16,128]{2,1,0:T(8,128)S(1)}, f32[20,16,128]{2,1,0:T(8,128)S(1)}, u32[]{:S(2)}, u32[]{:S(2)}) %collective-permute-start.14) | collective-permute-done | bytes 163872 | tf_op jit(solution)/shard_map/ppermute | solution.py:581
  58.4 1.8 %shard_map.55 = f32[5,16,16,128]{3,2,1,0:T(8,128)} custom-call(f32[20,16,128]{2,1,0:T(8,128)S(1)} %get-tuple-element.49.r0, f32[20,16,128]{2,1,0:T(8,128)S(1)} %collective-permute-done.12.r1, f32[20,16,128]{2,1,0:T(8,128)S(1)} %collective-permute-done.13.r2, f32[20,16,128]{2,1,0:T(8,128)S(1)} %collective-permute-done.14.r3), custom_call_target="tpu_custom_call" | custom-call | flops 1 | bytes 1 | tf_op jit(solution)/shard_map/pallas_call | solution.py:619
  (2 shorter events, 0.0 us)
Async XLA Ops:
  0.7 9.9 %copy-start = (f32[1,5,16,16,128]{4,3,2,1,0:T(8,128)S(1)}, f32[1,5,16,16,128]{4,3,2,1,0:T(8,128)}, u32[]{:S(2)}) copy-start(f32[1,5,16,16,128]{4,3,2,1,0:T(8,128)} %param.5) | copy-start | bytes 1966084
  1.9 12.6 %copy-start.1 = (f32[5,16,16,128]{3,2,1,0:T(8,128)S(1)}, f32[5,16,16,128]{3,2,1,0:T(8,128)}, u32[]{:S(2)}) copy-start(f32[5,16,16,128]{3,2,1,0:T(8,128)} %w_ref.3) | copy-start | bytes 1966084
  1.9 14.9 %collective-permute-start.5 = (f32[5,40,128]{2,1,0:T(8,128)S(1)}, f32[5,40,128]{2,1,0:T(8,128)S(1)}, u32[]{:S(2)}, u32[]{:S(2)}) collective-permute-start(f32[5,40,128]{2,1,0:T(8,128)S(1)} %get-tuple-element.37), channel_id=1, source_target_pairs={{0,1},{1,2},{2,3},{3,4},{4,5},{5,6},{6,7},{7,0},{8,9},{9,10},{10,1... | collective-permute-start | bytes 307208 | tf_op jit(solution)/shard_map/ppermute | solution.py:576
  8.0 8.8 %collective-permute-start.6 = (f32[5,40,128]{2,1,0:T(8,128)S(1)}, f32[5,40,128]{2,1,0:T(8,128)S(1)}, u32[]{:S(2)}, u32[]{:S(2)}) collective-permute-start(f32[5,40,128]{2,1,0:T(8,128)S(1)} %get-tuple-element.38), channel_id=1, source_target_pairs={{1,0},{2,1},{3,2},{4,3},{5,4},{6,5},{7,6},{0,7},{9,8},{10,9},{11,1... | collective-permute-start | bytes 307208 | tf_op jit(solution)/shard_map/ppermute | solution.py:577
  12.5 16.8 %collective-permute-start = (f32[18,16,128]{2,1,0:T(8,128)S(1)}, f32[18,16,128]{2,1,0:T(8,128)S(1)}, u32[]{:S(2)}, u32[]{:S(2)}) collective-permute-start(f32[18,16,128]{2,1,0:T(8,128)S(1)} %get-tuple-element.30._after), channel_id=1, source_target_pairs={{0,128},{64,192},{128,0},{192,64},{1,129},{65,193},{129,1},{193,65... | collective-permute-start | bytes 442376 | tf_op jit(solution)/shard_map/ppermute | solution.py:581
  14.5 4.3 %collective-permute-start.3 = (f32[16,16,128]{2,1,0:T(8,128)S(1)}, f32[16,16,128]{2,1,0:T(8,128)S(1)}, u32[]{:S(2)}, u32[]{:S(2)}) collective-permute-start(f32[16,16,128]{2,1,0:T(8,128)S(1)} %get-tuple-element.35), channel_id=1, source_target_pairs={{0,8},{8,16},{16,24},{24,32},{32,40},{40,48},{48,56},{56,0},{1,9},... | collective-permute-start | bytes 393224 | tf_op jit(solution)/shard_map/ppermute | solution.py:576
  16.8 6.5 %collective-permute-start.4 = (f32[16,16,128]{2,1,0:T(8,128)S(1)}, f32[16,16,128]{2,1,0:T(8,128)S(1)}, u32[]{:S(2)}, u32[]{:S(2)}) collective-permute-start(f32[16,16,128]{2,1,0:T(8,128)S(1)} %get-tuple-element.36), channel_id=1, source_target_pairs={{8,0},{16,8},{24,16},{32,24},{40,32},{48,40},{56,48},{0,56},{9,1},... | collective-permute-start | bytes 393224 | tf_op jit(solution)/shard_map/ppermute | solution.py:577
  16.8 17.6 %collective-permute-start.1 = (f32[18,16,128]{2,1,0:T(8,128)S(1)}, f32[18,16,128]{2,1,0:T(8,128)S(1)}, u32[]{:S(2)}, u32[]{:S(2)}) collective-permute-start(f32[18,16,128]{2,1,0:T(8,128)S(1)} %get-tuple-element.31), channel_id=1, source_target_pairs={{0,192},{64,128},{128,64},{192,0},{1,193},{65,129},{129,65},{193,1... | collective-permute-start | bytes 442376 | tf_op jit(solution)/shard_map/ppermute | solution.py:581
  16.9 17.6 %collective-permute-start.2 = (f32[18,16,128]{2,1,0:T(8,128)S(1)}, f32[18,16,128]{2,1,0:T(8,128)S(1)}, u32[]{:S(2)}, u32[]{:S(2)}) collective-permute-start(f32[18,16,128]{2,1,0:T(8,128)S(1)} %get-tuple-element.33), channel_id=1, source_target_pairs={{0,64},{64,0},{128,192},{192,128},{1,65},{65,1},{129,193},{193,129... | collective-permute-start | bytes 442376 | tf_op jit(solution)/shard_map/ppermute | solution.py:581
  18.8 5.3 %collective-permute-start.7 = (f32[16,128]{1,0:T(8,128)S(1)}, f32[16,128]{1,0:T(8,128)S(1)}, u32[]{:S(2)}, u32[]{:S(2)}) collective-permute-start(f32[16,128]{1,0:T(8,128)S(1)} %get-tuple-element.39), channel_id=1, source_target_pairs={{0,8},{8,16},{16,24},{24,32},{32,40},{40,48},{48,56},{56,0},{1,9},... | collective-permute-start | bytes 24584 | tf_op jit(solution)/shard_map/ppermute | solution.py:576
  23.3 3.4 %collective-permute-start.8 = (f32[16,128]{1,0:T(8,128)S(1)}, f32[16,128]{1,0:T(8,128)S(1)}, u32[]{:S(2)}, u32[]{:S(2)}) collective-permute-start(f32[16,128]{1,0:T(8,128)S(1)} %get-tuple-element.40), channel_id=1, source_target_pairs={{8,0},{16,8},{24,16},{32,24},{40,32},{48,40},{56,48},{0,56},{9,1},... | collective-permute-start | bytes 24584 | tf_op jit(solution)/shard_map/ppermute | solution.py:577
  28.3 8.5 %collective-permute-start.10 = (f32[12,16,128]{2,1,0:T(8,128)S(1)}, f32[12,16,128]{2,1,0:T(8,128)S(1)}, u32[]{:S(2)}, u32[]{:S(2)}) collective-permute-start(f32[12,16,128]{2,1,0:T(8,128)S(1)} %get-tuple-element.44._after), channel_id=1, source_target_pairs={{0,128},{64,192},{128,0},{192,64},{1,129},{65,193},{129,1},{193,65... | collective-permute-start | bytes 294920 | tf_op jit(solution)/shard_map/ppermute | solution.py:581
  28.4 11.2 %collective-permute-start.11 = (f32[12,16,128]{2,1,0:T(8,128)S(1)}, f32[12,16,128]{2,1,0:T(8,128)S(1)}, u32[]{:S(2)}, u32[]{:S(2)}) collective-permute-start(f32[12,16,128]{2,1,0:T(8,128)S(1)} %get-tuple-element.45), channel_id=1, source_target_pairs={{0,192},{64,128},{128,64},{192,0},{1,193},{65,129},{129,65},{193,1... | collective-permute-start | bytes 294920 | tf_op jit(solution)/shard_map/ppermute | solution.py:581
  29.3 10.3 %collective-permute-start.9 = (f32[12,16,128]{2,1,0:T(8,128)S(1)}, f32[12,16,128]{2,1,0:T(8,128)S(1)}, u32[]{:S(2)}, u32[]{:S(2)}) collective-permute-start(f32[12,16,128]{2,1,0:T(8,128)S(1)} %get-tuple-element.43), channel_id=1, source_target_pairs={{0,64},{64,0},{128,192},{192,128},{1,65},{65,1},{129,193},{193,129... | collective-permute-start | bytes 294920 | tf_op jit(solution)/shard_map/ppermute | solution.py:581
  41.5 6.6 %collective-permute-start.12 = (f32[20,16,128]{2,1,0:T(8,128)S(1)}, f32[20,16,128]{2,1,0:T(8,128)S(1)}, u32[]{:S(2)}, u32[]{:S(2)}) collective-permute-start(f32[20,16,128]{2,1,0:T(8,128)S(1)} %get-tuple-element.50), channel_id=1, source_target_pairs={{0,64},{64,0},{128,192},{192,128},{1,65},{65,1},{129,193},{193,129... | collective-permute-start | bytes 491528 | tf_op jit(solution)/shard_map/ppermute | solution.py:581
  42.5 9.2 %collective-permute-start.13 = (f32[20,16,128]{2,1,0:T(8,128)S(1)}, f32[20,16,128]{2,1,0:T(8,128)S(1)}, u32[]{:S(2)}, u32[]{:S(2)}) collective-permute-start(f32[20,16,128]{2,1,0:T(8,128)S(1)} %get-tuple-element.51), channel_id=1, source_target_pairs={{0,128},{64,192},{128,0},{192,64},{1,129},{65,193},{129,1},{193,65... | collective-permute-start | bytes 491528 | tf_op jit(solution)/shard_map/ppermute | solution.py:581
  44.3 14.1 %collective-permute-start.14 = (f32[20,16,128]{2,1,0:T(8,128)S(1)}, f32[20,16,128]{2,1,0:T(8,128)S(1)}, u32[]{:S(2)}, u32[]{:S(2)}) collective-permute-start(f32[20,16,128]{2,1,0:T(8,128)S(1)} %get-tuple-element.52), channel_id=1, source_target_pairs={{0,192},{64,128},{128,64},{192,0},{1,193},{65,129},{129,65},{193,1... | collective-permute-start | bytes 491528 | tf_op jit(solution)/shard_map/ppermute | solution.py:581

commit v4 on v3

--- a/solution.py
+++ b/solution.py
@@ -154,7 +154,7 @@
             ref[15, pl.ds(side, 1), :] = ((slip_ref[side, pl.ds(15, 1), :]) if up else slip_ref[side, pl.ds(0, 1), :])
 
 
-def first_kernel(power_ref, s_ref, m0, m1, m2, m3, rates, der, packed):
+def first_kernel(power_ref, s_ref, _after, m0, m1, m2, m3, rates, der, packed):
     me = lax.axis_index("node")
     sub, lane = iotas()
     power = power_ref[0:1, :]
@@ -221,7 +221,7 @@
     return pick(swap_blocks(tiles, 1, 32, lane), me)
 
 
-def slab_kernel(reg_hbm, flag_hbm, s_hbm, w_hbm, up_ref, down_ref, slip_ref, power_ref, rows, flags, reg, sems):
+def slab_kernel(flag_hbm, s_hbm, w_hbm, up_ref, down_ref, slip_ref, rows, flags, sems):
     me = lax.axis_index("node")
     sub, lane = iotas()
 
@@ -233,7 +233,6 @@
                     s_hbm.at[:, :, ys[r], :], ref.at[:, pl.ds(16 * r, 16), :], sems.at[2 * k + r]))
             copies.append(pltpu.make_async_copy(w_hbm.at[:, :, (15, 0)[k], :], rows.at[k], sems.at[4 + k]))
         copies.append(pltpu.make_async_copy(flag_hbm, flags, sems.at[6]))
-        copies.append(pltpu.make_async_copy(reg_hbm, reg, sems.at[7]))
         for copy in copies:
             copy.start()
         copies[2].wait()
@@ -243,13 +242,12 @@
             for ref, place in ((up_ref, 8), (down_ref, 4)):
                 ref[f, pl.ds(32, 4), :] = start[place:place + 4]
                 ref[f, pl.ds(36, 4), :] = jnp.zeros((4, 128), jnp.float32)
-        for k in (0, 1, 3, 4, 6, 7):
+        for k in (0, 1, 3, 4, 6):
             copies[k].wait()
 
     run(up_ref, down_ref)
 
     slip_ref[...] = slip_of(flags[...])
-    power_ref[...] = jnp.full((8, 128), 0.2 + 0.05 * reg[0].astype(jnp.float32))
 
 
 def corner_kernel(slow_ref, shigh_ref, up_ref, down_ref):
@@ -307,7 +305,7 @@
 
 
 def edge_kernel(power_ref, s_ref, tlow_ref, thigh_ref, slow_ref, shigh_ref, clow_ref, chigh_ref, slip_ref,
-                inner_ref, e0, e1, e2, e3, ext, yh, band, edge):
+                inner_ref, _a1, _a2, e0, e1, e2, e3, ext, yh, band, edge):
     me, t0, t7, s0, s7 = edges()
     sub, lane = iotas()
     power = power_ref[0:1, :]
@@ -522,7 +520,7 @@
                 rates[m, f * 4 + xq] = out[f]
         return _
 
-    lax.fori_loop(0, 4, node, 0)
+    lax.fori_loop(0, 4, node, 0, unroll=2)
 
     def combine(k, _):
         have = [rates[r, k] for r in range(4)]
@@ -533,24 +531,28 @@
             o[k] = out
         return _
 
-    lax.fori_loop(0, 20, combine, 0)
+    lax.fori_loop(0, 20, combine, 0, unroll=4)
 
 
 def last_kernel(r0, r1, r2, r3, out_hbm, quarter, out, sems):
     me = lax.axis_index("node")
     _, lane = iotas()
-    copies = []
-    for f in range(5):
+    def copy(f):
+        return pltpu.make_async_copy(out.at[f], out_hbm.at[f], sems.at[f])
+
+    def field(f, _):
         for r, ref in enumerate((r0, r1, r2, r3)):
             quarter[me ^ r, pl.ds(4 * f, 4)] = ref[pl.ds(4 * f, 4)]
         for xq in range(4):
             tiles = swap_blocks([quarter[q, 4 * f + xq] for q in range(4)], 1, 32, lane)
             for g in range(4):
                 out[f, 4 * g + xq] = tiles[g]
-        copies.append(pltpu.make_async_copy(out.at[f], out_hbm.at[f], sems.at[f]))
-        copies[f].start()
-    for copy in copies:
-        copy.wait()
+        copy(f).start()
+        return _
+
+    lax.fori_loop(0, 5, field, 0)
+    for f in range(5):
+        copy(f).wait()
 
 
 def tiles_of(n):
@@ -581,15 +583,16 @@
         return lax.ppermute(tiles, "node", [(i, i ^ r) for i in range(4)])
 
     far = lambda x: pltpu.with_memory_space_constraint(x, pltpu.HBM)
-    slab_near, slab_next, slip, power = call(
-        slab_kernel, [ANY] + [HBM] * 3, [shape(5, 40, 128)] * 2 + [shape(2, 16, 128), shape(8, 128)],
-        [scratch(2, 5), pltpu.VMEM((2, 16, 128), jnp.int32), pltpu.SMEM((1,), jnp.int32), dma(8)])(
-        reg_index, far(wall_flags), far(state), far(start_state))
+    slab_near, slab_next, slip = call(
+        slab_kernel, [HBM] * 3, [shape(5, 40, 128)] * 2 + [shape(2, 16, 128)],
+        [scratch(2, 5), pltpu.VMEM((2, 16, 128), jnp.int32), dma(7)])(
+        far(wall_flags), far(state), far(start_state))
+    power = jnp.broadcast_to(0.2 + 0.05 * reg_index.astype(jnp.float32), (8, 128))
     slab = neighbours(slab_near, slab_next, "slab")
 
     m0, m1, m2, m3, rates = call(
-        first_kernel, [VMEM, VMEM], [tiles_of(MAIN)] * 4 + [shape(5, 16, 16, 128)],
-        [scratch(3, 16), scratch(4, 20)])(power, state)
+        first_kernel, [VMEM, VMEM, ANY], [tiles_of(MAIN)] * 4 + [shape(5, 16, 16, 128)],
+        [scratch(3, 16), scratch(4, 20)])(power, state, slip)
     a2, a3, a1 = send(m2, 2), send(m3, 3), send(m1, 1)
 
     tile = neighbours(*call(tile_kernel, [VMEM] * 3 + [ANY], [tiles_of(16)] * 2)(
@@ -601,9 +604,9 @@
     corner = neighbours(*call(corner_kernel, [VMEM] * 2, [shape(16, 128)] * 2)(*slab), "tile")
 
     e0, e1, e2, e3 = call(
-        edge_kernel, [VMEM] * 10, [tiles_of(EDGE)] * 4,
+        edge_kernel, [VMEM] * 10 + [ANY] * 2, [tiles_of(EDGE)] * 4,
         [scratch(8, 8), pltpu.VMEM((8, 2, 24, 128), jnp.float32), scratch(8, 2, 4), scratch(4, EDGE)])(
-        power, flat, *tile, *slab, *corner, slip, inner)
+        power, flat, *tile, *slab, *corner, slip, inner, a1, a2)
     b2, b3, b1 = send(e2, 2), send(e3, 3), send(e1, 1)
 
     wq, wz, slipq = call(

time: 61.3 us -> 60.5 us (0.987)
  starting transfers between devices: 25.2 us -> 23.5 us
  waiting for transfers between devices: 22.8 us -> 24.1 us
    ppermute x3, starting transfers between devices: 13 us -> 11 us  [neighbours(): lax.ppermute(up, axis, [(i, (i + 1) % size) for i in range(size)])]
  transfers between devices with their start and end apart: 15 -> 15, of which waited for: 8 -> 9; matrix products, arithmetic and copies ran while one was open for 0% -> 0% of each run, Pallas kernels for 10% -> 11%
where the time goes in v4:
time: 60.5 us; the launch traced here: 59.3 us
  waiting for transfers between devices  24.1 us (40%)
  starting transfers between devices  23.5 us (39%)
  Pallas kernels  10.9 us (18%)
  between operations  0.77 us (1%)
    ppermute x9, waiting for transfers between devices, send(): return lax.ppermute(tiles, 'node', [(i, i ^ r) for i in range(4)])  20 us
    ppermute x3, starting transfers between devices, neighbours(): lax.ppermute(up, axis, [(i, (i + 1) % size) for i in range(size)])  11 us
    ppermute x9, starting transfers between devices, send(): return lax.ppermute(tiles, 'node', [(i, i ^ r) for i in range(4)])  10 us
    ppermute x3, waiting for transfers between devices, neighbours(): lax.ppermute(down, axis, [((i + 1) % size, i) for i in range(size)])  2.91 us
    ppermute x3, starting transfers between devices, neighbours(): lax.ppermute(down, axis, [((i + 1) % size, i) for i in range(size)])  2.55 us
    pallas_call x1, Pallas kernels, shards(): call(start_kernel, [VMEM, VMEM, ANY], [tiles_of(20), tiles_of(2), shape(1...  1.95 us
    pallas_call x1, Pallas kernels, shards(): call(first_kernel, [VMEM, VMEM, ANY], [tiles_of(MAIN)] * 4 + [shape(5, 16...  1.9 us
    pallas_call x1, Pallas kernels, shards(): call(second_kernel, [VMEM] * 12, [tiles_of(20)] * 4, [scratch(8, 4), scra...  1.77 us
  transfers between devices with their start and end apart: 15, of which 9 were waited for; matrix products, arithmetic and copies ran while one was open for 0% of the time, Pallas kernels for 11%

profile of v4, /device:TPU:37, one launch (start us, length us, event | category | flops | bytes accessed | tf_op | source)
XLA Modules:
  0.0 59.3 jit_solution(14286760565447447884)
XLA Ops:
  0.0 0.0 copy-start
  0.0 1.2 %shard_map.46 = (f32[5,40,128]{2,1,0:T(8,128)S(1)}, f32[5,40,128]{2,1,0:T(8,128)S(1)}, f32[2,16,128]{2,1,0:T(8,128)S(1)}) custom-call(s32[2,16,128]{2,1,0:T(8,128)} %flag_hbm.1, f32[5,16,16,128]{3,2,1,0:T(8,128)} %bitcast.4, f32[5,16,16,128]{3,2,1,0:T(8,128)} %w_ref.3), custom_call_target="tpu_custom_call" | custom-call | flops 1 | bytes 1 | tf_op jit(solution)/shard_map/pallas_call | solution.py:586
  1.2 0.0 copy-start.1
  1.3 6.1 %collective-permute-start.5 = (f32[5,40,128]{2,1,0:T(8,128)S(1)}, f32[5,40,128]{2,1,0:T(8,128)S(1)}, u32[]{:S(2)}, u32[]{:S(2)}) collective-permute-start(f32[5,40,128]{2,1,0:T(8,128)S(1)} %get-tuple-element.35), channel_id=1, source_target_pairs={{0,1},{1,2},{2,3},{3,4},{4,5},{5,6},{6,7},{7,0},{8,9},{9,10},{10,1... | collective-permute-start | bytes 307208 | tf_op jit(solution)/shard_map/ppermute | solution.py:578
  7.3 2.5 %collective-permute-start.6 = (f32[5,40,128]{2,1,0:T(8,128)S(1)}, f32[5,40,128]{2,1,0:T(8,128)S(1)}, u32[]{:S(2)}, u32[]{:S(2)}) collective-permute-start(f32[5,40,128]{2,1,0:T(8,128)S(1)} %get-tuple-element.36), channel_id=1, source_target_pairs={{1,0},{2,1},{3,2},{4,3},{5,4},{6,5},{7,6},{0,7},{9,8},{10,9},{11,1... | collective-permute-start | bytes 307208 | tf_op jit(solution)/shard_map/ppermute | solution.py:579
  10.5 0.0 copy-done
  10.6 1.9 %shard_map.47 = (f32[18,16,128]{2,1,0:T(8,128)S(1)}, f32[18,16,128]{2,1,0:T(8,128)S(1)}, f32[18,16,128]{2,1,0:T(8,128)S(1)}, f32[18,16,128]{2,1,0:T(8,128)S(1)}, f32[5,16,16,128]{3,2,1,0:T(8,128)S(1)}) custom-call(f32[8,128]{1,0:T(8,128)S(1)} %broadcast_in_dim.8.power_ref, f32[5,16,16,128]{3,2,1,0:T(8,128)S(1)} %bitcast.5, ...), custom_call_target="tpu_custom_call" | custom-call | flops 1 | bytes 1 | tf_op jit(solution)/shard_map/pallas_call | solution.py:593
  12.5 2.0 %collective-permute-start = (f32[18,16,128]{2,1,0:T(8,128)S(1)}, f32[18,16,128]{2,1,0:T(8,128)S(1)}, u32[]{:S(2)}, u32[]{:S(2)}) collective-permute-start(f32[18,16,128]{2,1,0:T(8,128)S(1)} %get-tuple-element.29._after), channel_id=1, source_target_pairs={{0,128},{64,192},{128,0},{192,64},{1,129},{65,193},{129,1},{193,65... | collective-permute-start | bytes 442376 | tf_op jit(solution)/shard_map/ppermute | solution.py:583
  14.5 0.0 collective-permute-start.2
  14.5 0.0 copy-done.1
  14.5 2.4 %collective-permute-start.3 = (f32[16,16,128]{2,1,0:T(8,128)S(1)}, f32[16,16,128]{2,1,0:T(8,128)S(1)}, u32[]{:S(2)}, u32[]{:S(2)}) collective-permute-start(f32[16,16,128]{2,1,0:T(8,128)S(1)} %get-tuple-element.33), channel_id=1, source_target_pairs={{0,8},{8,16},{16,24},{24,32},{32,40},{40,48},{48,56},{56,0},{1,9},... | collective-permute-start | bytes 393224 | tf_op jit(solution)/shard_map/ppermute | solution.py:578
  16.9 0.0 collective-permute-done.5.slow_ref
  16.9 0.0 collective-permute-start.4
  16.9 0.0 collective-permute-done.6.shigh_ref
  17.0 0.7 %collective-permute-start.1 = (f32[18,16,128]{2,1,0:T(8,128)S(1)}, f32[18,16,128]{2,1,0:T(8,128)S(1)}, u32[]{:S(2)}, u32[]{:S(2)}) collective-permute-start(f32[18,16,128]{2,1,0:T(8,128)S(1)} %get-tuple-element.30), channel_id=1, source_target_pairs={{0,192},{64,128},{128,64},{192,0},{1,193},{65,129},{129,65},{193,1... | collective-permute-start | bytes 442376 | tf_op jit(solution)/shard_map/ppermute | solution.py:583
  17.7 1.2 %collective-permute-done.3.tlow_ref = f32[16,16,128]{2,1,0:T(8,128)S(1)} collective-permute-done((f32[16,16,128]{2,1,0:T(8,128)S(1)}, f32[16,16,128]{2,1,0:T(8,128)S(1)}, u32[]{:S(2)}, u32[]{:S(2)}) %collective-permute-start.3) | collective-permute-done | bytes 131104 | tf_op jit(solution)/shard_map/ppermute | solution.py:578
  18.9 2.4 %collective-permute-start.7 = (f32[16,128]{1,0:T(8,128)S(1)}, f32[16,128]{1,0:T(8,128)S(1)}, u32[]{:S(2)}, u32[]{:S(2)}) collective-permute-start(f32[16,128]{1,0:T(8,128)S(1)} %get-tuple-element.37), channel_id=1, source_target_pairs={{0,8},{8,16},{16,24},{24,32},{32,40},{40,48},{48,56},{56,0},{1,9},... | collective-permute-start | bytes 24584 | tf_op jit(solution)/shard_map/ppermute | solution.py:578
  21.3 0.3 collective-permute-done.4.thigh_ref
  21.6 0.0 collective-permute-start.8
  21.6 0.7 %shard_map.50.inner_ref = f32[4,7,16,128]{3,2,1,0:T(8,128)S(1)} custom-call(f32[8,128]{1,0:T(8,128)S(1)} %broadcast_in_dim.8.power_ref, f32[5,256,128]{2,1,0:T(8,128)S(1)} %bitcast.7, f32[16,16,128]{2,1,0:T(8,128)S(1)} %collective-permute-done.3.tlow_ref, f32[16,16,128]{2,1,0:T(8,128)S(1)} %collective-permute-done.4.thigh_ref, ...), custom_call_target="tpu_custom_call" | custom-call | flops 1 | bytes 1 | tf_op jit(solution)/shard_map/pallas_call | solution.py:601
  22.4 0.0 collective-permute-done.7.clow_ref
  22.4 2.6 %collective-permute-done.8.chigh_ref = f32[16,128]{1,0:T(8,128)S(1)} collective-permute-done((f32[16,128]{1,0:T(8,128)S(1)}, f32[16,128]{1,0:T(8,128)S(1)}, u32[]{:S(2)}, u32[]{:S(2)}) %collective-permute-start.8) | collective-permute-done | bytes 8224 | tf_op jit(solution)/shard_map/ppermute | solution.py:579
  25.0 0.0 collective-permute-done._a2.a2
  25.0 0.0 collective-permute-done.2._a1.a1
  25.0 1.5 %shard_map.51 = (f32[12,16,128]{2,1,0:T(8,128)S(1)}, f32[12,16,128]{2,1,0:T(8,128)S(1)}, f32[12,16,128]{2,1,0:T(8,128)S(1)}, f32[12,16,128]{2,1,0:T(8,128)S(1)}) custom-call(f32[8,128]{1,0:T(8,128)S(1)} %broadcast_in_dim.8.power_ref, f32[5,256,128]{2,1,0:T(8,128)S(1)} %bitcast.8, f32[16,16,128]{2,1,0:T(8,128)S(1)} %collective-permute-done.3.tlow_ref, ...), custom_call_target="tpu_custom_call" | custom-call | flops 1 | bytes 1 | tf_op jit(solution)/shard_map/pallas_call | solution.py:606
  26.5 3.3 %collective-permute-start.10 = (f32[12,16,128]{2,1,0:T(8,128)S(1)}, f32[12,16,128]{2,1,0:T(8,128)S(1)}, u32[]{:S(2)}, u32[]{:S(2)}) collective-permute-start(f32[12,16,128]{2,1,0:T(8,128)S(1)} %get-tuple-element.42._after), channel_id=1, source_target_pairs={{0,128},{64,192},{128,0},{192,64},{1,129},{65,193},{129,1},{193,65... | collective-permute-start | bytes 294920 | tf_op jit(solution)/shard_map/ppermute | solution.py:583
  29.8 0.0 collective-permute-start.11
  29.8 1.3 %collective-permute-start.9 = (f32[12,16,128]{2,1,0:T(8,128)S(1)}, f32[12,16,128]{2,1,0:T(8,128)S(1)}, u32[]{:S(2)}, u32[]{:S(2)}) collective-permute-start(f32[12,16,128]{2,1,0:T(8,128)S(1)} %get-tuple-element.41), channel_id=1, source_target_pairs={{0,64},{64,0},{128,192},{192,128},{1,65},{65,1},{129,193},{193,129... | collective-permute-start | bytes 294920 | tf_op jit(solution)/shard_map/ppermute | solution.py:583
  31.1 2.0 %shard_map.52 = (f32[20,16,128]{2,1,0:T(8,128)S(1)}, f32[2,16,128]{2,1,0:T(8,128)S(1)}, f32[16,128]{1,0:T(8,128)S(1)}) custom-call(f32[5,16,16,128]{3,2,1,0:T(8,128)S(1)} %copy-done.1, f32[2,16,128]{2,1,0:T(8,128)S(1)} %get-tuple-element.28._after.slip_ref, f32[12,16,128]{2,1,0:T(8,128)S(1)} %get-tuple-element.42._after), custom_call_target="tpu_custom_call" | custom-call | flops 1 | bytes 1 | tf_op jit(solution)/shard_map/pallas_call | solution.py:612
  33.1 0.1 shard_map.53.wxy_ref
  33.2 0.6 collective-permute-done.1.a3
  33.7 2.2 %collective-permute-done.10.b2 = f32[12,16,128]{2,1,0:T(8,128)S(1)} collective-permute-done((f32[12,16,128]{2,1,0:T(8,128)S(1)}, f32[12,16,128]{2,1,0:T(8,128)S(1)}, u32[]{:S(2)}, u32[]{:S(2)}) %collective-permute-start.10) | collective-permute-done | bytes 98336 | tf_op jit(solution)/shard_map/ppermute | solution.py:583
  36.0 3.1 %collective-permute-done.11.b3 = f32[12,16,128]{2,1,0:T(8,128)S(1)} collective-permute-done((f32[12,16,128]{2,1,0:T(8,128)S(1)}, f32[12,16,128]{2,1,0:T(8,128)S(1)}, u32[]{:S(2)}, u32[]{:S(2)}) %collective-permute-start.11) | collective-permute-done | bytes 98336 | tf_op jit(solution)/shard_map/ppermute | solution.py:583
  39.1 0.0 collective-permute-done.9.b1
  39.1 1.8 %shard_map.54 = (f32[20,16,128]{2,1,0:T(8,128)S(1)}, f32[20,16,128]{2,1,0:T(8,128)S(1)}, f32[20,16,128]{2,1,0:T(8,128)S(1)}, f32[20,16,128]{2,1,0:T(8,128)S(1)}) custom-call(f32[18,16,128]{2,1,0:T(8,128)S(1)} %collective-permute-done._a2.a2, f32[18,16,128]{2,1,0:T(8,128)S(1)} %collective-permute-done.1.a3, f32[8,128]{1,0:T(8,128)S(1)} %broadcast_in_dim.8.power_ref, ...), custom_call_target="tpu_custom_call" | custom-call | flops 1 | bytes 1 | tf_op jit(solution)/shard_map/pallas_call | solution.py:616
  40.9 1.0 %collective-permute-start.12 = (f32[20,16,128]{2,1,0:T(8,128)S(1)}, f32[20,16,128]{2,1,0:T(8,128)S(1)}, u32[]{:S(2)}, u32[]{:S(2)}) collective-permute-start(f32[20,16,128]{2,1,0:T(8,128)S(1)} %get-tuple-element.48), channel_id=1, source_target_pairs={{0,64},{64,0},{128,192},{192,128},{1,65},{65,1},{129,193},{193,129... | collective-permute-start | bytes 491528 | tf_op jit(solution)/shard_map/ppermute | solution.py:583
  41.8 1.5 %collective-permute-start.13 = (f32[20,16,128]{2,1,0:T(8,128)S(1)}, f32[20,16,128]{2,1,0:T(8,128)S(1)}, u32[]{:S(2)}, u32[]{:S(2)}) collective-permute-start(f32[20,16,128]{2,1,0:T(8,128)S(1)} %get-tuple-element.49), channel_id=1, source_target_pairs={{0,128},{64,192},{128,0},{192,64},{1,129},{65,193},{129,1},{193,65... | collective-permute-start | bytes 491528 | tf_op jit(solution)/shard_map/ppermute | solution.py:583
  43.3 0.3 collective-permute-start.14
  43.6 3.7 %collective-permute-done.12.r1 = f32[20,16,128]{2,1,0:T(8,128)S(1)} collective-permute-done((f32[20,16,128]{2,1,0:T(8,128)S(1)}, f32[20,16,128]{2,1,0:T(8,128)S(1)}, u32[]{:S(2)}, u32[]{:S(2)}) %collective-permute-start.12) | collective-permute-done | bytes 163872 | tf_op jit(solution)/shard_map/ppermute | solution.py:583
  47.3 3.4 %collective-permute-done.13.r2 = f32[20,16,128]{2,1,0:T(8,128)S(1)} collective-permute-done((f32[20,16,128]{2,1,0:T(8,128)S(1)}, f32[20,16,128]{2,1,0:T(8,128)S(1)}, u32[]{:S(2)}, u32[]{:S(2)}) %collective-permute-start.13) | collective-permute-done | bytes 163872 | tf_op jit(solution)/shard_map/ppermute | solution.py:583
  50.7 7.0 %collective-permute-done.14.r3 = f32[20,16,128]{2,1,0:T(8,128)S(1)} collective-permute-done((f32[20,16,128]{2,1,0:T(8,128)S(1)}, f32[20,16,128]{2,1,0:T(8,128)S(1)}, u32[]{:S(2)}, u32[]{:S(2)}) %collective-permute-start.14) | collective-permute-done | bytes 163872 | tf_op jit(solution)/shard_map/ppermute | solution.py:583
  57.7 1.6 %shard_map.55 = f32[5,16,16,128]{3,2,1,0:T(8,128)} custom-call(f32[20,16,128]{2,1,0:T(8,128)S(1)} %get-tuple-element.47.r0, f32[20,16,128]{2,1,0:T(8,128)S(1)} %collective-permute-done.12.r1, f32[20,16,128]{2,1,0:T(8,128)S(1)} %collective-permute-done.13.r2, f32[20,16,128]{2,1,0:T(8,128)S(1)} %collective-permute-done.14.r3), custom_call_target="tpu_custom_call" | custom-call | flops 1 | bytes 1 | tf_op jit(solution)/shard_map/pallas_call | solution.py:622
  (3 shorter events, 0.0 us)
Async XLA Ops:
  0.0 10.6 %copy-start = (f32[1,5,16,16,128]{4,3,2,1,0:T(8,128)S(1)}, f32[1,5,16,16,128]{4,3,2,1,0:T(8,128)}, u32[]{:S(2)}) copy-start(f32[1,5,16,16,128]{4,3,2,1,0:T(8,128)} %param.5) | copy-start | bytes 1966084
  1.2 13.2 %copy-start.1 = (f32[5,16,16,128]{3,2,1,0:T(8,128)S(1)}, f32[5,16,16,128]{3,2,1,0:T(8,128)}, u32[]{:S(2)}) copy-start(f32[5,16,16,128]{3,2,1,0:T(8,128)} %w_ref.3) | copy-start | bytes 1966084
  1.3 15.7 %collective-permute-start.5 = (f32[5,40,128]{2,1,0:T(8,128)S(1)}, f32[5,40,128]{2,1,0:T(8,128)S(1)}, u32[]{:S(2)}, u32[]{:S(2)}) collective-permute-start(f32[5,40,128]{2,1,0:T(8,128)S(1)} %get-tuple-element.35), channel_id=1, source_target_pairs={{0,1},{1,2},{2,3},{3,4},{4,5},{5,6},{6,7},{7,0},{8,9},{9,10},{10,1... | collective-permute-start | bytes 307208 | tf_op jit(solution)/shard_map/ppermute | solution.py:578
  7.3 9.6 %collective-permute-start.6 = (f32[5,40,128]{2,1,0:T(8,128)S(1)}, f32[5,40,128]{2,1,0:T(8,128)S(1)}, u32[]{:S(2)}, u32[]{:S(2)}) collective-permute-start(f32[5,40,128]{2,1,0:T(8,128)S(1)} %get-tuple-element.36), channel_id=1, source_target_pairs={{1,0},{2,1},{3,2},{4,3},{5,4},{6,5},{7,6},{0,7},{9,8},{10,9},{11,1... | collective-permute-start | bytes 307208 | tf_op jit(solution)/shard_map/ppermute | solution.py:579
  12.5 12.5 %collective-permute-start = (f32[18,16,128]{2,1,0:T(8,128)S(1)}, f32[18,16,128]{2,1,0:T(8,128)S(1)}, u32[]{:S(2)}, u32[]{:S(2)}) collective-permute-start(f32[18,16,128]{2,1,0:T(8,128)S(1)} %get-tuple-element.29._after), channel_id=1, source_target_pairs={{0,128},{64,192},{128,0},{192,64},{1,129},{65,193},{129,1},{193,65... | collective-permute-start | bytes 442376 | tf_op jit(solution)/shard_map/ppermute | solution.py:583
  14.5 10.5 %collective-permute-start.2 = (f32[18,16,128]{2,1,0:T(8,128)S(1)}, f32[18,16,128]{2,1,0:T(8,128)S(1)}, u32[]{:S(2)}, u32[]{:S(2)}) collective-permute-start(f32[18,16,128]{2,1,0:T(8,128)S(1)} %get-tuple-element.32), channel_id=1, source_target_pairs={{0,64},{64,0},{128,192},{192,128},{1,65},{65,1},{129,193},{193,129... | collective-permute-start | bytes 442376 | tf_op jit(solution)/shard_map/ppermute | solution.py:583
  14.5 4.4 %collective-permute-start.3 = (f32[16,16,128]{2,1,0:T(8,128)S(1)}, f32[16,16,128]{2,1,0:T(8,128)S(1)}, u32[]{:S(2)}, u32[]{:S(2)}) collective-permute-start(f32[16,16,128]{2,1,0:T(8,128)S(1)} %get-tuple-element.33), channel_id=1, source_target_pairs={{0,8},{8,16},{16,24},{24,32},{32,40},{40,48},{48,56},{56,0},{1,9},... | collective-permute-start | bytes 393224 | tf_op jit(solution)/shard_map/ppermute | solution.py:578
  16.9 4.7 %collective-permute-start.4 = (f32[16,16,128]{2,1,0:T(8,128)S(1)}, f32[16,16,128]{2,1,0:T(8,128)S(1)}, u32[]{:S(2)}, u32[]{:S(2)}) collective-permute-start(f32[16,16,128]{2,1,0:T(8,128)S(1)} %get-tuple-element.34), channel_id=1, source_target_pairs={{8,0},{16,8},{24,16},{32,24},{40,32},{48,40},{56,48},{0,56},{9,1},... | collective-permute-start | bytes 393224 | tf_op jit(solution)/shard_map/ppermute | solution.py:579
  17.0 16.8 %collective-permute-start.1 = (f32[18,16,128]{2,1,0:T(8,128)S(1)}, f32[18,16,128]{2,1,0:T(8,128)S(1)}, u32[]{:S(2)}, u32[]{:S(2)}) collective-permute-start(f32[18,16,128]{2,1,0:T(8,128)S(1)} %get-tuple-element.30), channel_id=1, source_target_pairs={{0,192},{64,128},{128,64},{192,0},{1,193},{65,129},{129,65},{193,1... | collective-permute-start | bytes 442376 | tf_op jit(solution)/shard_map/ppermute | solution.py:583
  18.9 3.5 %collective-permute-start.7 = (f32[16,128]{1,0:T(8,128)S(1)}, f32[16,128]{1,0:T(8,128)S(1)}, u32[]{:S(2)}, u32[]{:S(2)}) collective-permute-start(f32[16,128]{1,0:T(8,128)S(1)} %get-tuple-element.37), channel_id=1, source_target_pairs={{0,8},{8,16},{16,24},{24,32},{32,40},{40,48},{48,56},{56,0},{1,9},... | collective-permute-start | bytes 24584 | tf_op jit(solution)/shard_map/ppermute | solution.py:578
  21.6 3.4 %collective-permute-start.8 = (f32[16,128]{1,0:T(8,128)S(1)}, f32[16,128]{1,0:T(8,128)S(1)}, u32[]{:S(2)}, u32[]{:S(2)}) collective-permute-start(f32[16,128]{1,0:T(8,128)S(1)} %get-tuple-element.38), channel_id=1, source_target_pairs={{8,0},{16,8},{24,16},{32,24},{40,32},{48,40},{56,48},{0,56},{9,1},... | collective-permute-start | bytes 24584 | tf_op jit(solution)/shard_map/ppermute | solution.py:579
  26.5 9.4 %collective-permute-start.10 = (f32[12,16,128]{2,1,0:T(8,128)S(1)}, f32[12,16,128]{2,1,0:T(8,128)S(1)}, u32[]{:S(2)}, u32[]{:S(2)}) collective-permute-start(f32[12,16,128]{2,1,0:T(8,128)S(1)} %get-tuple-element.42._after), channel_id=1, source_target_pairs={{0,128},{64,192},{128,0},{192,64},{1,129},{65,193},{129,1},{193,65... | collective-permute-start | bytes 294920 | tf_op jit(solution)/shard_map/ppermute | solution.py:583
  29.8 9.3 %collective-permute-start.11 = (f32[12,16,128]{2,1,0:T(8,128)S(1)}, f32[12,16,128]{2,1,0:T(8,128)S(1)}, u32[]{:S(2)}, u32[]{:S(2)}) collective-permute-start(f32[12,16,128]{2,1,0:T(8,128)S(1)} %get-tuple-element.43), channel_id=1, source_target_pairs={{0,192},{64,128},{128,64},{192,0},{1,193},{65,129},{129,65},{193,1... | collective-permute-start | bytes 294920 | tf_op jit(solution)/shard_map/ppermute | solution.py:583
  29.8 9.3 %collective-permute-start.9 = (f32[12,16,128]{2,1,0:T(8,128)S(1)}, f32[12,16,128]{2,1,0:T(8,128)S(1)}, u32[]{:S(2)}, u32[]{:S(2)}) collective-permute-start(f32[12,16,128]{2,1,0:T(8,128)S(1)} %get-tuple-element.41), channel_id=1, source_target_pairs={{0,64},{64,0},{128,192},{192,128},{1,65},{65,1},{129,193},{193,129... | collective-permute-start | bytes 294920 | tf_op jit(solution)/shard_map/ppermute | solution.py:583
  40.9 6.4 %collective-permute-start.12 = (f32[20,16,128]{2,1,0:T(8,128)S(1)}, f32[20,16,128]{2,1,0:T(8,128)S(1)}, u32[]{:S(2)}, u32[]{:S(2)}) collective-permute-start(f32[20,16,128]{2,1,0:T(8,128)S(1)} %get-tuple-element.48), channel_id=1, source_target_pairs={{0,64},{64,0},{128,192},{192,128},{1,65},{65,1},{129,193},{193,129... | collective-permute-start | bytes 491528 | tf_op jit(solution)/shard_map/ppermute | solution.py:583
  41.8 8.9 %collective-permute-start.13 = (f32[20,16,128]{2,1,0:T(8,128)S(1)}, f32[20,16,128]{2,1,0:T(8,128)S(1)}, u32[]{:S(2)}, u32[]{:S(2)}) collective-permute-start(f32[20,16,128]{2,1,0:T(8,128)S(1)} %get-tuple-element.49), channel_id=1, source_target_pairs={{0,128},{64,192},{128,0},{192,64},{1,129},{65,193},{129,1},{193,65... | collective-permute-start | bytes 491528 | tf_op jit(solution)/shard_map/ppermute | solution.py:583
  43.3 14.4 %collective-permute-start.14 = (f32[20,16,128]{2,1,0:T(8,128)S(1)}, f32[20,16,128]{2,1,0:T(8,128)S(1)}, u32[]{:S(2)}, u32[]{:S(2)}) collective-permute-start(f32[20,16,128]{2,1,0:T(8,128)S(1)} %get-tuple-element.50), channel_id=1, source_target_pairs={{0,192},{64,128},{128,64},{192,0},{1,193},{65,129},{129,65},{193,1... | collective-permute-start | bytes 491528 | tf_op jit(solution)/shard_map/ppermute | solution.py:583

commit v5 on v4

--- a/solution.py
+++ b/solution.py
@@ -143,15 +143,17 @@
     return 1.0 - 2.0 * flags.astype(jnp.float32)
 
 
-def tile_kernel(s_ref, w_ref, slip_ref, _after, up_ref, down_ref):
-    for ref, up in ((up_ref, True), (down_ref, False)):
-        for f in range(5):
-            ref[f] = ((s_ref[f, 14]) if up else s_ref[f, 0])
-            ref[5 + f] = ((s_ref[f, 15]) if up else s_ref[f, 1])
-            ref[10 + f] = ((w_ref[f, 15]) if up else w_ref[f, 0])
-        ref[15] = jnp.zeros((16, 128), jnp.float32)
-        for side in range(2):
-            ref[15, pl.ds(side, 1), :] = ((slip_ref[side, pl.ds(15, 1), :]) if up else slip_ref[side, pl.ds(0, 1), :])
+def tile_kernel(s_ref, w_ref, _after, up_ref, down_ref):
+    me = lax.axis_index("node")
+    _, lane = iotas()
+    for ref, rows, x in ((up_ref, (14, 15), 15), (down_ref, (0, 1), 0)):
+        for f in range(5):
+            ref[f] = s_ref[f, rows[0]]
+            ref[5 + f] = s_ref[f, rows[1]]
+        own = [pltpu.roll(w_ref[f, x], (f + 4 - me) % 4 * 32, 1) for f in range(5)]
+        ref[10] = jnp.where(lane < 32, own[0], jnp.where(lane < 64, own[1], jnp.where(lane < 96, own[2], own[3])))
+        ref[11] = own[4]
+        ref[12] = own[4]
 
 
 def first_kernel(power_ref, s_ref, _after, m0, m1, m2, m3, rates, der, packed):
@@ -188,18 +190,24 @@
     lax.fori_loop(0, 4, column, 0)
     for r, m in enumerate((m0, m1, m2, m3)):
         q = me ^ r
+
+        def put(k, tile):
+            m[pl.ds(14 * k + 1, 14), :] = tile[1:15]
+
+        m[pl.ds(0, 1), :] = jnp.zeros((1, 128), jnp.float32)
+        m[pl.ds(14 * MAIN + 1, 3), :] = jnp.zeros((3, 128), jnp.float32)
         for f in range(5):
             for xq in (1, 2):
-                m[2 * f + xq - 1] = packed[q, f * 4 + xq]
+                put(2 * f + xq - 1, packed[q, f * 4 + xq])
         for p in range(2):
             a0, a3 = packed[q, 8 * p], packed[q, 8 * p + 3]
             b0, b3 = packed[q, 8 * p + 4], packed[q, 8 * p + 7]
-            m[10 + 3 * p] = jnp.where(lane < 32, b3, a0)
-            m[11 + 3 * p] = jnp.where(lane >= 96, b0, a3)
-            m[12 + 3 * p] = jnp.where(
-                lane < 32, pltpu.roll(b3, 96, 1), jnp.where(lane < 96, b0, pltpu.roll(b3, 32, 1)))
-        m[16] = packed[q, 16]
-        m[17] = packed[q, 19]
+            put(10 + 3 * p, jnp.where(lane < 32, b3, a0))
+            put(11 + 3 * p, jnp.where(lane >= 96, b0, a3))
+            put(12 + 3 * p, jnp.where(
+                lane < 32, pltpu.roll(b3, 96, 1), jnp.where(lane < 96, b0, pltpu.roll(b3, 32, 1))))
+        put(16, packed[q, 16])
+        put(17, packed[q, 19])
 
 
 def start_kernel(w_ref, slip_ref, _after, wq_ref, wz_ref, slipq_ref):
@@ -250,10 +258,12 @@
     slip_ref[...] = slip_of(flags[...])
 
 
-def corner_kernel(slow_ref, shigh_ref, up_ref, down_ref):
+def corner_kernel(slow_ref, shigh_ref, slip_ref, up_ref, down_ref):
     below, above = reads(slow_ref, shigh_ref)
     for ref, up in ((up_ref, True), (down_ref, False)):
-        ref[pl.ds(10, 6), :] = jnp.zeros((6, 128), jnp.float32)
+        for side in range(2):
+            ref[pl.ds(10 + side, 1), :] = slip_ref[side, pl.ds(15 if up else 0, 1), :]
+        ref[pl.ds(12, 4), :] = jnp.zeros((4, 128), jnp.float32)
         for f in range(5):
             ref[pl.ds(f, 1), :] = ((below(f, pl.ds(31, 1))) if up else below(f, pl.ds(16, 1)))
             ref[pl.ds(5 + f, 1), :] = ((above(f, pl.ds(15, 1))) if up else above(f, pl.ds(0, 1)))
@@ -304,16 +314,13 @@
             out_ref[q, 5 + side] = out[q]
 
 
-def edge_kernel(power_ref, s_ref, tlow_ref, thigh_ref, slow_ref, shigh_ref, clow_ref, chigh_ref, slip_ref,
-                inner_ref, _a1, _a2, e0, e1, e2, e3, ext, yh, band, edge):
+def edge_kernel(power_ref, s_ref, slow_ref, shigh_ref, clow_ref, chigh_ref, slip_ref,
+                inner_ref, ext, _a1, _a2, e0, e1, e2, e3, yh, band, edge):
     me, t0, t7, s0, s7 = edges()
     sub, lane = iotas()
     power = power_ref[0:1, :]
-    lo, hi = reads(tlow_ref, thigh_ref)
     corner_lo, corner_hi = reads(clow_ref, chigh_ref)
     below_row, above_row = reads(slow_ref, shigh_ref)
-    fill_ext(ext, s_ref, tlow_ref, thigh_ref, t0, t7)
-    ext[5], ext[6], ext[7] = derived(ext[0], ext[1], power)
 
     for side in range(2):
         ref = (below_row, above_row)[side]
@@ -321,8 +328,8 @@
         y, inward = ((0, 1), (15, 14))[side]
         wall = (s0, s7)[side]
         slip = slip_ref[side]
-        slip_lo = lo(15, pl.ds(side, 1))
-        slip_hi = hi(15, pl.ds(side, 1))
+        slip_lo = corner_lo(pl.ds(10 + side, 1))
+        slip_hi = corner_hi(pl.ds(10 + side, 1))
         for f in range(5):
             def ghost(value, flag):
                 return -value if f == 3 else value * flag if f in (2, 4) else value
@@ -410,8 +417,8 @@
     lo, hi = reads(tlow_ref, thigh_ref)
     below, above = reads(slow_ref, shigh_ref)
     for f in range(5):
-        a = pltpu.roll(lo(10 + f), (5 - me) % 4 * 32, 1)
-        b = pltpu.roll(hi(10 + f), (6 - me) % 4 * 32, 1)
+        a = pltpu.roll(lo(10 + f // 4), (5 - f % 4) % 4 * 32, 1)
+        b = pltpu.roll(hi(10 + f // 4), (6 - f % 4) % 4 * 32, 1)
         wxy_ref[f] = jnp.where(
             lane < 32, wq_ref[f * 4], jnp.where(lane < 64, a, jnp.where(lane < 96, b, wq_ref[f * 4 + 3])))
         wxy_ref[5 + f, pl.ds(4, 4), :] = below(f, pl.ds(32, 4))
@@ -431,8 +438,7 @@
     slip = slipq_ref[...]
     at_lower = jnp.logical_and(jnp.logical_and(sub >= 4, sub < 8), s0)
     at_upper = jnp.logical_and(jnp.logical_and(sub >= 8, sub < 12), s7)
-    arrived = ((a0, 0), (a1, 0), (a2, 0), (a3, 0))
-    edge = ((b0, 0), (b1, 0), (b2, 0), (b3, 0))
+    arrived, edge = (a0, a1, a2, a3), (b0, b1, b2, b3)
     weights = relative_weights(me)
     for m in range(4):
         for r in range(4):
@@ -443,8 +449,8 @@
 
         def mix(refs, k):
             out = None
-            for r, (ref, base) in enumerate(refs):
-                term = weight[r] * ref[base + k]
+            for r, ref in enumerate(refs):
+                term = weight[r] * (ref[pl.ds(14 * k, 16), :] if refs is arrived else ref[k])
                 out = term if out is None else out + term
             return out
 
@@ -534,7 +540,7 @@
     lax.fori_loop(0, 20, combine, 0, unroll=4)
 
 
-def last_kernel(r0, r1, r2, r3, out_hbm, quarter, out, sems):
+def last_kernel(r2, r3, r1, r0, out_hbm, quarter, out, sems):
     me = lax.axis_index("node")
     _, lane = iotas()
     def copy(f):
@@ -591,22 +597,22 @@
     slab = neighbours(slab_near, slab_next, "slab")
 
     m0, m1, m2, m3, rates = call(
-        first_kernel, [VMEM, VMEM, ANY], [tiles_of(MAIN)] * 4 + [shape(5, 16, 16, 128)],
+        first_kernel, [VMEM, VMEM, ANY], [shape(256, 128)] * 4 + [shape(5, 16, 16, 128)],
         [scratch(3, 16), scratch(4, 20)])(power, state, slip)
     a2, a3, a1 = send(m2, 2), send(m3, 3), send(m1, 1)
 
-    tile = neighbours(*call(tile_kernel, [VMEM] * 3 + [ANY], [tiles_of(16)] * 2)(
-        state, start_state, slip, m2), "tile")
-
-    inner, = call(
-        inner_kernel, [VMEM] * 5, [shape(4, 7, 16, 128)], [scratch(8, 8)])(power, flat, *tile, rates)
-
-    corner = neighbours(*call(corner_kernel, [VMEM] * 2, [shape(16, 128)] * 2)(*slab), "tile")
+    tile = neighbours(*call(tile_kernel, [VMEM] * 2 + [ANY], [tiles_of(13)] * 2)(
+        state, start_state, m2), "tile")
+
+    inner, ext = call(
+        inner_kernel, [VMEM] * 5, [shape(4, 7, 16, 128), shape(8, 8, 16, 128)])(power, flat, *tile, rates)
+
+    corner = neighbours(*call(corner_kernel, [VMEM] * 3, [shape(16, 128)] * 2)(*slab, slip), "tile")
 
     e0, e1, e2, e3 = call(
-        edge_kernel, [VMEM] * 10 + [ANY] * 2, [tiles_of(EDGE)] * 4,
-        [scratch(8, 8), pltpu.VMEM((8, 2, 24, 128), jnp.float32), scratch(8, 2, 4), scratch(4, EDGE)])(
-        power, flat, *tile, *slab, *corner, slip, inner, a1, a2)
+        edge_kernel, [VMEM] * 9 + [ANY] * 2, [tiles_of(EDGE)] * 4,
+        [pltpu.VMEM((8, 2, 24, 128), jnp.float32), scratch(8, 2, 4), scratch(4, EDGE)])(
+        power, flat, *slab, *corner, slip, inner, ext, a1, a2)
     b2, b3, b1 = send(e2, 2), send(e3, 3), send(e1, 1)
 
     wq, wz, slipq = call(
@@ -621,7 +627,7 @@
 
     result, = call(
         last_kernel, [VMEM] * 4, [shape(5, 16, 16, 128)], [scratch(4, 20), scratch(5, 16), dma(5)], HBM)(
-        outs[0], back[1], back[2], back[3])
+        back[2], back[3], back[1], outs[0])
     return result[None]
 
 

time: 60.5 us -> 59.1 us (0.977); the launches traced: 59.3 us -> 58.7 us
  waiting for transfers between devices: 24.1 us -> 22.4 us
  starting transfers between devices: 23.5 us -> 24.6 us
    ppermute x9, waiting for transfers between devices: 20 us -> 18.5 us  [send(): return lax.ppermute(tiles, 'node', [(i, i ^ r) for i in range(4)])]
    ppermute x9, starting transfers between devices: 10 us -> 11.1 us  [send(): return lax.ppermute(tiles, 'node', [(i, i ^ r) for i in range(4)])]
  transfers between devices with their start and end apart: 15 -> 15, of which waited for: 9 -> 7; matrix products, arithmetic and copies ran while one was open for 0% -> 0% of each run, Pallas kernels for 11% -> 11%
where the time goes in v5:
time: 59.1 us; the launch traced here: 58.7 us
  starting transfers between devices  24.6 us (42%)
  waiting for transfers between devices  22.4 us (38%)
  Pallas kernels  11 us (19%)
  between operations  0.77 us (1%)
    ppermute x9, waiting for transfers between devices, send(): return lax.ppermute(tiles, 'node', [(i, i ^ r) for i in range(4)])  18.5 us
    ppermute x9, starting transfers between devices, send(): return lax.ppermute(tiles, 'node', [(i, i ^ r) for i in range(4)])  11.1 us
    ppermute x3, starting transfers between devices, neighbours(): lax.ppermute(up, axis, [(i, (i + 1) % size) for i in range(size)])  10.9 us
    ppermute x3, waiting for transfers between devices, neighbours(): lax.ppermute(down, axis, [((i + 1) % size, i) for i in range(size)])  2.9 us
    ppermute x3, starting transfers between devices, neighbours(): lax.ppermute(down, axis, [((i + 1) % size, i) for i in range(size)])  2.55 us
    pallas_call x1, Pallas kernels, shards(): call(start_kernel, [VMEM, VMEM, ANY], [tiles_of(20), tiles_of(2), shape(1...  1.95 us
    pallas_call x1, Pallas kernels, shards(): call(first_kernel, [VMEM, VMEM, ANY], [shape(256, 128)] * 4 + [shape(5, 1...  1.9 us
    pallas_call x1, Pallas kernels, shards(): call(second_kernel, [VMEM] * 12, [tiles_of(20)] * 4, [scratch(8, 4), scra...  1.84 us
  transfers between devices with their start and end apart: 15, of which 7 were waited for; matrix products, arithmetic and copies ran while one was open for 0% of the time, Pallas kernels for 11%

profile of v5, /device:TPU:37, one launch (start us, length us, event | category | flops | bytes accessed | tf_op | source)
XLA Modules:
  0.0 58.7 jit_solution(3954169041752727879)
XLA Ops:
  0.0 0.0 copy-start
  0.0 1.2 %shard_map.46 = (f32[5,40,128]{2,1,0:T(8,128)S(1)}, f32[5,40,128]{2,1,0:T(8,128)S(1)}, f32[2,16,128]{2,1,0:T(8,128)S(1)}) custom-call(s32[2,16,128]{2,1,0:T(8,128)} %flag_hbm.1, f32[5,16,16,128]{3,2,1,0:T(8,128)} %bitcast.4, f32[5,16,16,128]{3,2,1,0:T(8,128)} %w_ref.3), custom_call_target="tpu_custom_call" | custom-call | flops 1 | bytes 1 | tf_op jit(solution)/shard_map/pallas_call | solution.py:592
  1.2 0.0 copy-start.1
  1.3 6.1 %collective-permute-start.3 = (f32[5,40,128]{2,1,0:T(8,128)S(1)}, f32[5,40,128]{2,1,0:T(8,128)S(1)}, u32[]{:S(2)}, u32[]{:S(2)}) collective-permute-start(f32[5,40,128]{2,1,0:T(8,128)S(1)} %get-tuple-element.35), channel_id=1, source_target_pairs={{0,1},{1,2},{2,3},{3,4},{4,5},{5,6},{6,7},{7,0},{8,9},{9,10},{10,1... | collective-permute-start | bytes 307208 | tf_op jit(solution)/shard_map/ppermute | solution.py:584
  7.3 2.5 %collective-permute-start.4 = (f32[5,40,128]{2,1,0:T(8,128)S(1)}, f32[5,40,128]{2,1,0:T(8,128)S(1)}, u32[]{:S(2)}, u32[]{:S(2)}) collective-permute-start(f32[5,40,128]{2,1,0:T(8,128)S(1)} %get-tuple-element.36), channel_id=1, source_target_pairs={{1,0},{2,1},{3,2},{4,3},{5,4},{6,5},{7,6},{0,7},{9,8},{10,9},{11,1... | collective-permute-start | bytes 307208 | tf_op jit(solution)/shard_map/ppermute | solution.py:585
  10.5 0.0 copy-done
  10.6 1.9 %shard_map.47 = (f32[256,128]{1,0:T(8,128)S(1)}, f32[256,128]{1,0:T(8,128)S(1)}, f32[256,128]{1,0:T(8,128)S(1)}, f32[256,128]{1,0:T(8,128)S(1)}, f32[5,16,16,128]{3,2,1,0:T(8,128)S(1)}) custom-call(f32[8,128]{1,0:T(8,128)S(1)} %broadcast_in_dim.8.power_ref, f32[5,16,16,128]{3,2,1,0:T(8,128)S(1)} %bitcast.5, f32[2,16,128]{2,1,0:T(8,128)S(1)} %get-tuple-element.30._after.slip_ref), custom_call_target="tpu_custom_call" | custom-call | flops 1 | bytes 1 | tf_op jit(solution)/shard_map/pallas_call | solution.py:599
  12.5 2.0 %collective-permute-start = (f32[256,128]{1,0:T(8,128)S(1)}, f32[256,128]{1,0:T(8,128)S(1)}, u32[]{:S(2)}, u32[]{:S(2)}) collective-permute-start(f32[256,128]{1,0:T(8,128)S(1)} %get-tuple-element.31._after), channel_id=1, source_target_pairs={{0,128},{64,192},{128,0},{192,64},{1,129},{65,193},{129,1},{193,65... | collective-permute-start | bytes 393224 | tf_op jit(solution)/shard_map/ppermute | solution.py:589
  14.5 0.0 collective-permute-start.2
  14.5 0.0 copy-done.1
  14.5 0.1 shard_map.49
  14.6 2.4 %collective-permute-start.7 = (f32[13,16,128]{2,1,0:T(8,128)S(1)}, f32[13,16,128]{2,1,0:T(8,128)S(1)}, u32[]{:S(2)}, u32[]{:S(2)}) collective-permute-start(f32[13,16,128]{2,1,0:T(8,128)S(1)} %get-tuple-element.39), channel_id=1, source_target_pairs={{0,8},{8,16},{16,24},{24,32},{32,40},{40,48},{48,56},{56,0},{1,9},... | collective-permute-start | bytes 319496 | tf_op jit(solution)/shard_map/ppermute | solution.py:584
  17.0 0.0 collective-permute-done.3.slow_ref
  17.0 0.0 collective-permute-start.8
  17.0 0.0 collective-permute-done.4.shigh_ref
  17.0 0.7 %collective-permute-start.1 = (f32[256,128]{1,0:T(8,128)S(1)}, f32[256,128]{1,0:T(8,128)S(1)}, u32[]{:S(2)}, u32[]{:S(2)}) collective-permute-start(f32[256,128]{1,0:T(8,128)S(1)} %get-tuple-element.32), channel_id=1, source_target_pairs={{0,192},{64,128},{128,64},{192,0},{1,193},{65,129},{129,65},{193,1... | collective-permute-start | bytes 393224 | tf_op jit(solution)/shard_map/ppermute | solution.py:589
  17.7 1.0 %collective-permute-done.7.tlow_ref = f32[13,16,128]{2,1,0:T(8,128)S(1)} collective-permute-done((f32[13,16,128]{2,1,0:T(8,128)S(1)}, f32[13,16,128]{2,1,0:T(8,128)S(1)}, u32[]{:S(2)}, u32[]{:S(2)}) %collective-permute-start.7) | collective-permute-done | bytes 106528 | tf_op jit(solution)/shard_map/ppermute | solution.py:584
  18.7 2.4 %collective-permute-start.5 = (f32[16,128]{1,0:T(8,128)S(1)}, f32[16,128]{1,0:T(8,128)S(1)}, u32[]{:S(2)}, u32[]{:S(2)}) collective-permute-start(f32[16,128]{1,0:T(8,128)S(1)} %get-tuple-element.37), channel_id=1, source_target_pairs={{0,8},{8,16},{16,24},{24,32},{32,40},{40,48},{48,56},{56,0},{1,9},... | collective-permute-start | bytes 24584 | tf_op jit(solution)/shard_map/ppermute | solution.py:584
  21.2 0.3 collective-permute-done.8.thigh_ref
  21.4 0.0 collective-permute-start.6
  21.5 0.7 %shard_map.50 = (f32[4,7,16,128]{3,2,1,0:T(8,128)S(1)}, f32[8,8,16,128]{3,2,1,0:T(8,128)S(1)}) custom-call(f32[8,128]{1,0:T(8,128)S(1)} %broadcast_in_dim.8.power_ref, f32[5,256,128]{2,1,0:T(8,128)S(1)} %bitcast.7, f32[13,16,128]{2,1,0:T(8,128)S(1)} %collective-permute-done.7.tlow_ref, f32[13,16,128]{2,1,0:T(8,128)S(1)} %collective-permute-done.8.thigh_ref, ...), custom_call_target="tpu_custom_call" | custom-call | flops 1 | bytes 1 | tf_op jit(solution)/shard_map/pallas_call | solution.py:607
  22.2 0.0 collective-permute-done.5.clow_ref
  22.2 2.6 %collective-permute-done.6.chigh_ref = f32[16,128]{1,0:T(8,128)S(1)} collective-permute-done((f32[16,128]{1,0:T(8,128)S(1)}, f32[16,128]{1,0:T(8,128)S(1)}, u32[]{:S(2)}, u32[]{:S(2)}) %collective-permute-start.6) | collective-permute-done | bytes 8224 | tf_op jit(solution)/shard_map/ppermute | solution.py:585
  24.8 0.0 collective-permute-done._a2.a2
  24.8 0.0 collective-permute-done.2._a1.a1
  24.8 1.5 %shard_map.51 = (f32[12,16,128]{2,1,0:T(8,128)S(1)}, f32[12,16,128]{2,1,0:T(8,128)S(1)}, f32[12,16,128]{2,1,0:T(8,128)S(1)}, f32[12,16,128]{2,1,0:T(8,128)S(1)}) custom-call(f32[8,128]{1,0:T(8,128)S(1)} %broadcast_in_dim.8.power_ref, f32[5,256,128]{2,1,0:T(8,128)S(1)} %bitcast.8, f32[5,40,128]{2,1,0:T(8,128)S(1)} %collective-permute-done.3.slow_ref, ...), custom_call_target="tpu_custom_call" | custom-call | flops 1 | bytes 1 | tf_op jit(solution)/shard_map/pallas_call | solution.py:612
  26.3 3.5 %collective-permute-start.10 = (f32[12,16,128]{2,1,0:T(8,128)S(1)}, f32[12,16,128]{2,1,0:T(8,128)S(1)}, u32[]{:S(2)}, u32[]{:S(2)}) collective-permute-start(f32[12,16,128]{2,1,0:T(8,128)S(1)} %get-tuple-element.46._after), channel_id=1, source_target_pairs={{0,128},{64,192},{128,0},{192,64},{1,129},{65,193},{129,1},{193,65... | collective-permute-start | bytes 294920 | tf_op jit(solution)/shard_map/ppermute | solution.py:589
  29.8 0.0 collective-permute-start.11
  29.8 1.3 %collective-permute-start.9 = (f32[12,16,128]{2,1,0:T(8,128)S(1)}, f32[12,16,128]{2,1,0:T(8,128)S(1)}, u32[]{:S(2)}, u32[]{:S(2)}) collective-permute-start(f32[12,16,128]{2,1,0:T(8,128)S(1)} %get-tuple-element.45), channel_id=1, source_target_pairs={{0,64},{64,0},{128,192},{192,128},{1,65},{65,1},{129,193},{193,129... | collective-permute-start | bytes 294920 | tf_op jit(solution)/shard_map/ppermute | solution.py:589
  31.1 2.0 %shard_map.52 = (f32[20,16,128]{2,1,0:T(8,128)S(1)}, f32[2,16,128]{2,1,0:T(8,128)S(1)}, f32[16,128]{1,0:T(8,128)S(1)}) custom-call(f32[5,16,16,128]{3,2,1,0:T(8,128)S(1)} %copy-done.1, f32[2,16,128]{2,1,0:T(8,128)S(1)} %get-tuple-element.30._after.slip_ref, f32[12,16,128]{2,1,0:T(8,128)S(1)} %get-tuple-element.46._after), custom_call_target="tpu_custom_call" | custom-call | flops 1 | bytes 1 | tf_op jit(solution)/shard_map/pallas_call | solution.py:618
  33.0 0.1 shard_map.53.wxy_ref
  33.1 0.0 collective-permute-done.1.a3
  33.1 1.7 %collective-permute-done.10.b2 = f32[12,16,128]{2,1,0:T(8,128)S(1)} collective-permute-done((f32[12,16,128]{2,1,0:T(8,128)S(1)}, f32[12,16,128]{2,1,0:T(8,128)S(1)}, u32[]{:S(2)}, u32[]{:S(2)}) %collective-permute-start.10) | collective-permute-done | bytes 98336 | tf_op jit(solution)/shard_map/ppermute | solution.py:589
  34.8 3.8 %collective-permute-done.11.b3 = f32[12,16,128]{2,1,0:T(8,128)S(1)} collective-permute-done((f32[12,16,128]{2,1,0:T(8,128)S(1)}, f32[12,16,128]{2,1,0:T(8,128)S(1)}, u32[]{:S(2)}, u32[]{:S(2)}) %collective-permute-start.11) | collective-permute-done | bytes 98336 | tf_op jit(solution)/shard_map/ppermute | solution.py:589
  38.6 0.0 collective-permute-done.9.b1
  38.6 1.8 %shard_map.54 = (f32[20,16,128]{2,1,0:T(8,128)S(1)}, f32[20,16,128]{2,1,0:T(8,128)S(1)}, f32[20,16,128]{2,1,0:T(8,128)S(1)}, f32[20,16,128]{2,1,0:T(8,128)S(1)}) custom-call(f32[256,128]{1,0:T(8,128)S(1)} %collective-permute-done._a2.a2, f32[256,128]{1,0:T(8,128)S(1)} %collective-permute-done.1.a3, f32[8,128]{1,0:T(8,128)S(1)} %broadcast_in_dim.8.power_ref, ...), custom_call_target="tpu_custom_call" | custom-call | flops 1 | bytes 1 | tf_op jit(solution)/shard_map/pallas_call | solution.py:622
  40.4 1.0 %collective-permute-start.12 = (f32[20,16,128]{2,1,0:T(8,128)S(1)}, f32[20,16,128]{2,1,0:T(8,128)S(1)}, u32[]{:S(2)}, u32[]{:S(2)}) collective-permute-start(f32[20,16,128]{2,1,0:T(8,128)S(1)} %get-tuple-element.51), channel_id=1, source_target_pairs={{0,128},{64,192},{128,0},{192,64},{1,129},{65,193},{129,1},{193,65... | collective-permute-start | bytes 491528 | tf_op jit(solution)/shard_map/ppermute | solution.py:589
  41.5 0.9 %collective-permute-start.13 = (f32[20,16,128]{2,1,0:T(8,128)S(1)}, f32[20,16,128]{2,1,0:T(8,128)S(1)}, u32[]{:S(2)}, u32[]{:S(2)}) collective-permute-start(f32[20,16,128]{2,1,0:T(8,128)S(1)} %get-tuple-element.52), channel_id=1, source_target_pairs={{0,192},{64,128},{128,64},{192,0},{1,193},{65,129},{129,65},{193,1... | collective-permute-start | bytes 491528 | tf_op jit(solution)/shard_map/ppermute | solution.py:589
  42.4 1.7 %collective-permute-start.14 = (f32[20,16,128]{2,1,0:T(8,128)S(1)}, f32[20,16,128]{2,1,0:T(8,128)S(1)}, u32[]{:S(2)}, u32[]{:S(2)}) collective-permute-start(f32[20,16,128]{2,1,0:T(8,128)S(1)} %get-tuple-element.53), channel_id=1, source_target_pairs={{0,64},{64,0},{128,192},{192,128},{1,65},{65,1},{129,193},{193,129... | collective-permute-start | bytes 491528 | tf_op jit(solution)/shard_map/ppermute | solution.py:589
  44.1 8.0 %collective-permute-done.12.r2 = f32[20,16,128]{2,1,0:T(8,128)S(1)} collective-permute-done((f32[20,16,128]{2,1,0:T(8,128)S(1)}, f32[20,16,128]{2,1,0:T(8,128)S(1)}, u32[]{:S(2)}, u32[]{:S(2)}) %collective-permute-start.12) | collective-permute-done | bytes 163872 | tf_op jit(solution)/shard_map/ppermute | solution.py:589
  52.1 4.9 %collective-permute-done.13.r3 = f32[20,16,128]{2,1,0:T(8,128)S(1)} collective-permute-done((f32[20,16,128]{2,1,0:T(8,128)S(1)}, f32[20,16,128]{2,1,0:T(8,128)S(1)}, u32[]{:S(2)}, u32[]{:S(2)}) %collective-permute-start.13) | collective-permute-done | bytes 163872 | tf_op jit(solution)/shard_map/ppermute | solution.py:589
  57.1 0.0 collective-permute-done.14.r1
  57.1 1.6 %shard_map.55 = f32[5,16,16,128]{3,2,1,0:T(8,128)} custom-call(f32[20,16,128]{2,1,0:T(8,128)S(1)} %collective-permute-done.12.r2, f32[20,16,128]{2,1,0:T(8,128)S(1)} %collective-permute-done.13.r3, f32[20,16,128]{2,1,0:T(8,128)S(1)} %collective-permute-done.14.r1, f32[20,16,128]{2,1,0:T(8,128)S(1)} %get-tuple-element.54.r0), custom_call_target="tpu_custom_call" | custom-call | flops 1 | bytes 1 | tf_op jit(solution)/shard_map/pallas_call | solution.py:628
  (2 shorter events, 0.0 us)
Async XLA Ops:
  0.0 10.6 %copy-start = (f32[1,5,16,16,128]{4,3,2,1,0:T(8,128)S(1)}, f32[1,5,16,16,128]{4,3,2,1,0:T(8,128)}, u32[]{:S(2)}) copy-start(f32[1,5,16,16,128]{4,3,2,1,0:T(8,128)} %param.5) | copy-start | bytes 1966084
  1.2 13.2 %copy-start.1 = (f32[5,16,16,128]{3,2,1,0:T(8,128)S(1)}, f32[5,16,16,128]{3,2,1,0:T(8,128)}, u32[]{:S(2)}) copy-start(f32[5,16,16,128]{3,2,1,0:T(8,128)} %w_ref.3) | copy-start | bytes 1966084
  1.3 15.8 %collective-permute-start.3 = (f32[5,40,128]{2,1,0:T(8,128)S(1)}, f32[5,40,128]{2,1,0:T(8,128)S(1)}, u32[]{:S(2)}, u32[]{:S(2)}) collective-permute-start(f32[5,40,128]{2,1,0:T(8,128)S(1)} %get-tuple-element.35), channel_id=1, source_target_pairs={{0,1},{1,2},{2,3},{3,4},{4,5},{5,6},{6,7},{7,0},{8,9},{9,10},{10,1... | collective-permute-start | bytes 307208 | tf_op jit(solution)/shard_map/ppermute | solution.py:584
  7.3 9.7 %collective-permute-start.4 = (f32[5,40,128]{2,1,0:T(8,128)S(1)}, f32[5,40,128]{2,1,0:T(8,128)S(1)}, u32[]{:S(2)}, u32[]{:S(2)}) collective-permute-start(f32[5,40,128]{2,1,0:T(8,128)S(1)} %get-tuple-element.36), channel_id=1, source_target_pairs={{1,0},{2,1},{3,2},{4,3},{5,4},{6,5},{7,6},{0,7},{9,8},{10,9},{11,1... | collective-permute-start | bytes 307208 | tf_op jit(solution)/shard_map/ppermute | solution.py:585
  12.5 12.4 %collective-permute-start = (f32[256,128]{1,0:T(8,128)S(1)}, f32[256,128]{1,0:T(8,128)S(1)}, u32[]{:S(2)}, u32[]{:S(2)}) collective-permute-start(f32[256,128]{1,0:T(8,128)S(1)} %get-tuple-element.31._after), channel_id=1, source_target_pairs={{0,128},{64,192},{128,0},{192,64},{1,129},{65,193},{129,1},{193,65... | collective-permute-start | bytes 393224 | tf_op jit(solution)/shard_map/ppermute | solution.py:589
  14.5 10.3 %collective-permute-start.2 = (f32[256,128]{1,0:T(8,128)S(1)}, f32[256,128]{1,0:T(8,128)S(1)}, u32[]{:S(2)}, u32[]{:S(2)}) collective-permute-start(f32[256,128]{1,0:T(8,128)S(1)} %get-tuple-element.34), channel_id=1, source_target_pairs={{0,64},{64,0},{128,192},{192,128},{1,65},{65,1},{129,193},{193,129... | collective-permute-start | bytes 393224 | tf_op jit(solution)/shard_map/ppermute | solution.py:589
  14.6 4.1 %collective-permute-start.7 = (f32[13,16,128]{2,1,0:T(8,128)S(1)}, f32[13,16,128]{2,1,0:T(8,128)S(1)}, u32[]{:S(2)}, u32[]{:S(2)}) collective-permute-start(f32[13,16,128]{2,1,0:T(8,128)S(1)} %get-tuple-element.39), channel_id=1, source_target_pairs={{0,8},{8,16},{16,24},{24,32},{32,40},{40,48},{48,56},{56,0},{1,9},... | collective-permute-start | bytes 319496 | tf_op jit(solution)/shard_map/ppermute | solution.py:584
  17.0 4.4 %collective-permute-start.8 = (f32[13,16,128]{2,1,0:T(8,128)S(1)}, f32[13,16,128]{2,1,0:T(8,128)S(1)}, u32[]{:S(2)}, u32[]{:S(2)}) collective-permute-start(f32[13,16,128]{2,1,0:T(8,128)S(1)} %get-tuple-element.40), channel_id=1, source_target_pairs={{8,0},{16,8},{24,16},{32,24},{40,32},{48,40},{56,48},{0,56},{9,1},... | collective-permute-start | bytes 319496 | tf_op jit(solution)/shard_map/ppermute | solution.py:585
  17.0 16.1 %collective-permute-start.1 = (f32[256,128]{1,0:T(8,128)S(1)}, f32[256,128]{1,0:T(8,128)S(1)}, u32[]{:S(2)}, u32[]{:S(2)}) collective-permute-start(f32[256,128]{1,0:T(8,128)S(1)} %get-tuple-element.32), channel_id=1, source_target_pairs={{0,192},{64,128},{128,64},{192,0},{1,193},{65,129},{129,65},{193,1... | collective-permute-start | bytes 393224 | tf_op jit(solution)/shard_map/ppermute | solution.py:589
  18.7 3.5 %collective-permute-start.5 = (f32[16,128]{1,0:T(8,128)S(1)}, f32[16,128]{1,0:T(8,128)S(1)}, u32[]{:S(2)}, u32[]{:S(2)}) collective-permute-start(f32[16,128]{1,0:T(8,128)S(1)} %get-tuple-element.37), channel_id=1, source_target_pairs={{0,8},{8,16},{16,24},{24,32},{32,40},{40,48},{48,56},{56,0},{1,9},... | collective-permute-start | bytes 24584 | tf_op jit(solution)/shard_map/ppermute | solution.py:584
  21.4 3.4 %collective-permute-start.6 = (f32[16,128]{1,0:T(8,128)S(1)}, f32[16,128]{1,0:T(8,128)S(1)}, u32[]{:S(2)}, u32[]{:S(2)}) collective-permute-start(f32[16,128]{1,0:T(8,128)S(1)} %get-tuple-element.38), channel_id=1, source_target_pairs={{8,0},{16,8},{24,16},{32,24},{40,32},{48,40},{56,48},{0,56},{9,1},... | collective-permute-start | bytes 24584 | tf_op jit(solution)/shard_map/ppermute | solution.py:585
  26.3 8.5 %collective-permute-start.10 = (f32[12,16,128]{2,1,0:T(8,128)S(1)}, f32[12,16,128]{2,1,0:T(8,128)S(1)}, u32[]{:S(2)}, u32[]{:S(2)}) collective-permute-start(f32[12,16,128]{2,1,0:T(8,128)S(1)} %get-tuple-element.46._after), channel_id=1, source_target_pairs={{0,128},{64,192},{128,0},{192,64},{1,129},{65,193},{129,1},{193,65... | collective-permute-start | bytes 294920 | tf_op jit(solution)/shard_map/ppermute | solution.py:589
  29.8 8.8 %collective-permute-start.11 = (f32[12,16,128]{2,1,0:T(8,128)S(1)}, f32[12,16,128]{2,1,0:T(8,128)S(1)}, u32[]{:S(2)}, u32[]{:S(2)}) collective-permute-start(f32[12,16,128]{2,1,0:T(8,128)S(1)} %get-tuple-element.47), channel_id=1, source_target_pairs={{0,192},{64,128},{128,64},{192,0},{1,193},{65,129},{129,65},{193,1... | collective-permute-start | bytes 294920 | tf_op jit(solution)/shard_map/ppermute | solution.py:589
  29.8 8.8 %collective-permute-start.9 = (f32[12,16,128]{2,1,0:T(8,128)S(1)}, f32[12,16,128]{2,1,0:T(8,128)S(1)}, u32[]{:S(2)}, u32[]{:S(2)}) collective-permute-start(f32[12,16,128]{2,1,0:T(8,128)S(1)} %get-tuple-element.45), channel_id=1, source_target_pairs={{0,64},{64,0},{128,192},{192,128},{1,65},{65,1},{129,193},{193,129... | collective-permute-start | bytes 294920 | tf_op jit(solution)/shard_map/ppermute | solution.py:589
  40.4 11.7 %collective-permute-start.12 = (f32[20,16,128]{2,1,0:T(8,128)S(1)}, f32[20,16,128]{2,1,0:T(8,128)S(1)}, u32[]{:S(2)}, u32[]{:S(2)}) collective-permute-start(f32[20,16,128]{2,1,0:T(8,128)S(1)} %get-tuple-element.51), channel_id=1, source_target_pairs={{0,128},{64,192},{128,0},{192,64},{1,129},{65,193},{129,1},{193,65... | collective-permute-start | bytes 491528 | tf_op jit(solution)/shard_map/ppermute | solution.py:589
  41.5 15.6 %collective-permute-start.13 = (f32[20,16,128]{2,1,0:T(8,128)S(1)}, f32[20,16,128]{2,1,0:T(8,128)S(1)}, u32[]{:S(2)}, u32[]{:S(2)}) collective-permute-start(f32[20,16,128]{2,1,0:T(8,128)S(1)} %get-tuple-element.52), channel_id=1, source_target_pairs={{0,192},{64,128},{128,64},{192,0},{1,193},{65,129},{129,65},{193,1... | collective-permute-start | bytes 491528 | tf_op jit(solution)/shard_map/ppermute | solution.py:589
  42.4 14.7 %collective-permute-start.14 = (f32[20,16,128]{2,1,0:T(8,128)S(1)}, f32[20,16,128]{2,1,0:T(8,128)S(1)}, u32[]{:S(2)}, u32[]{:S(2)}) collective-permute-start(f32[20,16,128]{2,1,0:T(8,128)S(1)} %get-tuple-element.53), channel_id=1, source_target_pairs={{0,64},{64,0},{128,192},{192,128},{1,65},{65,1},{129,193},{193,129... | collective-permute-start | bytes 491528 | tf_op jit(solution)/shard_map/ppermute | solution.py:589

commit v6 on v5

--- a/solution.py
+++ b/solution.py
@@ -315,7 +315,7 @@
 
 
 def edge_kernel(power_ref, s_ref, slow_ref, shigh_ref, clow_ref, chigh_ref, slip_ref,
-                inner_ref, ext, _a1, _a2, e0, e1, e2, e3, yh, band, edge):
+                inner_ref, ext, e0, e1, e2, e3, yh, band, edge):
     me, t0, t7, s0, s7 = edges()
     sub, lane = iotas()
     power = power_ref[0:1, :]
@@ -610,9 +610,9 @@
     corner = neighbours(*call(corner_kernel, [VMEM] * 3, [shape(16, 128)] * 2)(*slab, slip), "tile")
 
     e0, e1, e2, e3 = call(
-        edge_kernel, [VMEM] * 9 + [ANY] * 2, [tiles_of(EDGE)] * 4,
+        edge_kernel, [VMEM] * 9, [tiles_of(EDGE)] * 4,
         [pltpu.VMEM((8, 2, 24, 128), jnp.float32), scratch(8, 2, 4), scratch(4, EDGE)])(
-        power, flat, *slab, *corner, slip, inner, ext, a1, a2)
+        power, flat, *slab, *corner, slip, inner, ext)
     b2, b3, b1 = send(e2, 2), send(e3, 3), send(e1, 1)
 
     wq, wz, slipq = call(

time: 59.1 us -> 58.4 us (0.988)
  waiting for transfers between devices: 22.4 us -> 20.8 us
  starting transfers between devices: 24.6 us -> 25.7 us
    ppermute x3, starting transfers between devices: 10.9 us -> 12.5 us  [neighbours(): lax.ppermute(up, axis, [(i, (i + 1) % size) for i in range(size)])]
    ppermute x9, waiting for transfers between devices: 18.5 us -> 17.9 us  [send(): return lax.ppermute(tiles, 'node', [(i, i ^ r) for i in range(4)])]
    ppermute x3, waiting for transfers between devices: 0.99 us -> 0.39 us  [neighbours(): lax.ppermute(up, axis, [(i, (i + 1) % size) for i in range(size)])]
  transfers between devices with their start and end apart: 15 -> 15, of which waited for: 7 -> 6; matrix products, arithmetic and copies ran while one was open for 0% -> 0% of each run, Pallas kernels for 11% -> 11%
where the time goes in v6:
time: 58.4 us; the launch traced here: 58.3 us
  starting transfers between devices  25.7 us (44%)
  waiting for transfers between devices  20.8 us (36%)
  Pallas kernels  11 us (19%)
  between operations  0.79 us (1%)
    ppermute x9, waiting for transfers between devices, send(): return lax.ppermute(tiles, 'node', [(i, i ^ r) for i in range(4)])  17.9 us
    ppermute x3, starting transfers between devices, neighbours(): lax.ppermute(up, axis, [(i, (i + 1) % size) for i in range(size)])  12.5 us
    ppermute x9, starting transfers between devices, send(): return lax.ppermute(tiles, 'node', [(i, i ^ r) for i in range(4)])  10.6 us
    ppermute x3, waiting for transfers between devices, neighbours(): lax.ppermute(down, axis, [((i + 1) % size, i) for i in range(size)])  2.59 us
    ppermute x3, starting transfers between devices, neighbours(): lax.ppermute(down, axis, [((i + 1) % size, i) for i in range(size)])  2.55 us
    pallas_call x1, Pallas kernels, shards(): call(start_kernel, [VMEM, VMEM, ANY], [tiles_of(20), tiles_of(2), shape(1...  1.95 us
    pallas_call x1, Pallas kernels, shards(): call(first_kernel, [VMEM, VMEM, ANY], [shape(256, 128)] * 4 + [shape(5, 1...  1.9 us
    pallas_call x1, Pallas kernels, shards(): call(second_kernel, [VMEM] * 12, [tiles_of(20)] * 4, [scratch(8, 4), scra...  1.81 us
  transfers between devices with their start and end apart: 15, of which 6 were waited for; matrix products, arithmetic and copies ran while one was open for 0% of the time, Pallas kernels for 11%

profile of v6, /device:TPU:37, one launch (start us, length us, event | category | flops | bytes accessed | tf_op | source)
XLA Modules:
  0.0 58.3 jit_solution(17847428325244495266)
XLA Ops:
  0.0 0.0 copy-start
  0.0 1.2 %shard_map.46 = (f32[5,40,128]{2,1,0:T(8,128)S(1)}, f32[5,40,128]{2,1,0:T(8,128)S(1)}, f32[2,16,128]{2,1,0:T(8,128)S(1)}) custom-call(s32[2,16,128]{2,1,0:T(8,128)} %flag_hbm.1, f32[5,16,16,128]{3,2,1,0:T(8,128)} %bitcast.4, f32[5,16,16,128]{3,2,1,0:T(8,128)} %w_ref.3), custom_call_target="tpu_custom_call" | custom-call | flops 1 | bytes 1 | tf_op jit(solution)/shard_map/pallas_call | solution.py:592
  1.2 0.0 copy-start.1
  1.3 6.1 %collective-permute-start.3 = (f32[5,40,128]{2,1,0:T(8,128)S(1)}, f32[5,40,128]{2,1,0:T(8,128)S(1)}, u32[]{:S(2)}, u32[]{:S(2)}) collective-permute-start(f32[5,40,128]{2,1,0:T(8,128)S(1)} %get-tuple-element.35), channel_id=1, source_target_pairs={{0,1},{1,2},{2,3},{3,4},{4,5},{5,6},{6,7},{7,0},{8,9},{9,10},{10,1... | collective-permute-start | bytes 307208 | tf_op jit(solution)/shard_map/ppermute | solution.py:584
  7.3 2.5 %collective-permute-start.4 = (f32[5,40,128]{2,1,0:T(8,128)S(1)}, f32[5,40,128]{2,1,0:T(8,128)S(1)}, u32[]{:S(2)}, u32[]{:S(2)}) collective-permute-start(f32[5,40,128]{2,1,0:T(8,128)S(1)} %get-tuple-element.36), channel_id=1, source_target_pairs={{1,0},{2,1},{3,2},{4,3},{5,4},{6,5},{7,6},{0,7},{9,8},{10,9},{11,1... | collective-permute-start | bytes 307208 | tf_op jit(solution)/shard_map/ppermute | solution.py:585
  10.5 0.0 copy-done
  10.6 1.9 %shard_map.47 = (f32[256,128]{1,0:T(8,128)S(1)}, f32[256,128]{1,0:T(8,128)S(1)}, f32[256,128]{1,0:T(8,128)S(1)}, f32[256,128]{1,0:T(8,128)S(1)}, f32[5,16,16,128]{3,2,1,0:T(8,128)S(1)}) custom-call(f32[8,128]{1,0:T(8,128)S(1)} %broadcast_in_dim.8.power_ref, f32[5,16,16,128]{3,2,1,0:T(8,128)S(1)} %bitcast.5, f32[2,16,128]{2,1,0:T(8,128)S(1)} %get-tuple-element.30._after.slip_ref), custom_call_target="tpu_custom_call" | custom-call | flops 1 | bytes 1 | tf_op jit(solution)/shard_map/pallas_call | solution.py:599
  12.5 2.0 %collective-permute-start = (f32[256,128]{1,0:T(8,128)S(1)}, f32[256,128]{1,0:T(8,128)S(1)}, u32[]{:S(2)}, u32[]{:S(2)}) collective-permute-start(f32[256,128]{1,0:T(8,128)S(1)} %get-tuple-element.31._after), channel_id=1, source_target_pairs={{0,128},{64,192},{128,0},{192,64},{1,129},{65,193},{129,1},{193,65... | collective-permute-start | bytes 393224 | tf_op jit(solution)/shard_map/ppermute | solution.py:589
  14.5 0.0 copy-done.1
  14.5 0.1 shard_map.49
  14.6 2.3 %collective-permute-start.7 = (f32[13,16,128]{2,1,0:T(8,128)S(1)}, f32[13,16,128]{2,1,0:T(8,128)S(1)}, u32[]{:S(2)}, u32[]{:S(2)}) collective-permute-start(f32[13,16,128]{2,1,0:T(8,128)S(1)} %get-tuple-element.39), channel_id=1, source_target_pairs={{0,8},{8,16},{16,24},{24,32},{32,40},{40,48},{48,56},{56,0},{1,9},... | collective-permute-start | bytes 319496 | tf_op jit(solution)/shard_map/ppermute | solution.py:584
  16.9 0.0 collective-permute-start.8
  16.9 0.0 collective-permute-done.3.slow_ref
  16.9 0.0 collective-permute-start.1
  16.9 0.0 collective-permute-done.4.shigh_ref
  16.9 1.3 %collective-permute-start.2 = (f32[256,128]{1,0:T(8,128)S(1)}, f32[256,128]{1,0:T(8,128)S(1)}, u32[]{:S(2)}, u32[]{:S(2)}) collective-permute-start(f32[256,128]{1,0:T(8,128)S(1)} %get-tuple-element.34), channel_id=1, source_target_pairs={{0,64},{64,0},{128,192},{192,128},{1,65},{65,1},{129,193},{193,129... | collective-permute-start | bytes 393224 | tf_op jit(solution)/shard_map/ppermute | solution.py:589
  18.3 0.4 collective-permute-done.7.tlow_ref
  18.6 4.1 %collective-permute-start.5 = (f32[16,128]{1,0:T(8,128)S(1)}, f32[16,128]{1,0:T(8,128)S(1)}, u32[]{:S(2)}, u32[]{:S(2)}) collective-permute-start(f32[16,128]{1,0:T(8,128)S(1)} %get-tuple-element.37), channel_id=1, source_target_pairs={{0,8},{8,16},{16,24},{24,32},{32,40},{40,48},{48,56},{56,0},{1,9},... | collective-permute-start | bytes 24584 | tf_op jit(solution)/shard_map/ppermute | solution.py:584
  22.8 0.0 collective-permute-done.8.thigh_ref
  22.8 0.0 collective-permute-start.6
  22.8 0.7 %shard_map.50 = (f32[4,7,16,128]{3,2,1,0:T(8,128)S(1)}, f32[8,8,16,128]{3,2,1,0:T(8,128)S(1)}) custom-call(f32[8,128]{1,0:T(8,128)S(1)} %broadcast_in_dim.8.power_ref, f32[5,256,128]{2,1,0:T(8,128)S(1)} %bitcast.7, f32[13,16,128]{2,1,0:T(8,128)S(1)} %collective-permute-done.7.tlow_ref, f32[13,16,128]{2,1,0:T(8,128)S(1)} %collective-permute-done.8.thigh_ref, ...), custom_call_target="tpu_custom_call" | custom-call | flops 1 | bytes 1 | tf_op jit(solution)/shard_map/pallas_call | solution.py:607
  23.5 0.0 collective-permute-done.5.clow_ref
  23.6 2.6 %collective-permute-done.6.chigh_ref = f32[16,128]{1,0:T(8,128)S(1)} collective-permute-done((f32[16,128]{1,0:T(8,128)S(1)}, f32[16,128]{1,0:T(8,128)S(1)}, u32[]{:S(2)}, u32[]{:S(2)}) %collective-permute-start.6) | collective-permute-done | bytes 8224 | tf_op jit(solution)/shard_map/ppermute | solution.py:585
  26.1 1.5 %shard_map.51 = (f32[12,16,128]{2,1,0:T(8,128)S(1)}, f32[12,16,128]{2,1,0:T(8,128)S(1)}, f32[12,16,128]{2,1,0:T(8,128)S(1)}, f32[12,16,128]{2,1,0:T(8,128)S(1)}) custom-call(f32[8,128]{1,0:T(8,128)S(1)} %broadcast_in_dim.8.power_ref, f32[5,256,128]{2,1,0:T(8,128)S(1)} %bitcast.8, f32[5,40,128]{2,1,0:T(8,128)S(1)} %collective-permute-done.3.slow_ref, ...), custom_call_target="tpu_custom_call" | custom-call | flops 1 | bytes 1 | tf_op jit(solution)/shard_map/pallas_call | solution.py:612
  27.6 0.1 collective-permute-start.10
  27.7 0.9 %collective-permute-start.11 = (f32[12,16,128]{2,1,0:T(8,128)S(1)}, f32[12,16,128]{2,1,0:T(8,128)S(1)}, u32[]{:S(2)}, u32[]{:S(2)}) collective-permute-start(f32[12,16,128]{2,1,0:T(8,128)S(1)} %get-tuple-element.47), channel_id=1, source_target_pairs={{0,192},{64,128},{128,64},{192,0},{1,193},{65,129},{129,65},{193,1... | collective-permute-start | bytes 294920 | tf_op jit(solution)/shard_map/ppermute | solution.py:589
  28.6 0.0 collective-permute-done.a2
  28.6 2.6 %collective-permute-start.9 = (f32[12,16,128]{2,1,0:T(8,128)S(1)}, f32[12,16,128]{2,1,0:T(8,128)S(1)}, u32[]{:S(2)}, u32[]{:S(2)}) collective-permute-start(f32[12,16,128]{2,1,0:T(8,128)S(1)} %get-tuple-element.45), channel_id=1, source_target_pairs={{0,64},{64,0},{128,192},{192,128},{1,65},{65,1},{129,193},{193,129... | collective-permute-start | bytes 294920 | tf_op jit(solution)/shard_map/ppermute | solution.py:589
  31.3 2.0 %shard_map.52 = (f32[20,16,128]{2,1,0:T(8,128)S(1)}, f32[2,16,128]{2,1,0:T(8,128)S(1)}, f32[16,128]{1,0:T(8,128)S(1)}) custom-call(f32[5,16,16,128]{3,2,1,0:T(8,128)S(1)} %copy-done.1, f32[2,16,128]{2,1,0:T(8,128)S(1)} %get-tuple-element.30._after.slip_ref, f32[12,16,128]{2,1,0:T(8,128)S(1)} %get-tuple-element.46._after), custom_call_target="tpu_custom_call" | custom-call | flops 1 | bytes 1 | tf_op jit(solution)/shard_map/pallas_call | solution.py:618
  33.2 0.1 shard_map.53.wxy_ref
  33.3 0.0 collective-permute-done.1.a3
  33.3 0.0 collective-permute-done.2.a1
  33.3 1.3 %collective-permute-done.10.b2 = f32[12,16,128]{2,1,0:T(8,128)S(1)} collective-permute-done((f32[12,16,128]{2,1,0:T(8,128)S(1)}, f32[12,16,128]{2,1,0:T(8,128)S(1)}, u32[]{:S(2)}, u32[]{:S(2)}) %collective-permute-start.10) | collective-permute-done | bytes 98336 | tf_op jit(solution)/shard_map/ppermute | solution.py:589
  34.7 2.8 %collective-permute-done.11.b3 = f32[12,16,128]{2,1,0:T(8,128)S(1)} collective-permute-done((f32[12,16,128]{2,1,0:T(8,128)S(1)}, f32[12,16,128]{2,1,0:T(8,128)S(1)}, u32[]{:S(2)}, u32[]{:S(2)}) %collective-permute-start.11) | collective-permute-done | bytes 98336 | tf_op jit(solution)/shard_map/ppermute | solution.py:589
  37.4 0.0 collective-permute-done.9.b1
  37.5 1.8 %shard_map.54 = (f32[20,16,128]{2,1,0:T(8,128)S(1)}, f32[20,16,128]{2,1,0:T(8,128)S(1)}, f32[20,16,128]{2,1,0:T(8,128)S(1)}, f32[20,16,128]{2,1,0:T(8,128)S(1)}) custom-call(f32[256,128]{1,0:T(8,128)S(1)} %collective-permute-done.a2, f32[256,128]{1,0:T(8,128)S(1)} %collective-permute-done.1.a3, f32[8,128]{1,0:T(8,128)S(1)} %broadcast_in_dim.8.power_ref, ...), custom_call_target="tpu_custom_call" | custom-call | flops 1 | bytes 1 | tf_op jit(solution)/shard_map/pallas_call | solution.py:622
  39.3 1.1 %collective-permute-start.12 = (f32[20,16,128]{2,1,0:T(8,128)S(1)}, f32[20,16,128]{2,1,0:T(8,128)S(1)}, u32[]{:S(2)}, u32[]{:S(2)}) collective-permute-start(f32[20,16,128]{2,1,0:T(8,128)S(1)} %get-tuple-element.51), channel_id=1, source_target_pairs={{0,128},{64,192},{128,0},{192,64},{1,129},{65,193},{129,1},{193,65... | collective-permute-start | bytes 491528 | tf_op jit(solution)/shard_map/ppermute | solution.py:589
  40.4 1.2 %collective-permute-start.13 = (f32[20,16,128]{2,1,0:T(8,128)S(1)}, f32[20,16,128]{2,1,0:T(8,128)S(1)}, u32[]{:S(2)}, u32[]{:S(2)}) collective-permute-start(f32[20,16,128]{2,1,0:T(8,128)S(1)} %get-tuple-element.52), channel_id=1, source_target_pairs={{0,192},{64,128},{128,64},{192,0},{1,193},{65,129},{129,65},{193,1... | collective-permute-start | bytes 491528 | tf_op jit(solution)/shard_map/ppermute | solution.py:589
  41.6 1.3 %collective-permute-start.14 = (f32[20,16,128]{2,1,0:T(8,128)S(1)}, f32[20,16,128]{2,1,0:T(8,128)S(1)}, u32[]{:S(2)}, u32[]{:S(2)}) collective-permute-start(f32[20,16,128]{2,1,0:T(8,128)S(1)} %get-tuple-element.53), channel_id=1, source_target_pairs={{0,64},{64,0},{128,192},{192,128},{1,65},{65,1},{129,193},{193,129... | collective-permute-start | bytes 491528 | tf_op jit(solution)/shard_map/ppermute | solution.py:589
  42.9 7.6 %collective-permute-done.12.r2 = f32[20,16,128]{2,1,0:T(8,128)S(1)} collective-permute-done((f32[20,16,128]{2,1,0:T(8,128)S(1)}, f32[20,16,128]{2,1,0:T(8,128)S(1)}, u32[]{:S(2)}, u32[]{:S(2)}) %collective-permute-start.12) | collective-permute-done | bytes 163872 | tf_op jit(solution)/shard_map/ppermute | solution.py:589
  50.5 6.1 %collective-permute-done.13.r3 = f32[20,16,128]{2,1,0:T(8,128)S(1)} collective-permute-done((f32[20,16,128]{2,1,0:T(8,128)S(1)}, f32[20,16,128]{2,1,0:T(8,128)S(1)}, u32[]{:S(2)}, u32[]{:S(2)}) %collective-permute-start.13) | collective-permute-done | bytes 163872 | tf_op jit(solution)/shard_map/ppermute | solution.py:589
  56.6 0.0 collective-permute-done.14.r1
  56.6 1.6 %shard_map.55 = f32[5,16,16,128]{3,2,1,0:T(8,128)} custom-call(f32[20,16,128]{2,1,0:T(8,128)S(1)} %collective-permute-done.12.r2, f32[20,16,128]{2,1,0:T(8,128)S(1)} %collective-permute-done.13.r3, f32[20,16,128]{2,1,0:T(8,128)S(1)} %collective-permute-done.14.r1, f32[20,16,128]{2,1,0:T(8,128)S(1)} %get-tuple-element.54.r0), custom_call_target="tpu_custom_call" | custom-call | flops 1 | bytes 1 | tf_op jit(solution)/shard_map/pallas_call | solution.py:628
  (2 shorter events, 0.0 us)
Async XLA Ops:
  0.0 10.6 %copy-start = (f32[1,5,16,16,128]{4,3,2,1,0:T(8,128)S(1)}, f32[1,5,16,16,128]{4,3,2,1,0:T(8,128)}, u32[]{:S(2)}) copy-start(f32[1,5,16,16,128]{4,3,2,1,0:T(8,128)} %param.5) | copy-start | bytes 1966084
  1.2 13.2 %copy-start.1 = (f32[5,16,16,128]{3,2,1,0:T(8,128)S(1)}, f32[5,16,16,128]{3,2,1,0:T(8,128)}, u32[]{:S(2)}) copy-start(f32[5,16,16,128]{3,2,1,0:T(8,128)} %w_ref.3) | copy-start | bytes 1966084
  1.3 15.7 %collective-permute-start.3 = (f32[5,40,128]{2,1,0:T(8,128)S(1)}, f32[5,40,128]{2,1,0:T(8,128)S(1)}, u32[]{:S(2)}, u32[]{:S(2)}) collective-permute-start(f32[5,40,128]{2,1,0:T(8,128)S(1)} %get-tuple-element.35), channel_id=1, source_target_pairs={{0,1},{1,2},{2,3},{3,4},{4,5},{5,6},{6,7},{7,0},{8,9},{9,10},{10,1... | collective-permute-start | bytes 307208 | tf_op jit(solution)/shard_map/ppermute | solution.py:584
  7.3 9.6 %collective-permute-start.4 = (f32[5,40,128]{2,1,0:T(8,128)S(1)}, f32[5,40,128]{2,1,0:T(8,128)S(1)}, u32[]{:S(2)}, u32[]{:S(2)}) collective-permute-start(f32[5,40,128]{2,1,0:T(8,128)S(1)} %get-tuple-element.36), channel_id=1, source_target_pairs={{1,0},{2,1},{3,2},{4,3},{5,4},{6,5},{7,6},{0,7},{9,8},{10,9},{11,1... | collective-permute-start | bytes 307208 | tf_op jit(solution)/shard_map/ppermute | solution.py:585
  12.5 16.2 %collective-permute-start = (f32[256,128]{1,0:T(8,128)S(1)}, f32[256,128]{1,0:T(8,128)S(1)}, u32[]{:S(2)}, u32[]{:S(2)}) collective-permute-start(f32[256,128]{1,0:T(8,128)S(1)} %get-tuple-element.31._after), channel_id=1, source_target_pairs={{0,128},{64,192},{128,0},{192,64},{1,129},{65,193},{129,1},{193,65... | collective-permute-start | bytes 393224 | tf_op jit(solution)/shard_map/ppermute | solution.py:589
  14.6 4.0 %collective-permute-start.7 = (f32[13,16,128]{2,1,0:T(8,128)S(1)}, f32[13,16,128]{2,1,0:T(8,128)S(1)}, u32[]{:S(2)}, u32[]{:S(2)}) collective-permute-start(f32[13,16,128]{2,1,0:T(8,128)S(1)} %get-tuple-element.39), channel_id=1, source_target_pairs={{0,8},{8,16},{16,24},{24,32},{32,40},{40,48},{48,56},{56,0},{1,9},... | collective-permute-start | bytes 319496 | tf_op jit(solution)/shard_map/ppermute | solution.py:584
  16.9 5.9 %collective-permute-start.8 = (f32[13,16,128]{2,1,0:T(8,128)S(1)}, f32[13,16,128]{2,1,0:T(8,128)S(1)}, u32[]{:S(2)}, u32[]{:S(2)}) collective-permute-start(f32[13,16,128]{2,1,0:T(8,128)S(1)} %get-tuple-element.40), channel_id=1, source_target_pairs={{8,0},{16,8},{24,16},{32,24},{40,32},{48,40},{56,48},{0,56},{9,1},... | collective-permute-start | bytes 319496 | tf_op jit(solution)/shard_map/ppermute | solution.py:585
  16.9 16.4 %collective-permute-start.1 = (f32[256,128]{1,0:T(8,128)S(1)}, f32[256,128]{1,0:T(8,128)S(1)}, u32[]{:S(2)}, u32[]{:S(2)}) collective-permute-start(f32[256,128]{1,0:T(8,128)S(1)} %get-tuple-element.32), channel_id=1, source_target_pairs={{0,192},{64,128},{128,64},{192,0},{1,193},{65,129},{129,65},{193,1... | collective-permute-start | bytes 393224 | tf_op jit(solution)/shard_map/ppermute | solution.py:589
  16.9 16.4 %collective-permute-start.2 = (f32[256,128]{1,0:T(8,128)S(1)}, f32[256,128]{1,0:T(8,128)S(1)}, u32[]{:S(2)}, u32[]{:S(2)}) collective-permute-start(f32[256,128]{1,0:T(8,128)S(1)} %get-tuple-element.34), channel_id=1, source_target_pairs={{0,64},{64,0},{128,192},{192,128},{1,65},{65,1},{129,193},{193,129... | collective-permute-start | bytes 393224 | tf_op jit(solution)/shard_map/ppermute | solution.py:589
  18.6 4.9 %collective-permute-start.5 = (f32[16,128]{1,0:T(8,128)S(1)}, f32[16,128]{1,0:T(8,128)S(1)}, u32[]{:S(2)}, u32[]{:S(2)}) collective-permute-start(f32[16,128]{1,0:T(8,128)S(1)} %get-tuple-element.37), channel_id=1, source_target_pairs={{0,8},{8,16},{16,24},{24,32},{32,40},{40,48},{48,56},{56,0},{1,9},... | collective-permute-start | bytes 24584 | tf_op jit(solution)/shard_map/ppermute | solution.py:584
  22.8 3.4 %collective-permute-start.6 = (f32[16,128]{1,0:T(8,128)S(1)}, f32[16,128]{1,0:T(8,128)S(1)}, u32[]{:S(2)}, u32[]{:S(2)}) collective-permute-start(f32[16,128]{1,0:T(8,128)S(1)} %get-tuple-element.38), channel_id=1, source_target_pairs={{8,0},{16,8},{24,16},{32,24},{40,32},{48,40},{56,48},{0,56},{9,1},... | collective-permute-start | bytes 24584 | tf_op jit(solution)/shard_map/ppermute | solution.py:585
  27.6 7.0 %collective-permute-start.10 = (f32[12,16,128]{2,1,0:T(8,128)S(1)}, f32[12,16,128]{2,1,0:T(8,128)S(1)}, u32[]{:S(2)}, u32[]{:S(2)}) collective-permute-start(f32[12,16,128]{2,1,0:T(8,128)S(1)} %get-tuple-element.46._after), channel_id=1, source_target_pairs={{0,128},{64,192},{128,0},{192,64},{1,129},{65,193},{129,1},{193,65... | collective-permute-start | bytes 294920 | tf_op jit(solution)/shard_map/ppermute | solution.py:589
  27.7 9.7 %collective-permute-start.11 = (f32[12,16,128]{2,1,0:T(8,128)S(1)}, f32[12,16,128]{2,1,0:T(8,128)S(1)}, u32[]{:S(2)}, u32[]{:S(2)}) collective-permute-start(f32[12,16,128]{2,1,0:T(8,128)S(1)} %get-tuple-element.47), channel_id=1, source_target_pairs={{0,192},{64,128},{128,64},{192,0},{1,193},{65,129},{129,65},{193,1... | collective-permute-start | bytes 294920 | tf_op jit(solution)/shard_map/ppermute | solution.py:589
  28.6 8.8 %collective-permute-start.9 = (f32[12,16,128]{2,1,0:T(8,128)S(1)}, f32[12,16,128]{2,1,0:T(8,128)S(1)}, u32[]{:S(2)}, u32[]{:S(2)}) collective-permute-start(f32[12,16,128]{2,1,0:T(8,128)S(1)} %get-tuple-element.45), channel_id=1, source_target_pairs={{0,64},{64,0},{128,192},{192,128},{1,65},{65,1},{129,193},{193,129... | collective-permute-start | bytes 294920 | tf_op jit(solution)/shard_map/ppermute | solution.py:589
  39.3 11.3 %collective-permute-start.12 = (f32[20,16,128]{2,1,0:T(8,128)S(1)}, f32[20,16,128]{2,1,0:T(8,128)S(1)}, u32[]{:S(2)}, u32[]{:S(2)}) collective-permute-start(f32[20,16,128]{2,1,0:T(8,128)S(1)} %get-tuple-element.51), channel_id=1, source_target_pairs={{0,128},{64,192},{128,0},{192,64},{1,129},{65,193},{129,1},{193,65... | collective-permute-start | bytes 491528 | tf_op jit(solution)/shard_map/ppermute | solution.py:589
  40.4 16.3 %collective-permute-start.13 = (f32[20,16,128]{2,1,0:T(8,128)S(1)}, f32[20,16,128]{2,1,0:T(8,128)S(1)}, u32[]{:S(2)}, u32[]{:S(2)}) collective-permute-start(f32[20,16,128]{2,1,0:T(8,128)S(1)} %get-tuple-element.52), channel_id=1, source_target_pairs={{0,192},{64,128},{128,64},{192,0},{1,193},{65,129},{129,65},{193,1... | collective-permute-start | bytes 491528 | tf_op jit(solution)/shard_map/ppermute | solution.py:589
  41.6 15.1 %collective-permute-start.14 = (f32[20,16,128]{2,1,0:T(8,128)S(1)}, f32[20,16,128]{2,1,0:T(8,128)S(1)}, u32[]{:S(2)}, u32[]{:S(2)}) collective-permute-start(f32[20,16,128]{2,1,0:T(8,128)S(1)} %get-tuple-element.53), channel_id=1, source_target_pairs={{0,64},{64,0},{128,192},{192,128},{1,65},{65,1},{129,193},{193,129... | collective-permute-start | bytes 491528 | tf_op jit(solution)/shard_map/ppermute | solution.py:589

commit v7 on v6

--- a/solution.py
+++ b/solution.py
@@ -526,7 +526,7 @@
                 rates[m, f * 4 + xq] = out[f]
         return _
 
-    lax.fori_loop(0, 4, node, 0, unroll=2)
+    lax.fori_loop(0, 4, node, 0, unroll=4)
 
     def combine(k, _):
         have = [rates[r, k] for r in range(4)]

time: 58.4 us -> 58.4 us (level)
  no operation moved by 1% of the time
where the time goes in v7:
time: 58.4 us; the launch traced here: 58.3 us
  starting transfers between devices  25.7 us (44%)
  waiting for transfers between devices  20.9 us (36%)
  Pallas kernels  10.9 us (19%)
  between operations  0.79 us (1%)
    ppermute x9, waiting for transfers between devices, send(): return lax.ppermute(tiles, 'node', [(i, i ^ r) for i in range(4)])  17.9 us
    ppermute x3, starting transfers between devices, neighbours(): lax.ppermute(up, axis, [(i, (i + 1) % size) for i in range(size)])  12.5 us
    ppermute x9, starting transfers between devices, send(): return lax.ppermute(tiles, 'node', [(i, i ^ r) for i in range(4)])  10.6 us
    ppermute x3, waiting for transfers between devices, neighbours(): lax.ppermute(down, axis, [((i + 1) % size, i) for i in range(size)])  2.59 us
    ppermute x3, starting transfers between devices, neighbours(): lax.ppermute(down, axis, [((i + 1) % size, i) for i in range(size)])  2.55 us
    pallas_call x1, Pallas kernels, shards(): call(start_kernel, [VMEM, VMEM, ANY], [tiles_of(20), tiles_of(2), shape(1...  1.95 us
    pallas_call x1, Pallas kernels, shards(): call(first_kernel, [VMEM, VMEM, ANY], [shape(256, 128)] * 4 + [shape(5, 1...  1.9 us
    pallas_call x1, Pallas kernels, shards(): call(second_kernel, [VMEM] * 12, [tiles_of(20)] * 4, [scratch(8, 4), scra...  1.77 us
  transfers between devices with their start and end apart: 15, of which 6 were waited for; matrix products, arithmetic and copies ran while one was open for 0% of the time, Pallas kernels for 11%

profile of v7, /device:TPU:37, one launch (start us, length us, event | category | flops | bytes accessed | tf_op | source)
XLA Modules:
  0.0 58.3 jit_solution(4836047454612146585)
XLA Ops:
  0.0 0.0 copy-start
  0.0 1.2 %shard_map.46 = (f32[5,40,128]{2,1,0:T(8,128)S(1)}, f32[5,40,128]{2,1,0:T(8,128)S(1)}, f32[2,16,128]{2,1,0:T(8,128)S(1)}) custom-call(s32[2,16,128]{2,1,0:T(8,128)} %flag_hbm.1, f32[5,16,16,128]{3,2,1,0:T(8,128)} %bitcast.4, f32[5,16,16,128]{3,2,1,0:T(8,128)} %w_ref.3), custom_call_target="tpu_custom_call" | custom-call | flops 1 | bytes 1 | tf_op jit(solution)/shard_map/pallas_call | solution.py:592
  1.2 0.0 copy-start.1
  1.3 6.1 %collective-permute-start.3 = (f32[5,40,128]{2,1,0:T(8,128)S(1)}, f32[5,40,128]{2,1,0:T(8,128)S(1)}, u32[]{:S(2)}, u32[]{:S(2)}) collective-permute-start(f32[5,40,128]{2,1,0:T(8,128)S(1)} %get-tuple-element.35), channel_id=1, source_target_pairs={{0,1},{1,2},{2,3},{3,4},{4,5},{5,6},{6,7},{7,0},{8,9},{9,10},{10,1... | collective-permute-start | bytes 307208 | tf_op jit(solution)/shard_map/ppermute | solution.py:584
  7.3 2.5 %collective-permute-start.4 = (f32[5,40,128]{2,1,0:T(8,128)S(1)}, f32[5,40,128]{2,1,0:T(8,128)S(1)}, u32[]{:S(2)}, u32[]{:S(2)}) collective-permute-start(f32[5,40,128]{2,1,0:T(8,128)S(1)} %get-tuple-element.36), channel_id=1, source_target_pairs={{1,0},{2,1},{3,2},{4,3},{5,4},{6,5},{7,6},{0,7},{9,8},{10,9},{11,1... | collective-permute-start | bytes 307208 | tf_op jit(solution)/shard_map/ppermute | solution.py:585
  10.5 0.0 copy-done
  10.6 1.9 %shard_map.47 = (f32[256,128]{1,0:T(8,128)S(1)}, f32[256,128]{1,0:T(8,128)S(1)}, f32[256,128]{1,0:T(8,128)S(1)}, f32[256,128]{1,0:T(8,128)S(1)}, f32[5,16,16,128]{3,2,1,0:T(8,128)S(1)}) custom-call(f32[8,128]{1,0:T(8,128)S(1)} %broadcast_in_dim.8.power_ref, f32[5,16,16,128]{3,2,1,0:T(8,128)S(1)} %bitcast.5, f32[2,16,128]{2,1,0:T(8,128)S(1)} %get-tuple-element.30._after.slip_ref), custom_call_target="tpu_custom_call" | custom-call | flops 1 | bytes 1 | tf_op jit(solution)/shard_map/pallas_call | solution.py:599
  12.5 2.0 %collective-permute-start = (f32[256,128]{1,0:T(8,128)S(1)}, f32[256,128]{1,0:T(8,128)S(1)}, u32[]{:S(2)}, u32[]{:S(2)}) collective-permute-start(f32[256,128]{1,0:T(8,128)S(1)} %get-tuple-element.31._after), channel_id=1, source_target_pairs={{0,128},{64,192},{128,0},{192,64},{1,129},{65,193},{129,1},{193,65... | collective-permute-start | bytes 393224 | tf_op jit(solution)/shard_map/ppermute | solution.py:589
  14.5 0.0 copy-done.1
  14.5 0.1 shard_map.49
  14.6 2.3 %collective-permute-start.7 = (f32[13,16,128]{2,1,0:T(8,128)S(1)}, f32[13,16,128]{2,1,0:T(8,128)S(1)}, u32[]{:S(2)}, u32[]{:S(2)}) collective-permute-start(f32[13,16,128]{2,1,0:T(8,128)S(1)} %get-tuple-element.39), channel_id=1, source_target_pairs={{0,8},{8,16},{16,24},{24,32},{32,40},{40,48},{48,56},{56,0},{1,9},... | collective-permute-start | bytes 319496 | tf_op jit(solution)/shard_map/ppermute | solution.py:584
  16.9 0.0 collective-permute-start.8
  16.9 0.0 collective-permute-done.3.slow_ref
  16.9 0.0 collective-permute-start.1
  16.9 0.0 collective-permute-done.4.shigh_ref
  16.9 1.3 %collective-permute-start.2 = (f32[256,128]{1,0:T(8,128)S(1)}, f32[256,128]{1,0:T(8,128)S(1)}, u32[]{:S(2)}, u32[]{:S(2)}) collective-permute-start(f32[256,128]{1,0:T(8,128)S(1)} %get-tuple-element.34), channel_id=1, source_target_pairs={{0,64},{64,0},{128,192},{192,128},{1,65},{65,1},{129,193},{193,129... | collective-permute-start | bytes 393224 | tf_op jit(solution)/shard_map/ppermute | solution.py:589
  18.3 0.4 collective-permute-done.7.tlow_ref
  18.6 4.1 %collective-permute-start.5 = (f32[16,128]{1,0:T(8,128)S(1)}, f32[16,128]{1,0:T(8,128)S(1)}, u32[]{:S(2)}, u32[]{:S(2)}) collective-permute-start(f32[16,128]{1,0:T(8,128)S(1)} %get-tuple-element.37), channel_id=1, source_target_pairs={{0,8},{8,16},{16,24},{24,32},{32,40},{40,48},{48,56},{56,0},{1,9},... | collective-permute-start | bytes 24584 | tf_op jit(solution)/shard_map/ppermute | solution.py:584
  22.8 0.0 collective-permute-done.8.thigh_ref
  22.8 0.0 collective-permute-start.6
  22.8 0.7 %shard_map.50 = (f32[4,7,16,128]{3,2,1,0:T(8,128)S(1)}, f32[8,8,16,128]{3,2,1,0:T(8,128)S(1)}) custom-call(f32[8,128]{1,0:T(8,128)S(1)} %broadcast_in_dim.8.power_ref, f32[5,256,128]{2,1,0:T(8,128)S(1)} %bitcast.7, f32[13,16,128]{2,1,0:T(8,128)S(1)} %collective-permute-done.7.tlow_ref, f32[13,16,128]{2,1,0:T(8,128)S(1)} %collective-permute-done.8.thigh_ref, ...), custom_call_target="tpu_custom_call" | custom-call | flops 1 | bytes 1 | tf_op jit(solution)/shard_map/pallas_call | solution.py:607
  23.5 0.0 collective-permute-done.5.clow_ref
  23.6 2.6 %collective-permute-done.6.chigh_ref = f32[16,128]{1,0:T(8,128)S(1)} collective-permute-done((f32[16,128]{1,0:T(8,128)S(1)}, f32[16,128]{1,0:T(8,128)S(1)}, u32[]{:S(2)}, u32[]{:S(2)}) %collective-permute-start.6) | collective-permute-done | bytes 8224 | tf_op jit(solution)/shard_map/ppermute | solution.py:585
  26.1 1.5 %shard_map.51 = (f32[12,16,128]{2,1,0:T(8,128)S(1)}, f32[12,16,128]{2,1,0:T(8,128)S(1)}, f32[12,16,128]{2,1,0:T(8,128)S(1)}, f32[12,16,128]{2,1,0:T(8,128)S(1)}) custom-call(f32[8,128]{1,0:T(8,128)S(1)} %broadcast_in_dim.8.power_ref, f32[5,256,128]{2,1,0:T(8,128)S(1)} %bitcast.8, f32[5,40,128]{2,1,0:T(8,128)S(1)} %collective-permute-done.3.slow_ref, ...), custom_call_target="tpu_custom_call" | custom-call | flops 1 | bytes 1 | tf_op jit(solution)/shard_map/pallas_call | solution.py:612
  27.6 0.1 collective-permute-start.10
  27.7 0.9 %collective-permute-start.11 = (f32[12,16,128]{2,1,0:T(8,128)S(1)}, f32[12,16,128]{2,1,0:T(8,128)S(1)}, u32[]{:S(2)}, u32[]{:S(2)}) collective-permute-start(f32[12,16,128]{2,1,0:T(8,128)S(1)} %get-tuple-element.47), channel_id=1, source_target_pairs={{0,192},{64,128},{128,64},{192,0},{1,193},{65,129},{129,65},{193,1... | collective-permute-start | bytes 294920 | tf_op jit(solution)/shard_map/ppermute | solution.py:589
  28.6 0.0 collective-permute-done.a2
  28.6 2.6 %collective-permute-start.9 = (f32[12,16,128]{2,1,0:T(8,128)S(1)}, f32[12,16,128]{2,1,0:T(8,128)S(1)}, u32[]{:S(2)}, u32[]{:S(2)}) collective-permute-start(f32[12,16,128]{2,1,0:T(8,128)S(1)} %get-tuple-element.45), channel_id=1, source_target_pairs={{0,64},{64,0},{128,192},{192,128},{1,65},{65,1},{129,193},{193,129... | collective-permute-start | bytes 294920 | tf_op jit(solution)/shard_map/ppermute | solution.py:589
  31.3 2.0 %shard_map.52 = (f32[20,16,128]{2,1,0:T(8,128)S(1)}, f32[2,16,128]{2,1,0:T(8,128)S(1)}, f32[16,128]{1,0:T(8,128)S(1)}) custom-call(f32[5,16,16,128]{3,2,1,0:T(8,128)S(1)} %copy-done.1, f32[2,16,128]{2,1,0:T(8,128)S(1)} %get-tuple-element.30._after.slip_ref, f32[12,16,128]{2,1,0:T(8,128)S(1)} %get-tuple-element.46._after), custom_call_target="tpu_custom_call" | custom-call | flops 1 | bytes 1 | tf_op jit(solution)/shard_map/pallas_call | solution.py:618
  33.2 0.1 shard_map.53.wxy_ref
  33.3 0.0 collective-permute-done.1.a3
  33.3 0.0 collective-permute-done.2.a1
  33.3 1.3 %collective-permute-done.10.b2 = f32[12,16,128]{2,1,0:T(8,128)S(1)} collective-permute-done((f32[12,16,128]{2,1,0:T(8,128)S(1)}, f32[12,16,128]{2,1,0:T(8,128)S(1)}, u32[]{:S(2)}, u32[]{:S(2)}) %collective-permute-start.10) | collective-permute-done | bytes 98336 | tf_op jit(solution)/shard_map/ppermute | solution.py:589
  34.7 2.8 %collective-permute-done.11.b3 = f32[12,16,128]{2,1,0:T(8,128)S(1)} collective-permute-done((f32[12,16,128]{2,1,0:T(8,128)S(1)}, f32[12,16,128]{2,1,0:T(8,128)S(1)}, u32[]{:S(2)}, u32[]{:S(2)}) %collective-permute-start.11) | collective-permute-done | bytes 98336 | tf_op jit(solution)/shard_map/ppermute | solution.py:589
  37.4 0.0 collective-permute-done.9.b1
  37.5 1.8 %shard_map.54 = (f32[20,16,128]{2,1,0:T(8,128)S(1)}, f32[20,16,128]{2,1,0:T(8,128)S(1)}, f32[20,16,128]{2,1,0:T(8,128)S(1)}, f32[20,16,128]{2,1,0:T(8,128)S(1)}) custom-call(f32[256,128]{1,0:T(8,128)S(1)} %collective-permute-done.a2, f32[256,128]{1,0:T(8,128)S(1)} %collective-permute-done.1.a3, f32[8,128]{1,0:T(8,128)S(1)} %broadcast_in_dim.8.power_ref, ...), custom_call_target="tpu_custom_call" | custom-call | flops 1 | bytes 1 | tf_op jit(solution)/shard_map/pallas_call | solution.py:622
  39.2 1.1 %collective-permute-start.12 = (f32[20,16,128]{2,1,0:T(8,128)S(1)}, f32[20,16,128]{2,1,0:T(8,128)S(1)}, u32[]{:S(2)}, u32[]{:S(2)}) collective-permute-start(f32[20,16,128]{2,1,0:T(8,128)S(1)} %get-tuple-element.51), channel_id=1, source_target_pairs={{0,128},{64,192},{128,0},{192,64},{1,129},{65,193},{129,1},{193,65... | collective-permute-start | bytes 491528 | tf_op jit(solution)/shard_map/ppermute | solution.py:589
  40.4 1.2 %collective-permute-start.13 = (f32[20,16,128]{2,1,0:T(8,128)S(1)}, f32[20,16,128]{2,1,0:T(8,128)S(1)}, u32[]{:S(2)}, u32[]{:S(2)}) collective-permute-start(f32[20,16,128]{2,1,0:T(8,128)S(1)} %get-tuple-element.52), channel_id=1, source_target_pairs={{0,192},{64,128},{128,64},{192,0},{1,193},{65,129},{129,65},{193,1... | collective-permute-start | bytes 491528 | tf_op jit(solution)/shard_map/ppermute | solution.py:589
  41.5 1.3 %collective-permute-start.14 = (f32[20,16,128]{2,1,0:T(8,128)S(1)}, f32[20,16,128]{2,1,0:T(8,128)S(1)}, u32[]{:S(2)}, u32[]{:S(2)}) collective-permute-start(f32[20,16,128]{2,1,0:T(8,128)S(1)} %get-tuple-element.53), channel_id=1, source_target_pairs={{0,64},{64,0},{128,192},{192,128},{1,65},{65,1},{129,193},{193,129... | collective-permute-start | bytes 491528 | tf_op jit(solution)/shard_map/ppermute | solution.py:589
  42.9 7.6 %collective-permute-done.12.r2 = f32[20,16,128]{2,1,0:T(8,128)S(1)} collective-permute-done((f32[20,16,128]{2,1,0:T(8,128)S(1)}, f32[20,16,128]{2,1,0:T(8,128)S(1)}, u32[]{:S(2)}, u32[]{:S(2)}) %collective-permute-start.12) | collective-permute-done | bytes 163872 | tf_op jit(solution)/shard_map/ppermute | solution.py:589
  50.5 6.1 %collective-permute-done.13.r3 = f32[20,16,128]{2,1,0:T(8,128)S(1)} collective-permute-done((f32[20,16,128]{2,1,0:T(8,128)S(1)}, f32[20,16,128]{2,1,0:T(8,128)S(1)}, u32[]{:S(2)}, u32[]{:S(2)}) %collective-permute-start.13) | collective-permute-done | bytes 163872 | tf_op jit(solution)/shard_map/ppermute | solution.py:589
  56.6 0.0 collective-permute-done.14.r1
  56.6 1.6 %shard_map.55 = f32[5,16,16,128]{3,2,1,0:T(8,128)} custom-call(f32[20,16,128]{2,1,0:T(8,128)S(1)} %collective-permute-done.12.r2, f32[20,16,128]{2,1,0:T(8,128)S(1)} %collective-permute-done.13.r3, f32[20,16,128]{2,1,0:T(8,128)S(1)} %collective-permute-done.14.r1, f32[20,16,128]{2,1,0:T(8,128)S(1)} %get-tuple-element.54.r0), custom_call_target="tpu_custom_call" | custom-call | flops 1 | bytes 1 | tf_op jit(solution)/shard_map/pallas_call | solution.py:628
  (2 shorter events, 0.0 us)
Async XLA Ops:
  0.0 10.6 %copy-start = (f32[1,5,16,16,128]{4,3,2,1,0:T(8,128)S(1)}, f32[1,5,16,16,128]{4,3,2,1,0:T(8,128)}, u32[]{:S(2)}) copy-start(f32[1,5,16,16,128]{4,3,2,1,0:T(8,128)} %param.5) | copy-start | bytes 1966084
  1.2 13.2 %copy-start.1 = (f32[5,16,16,128]{3,2,1,0:T(8,128)S(1)}, f32[5,16,16,128]{3,2,1,0:T(8,128)}, u32[]{:S(2)}) copy-start(f32[5,16,16,128]{3,2,1,0:T(8,128)} %w_ref.3) | copy-start | bytes 1966084
  1.3 15.7 %collective-permute-start.3 = (f32[5,40,128]{2,1,0:T(8,128)S(1)}, f32[5,40,128]{2,1,0:T(8,128)S(1)}, u32[]{:S(2)}, u32[]{:S(2)}) collective-permute-start(f32[5,40,128]{2,1,0:T(8,128)S(1)} %get-tuple-element.35), channel_id=1, source_target_pairs={{0,1},{1,2},{2,3},{3,4},{4,5},{5,6},{6,7},{7,0},{8,9},{9,10},{10,1... | collective-permute-start | bytes 307208 | tf_op jit(solution)/shard_map/ppermute | solution.py:584
  7.3 9.6 %collective-permute-start.4 = (f32[5,40,128]{2,1,0:T(8,128)S(1)}, f32[5,40,128]{2,1,0:T(8,128)S(1)}, u32[]{:S(2)}, u32[]{:S(2)}) collective-permute-start(f32[5,40,128]{2,1,0:T(8,128)S(1)} %get-tuple-element.36), channel_id=1, source_target_pairs={{1,0},{2,1},{3,2},{4,3},{5,4},{6,5},{7,6},{0,7},{9,8},{10,9},{11,1... | collective-permute-start | bytes 307208 | tf_op jit(solution)/shard_map/ppermute | solution.py:585
  12.5 16.2 %collective-permute-start = (f32[256,128]{1,0:T(8,128)S(1)}, f32[256,128]{1,0:T(8,128)S(1)}, u32[]{:S(2)}, u32[]{:S(2)}) collective-permute-start(f32[256,128]{1,0:T(8,128)S(1)} %get-tuple-element.31._after), channel_id=1, source_target_pairs={{0,128},{64,192},{128,0},{192,64},{1,129},{65,193},{129,1},{193,65... | collective-permute-start | bytes 393224 | tf_op jit(solution)/shard_map/ppermute | solution.py:589
  14.6 4.0 %collective-permute-start.7 = (f32[13,16,128]{2,1,0:T(8,128)S(1)}, f32[13,16,128]{2,1,0:T(8,128)S(1)}, u32[]{:S(2)}, u32[]{:S(2)}) collective-permute-start(f32[13,16,128]{2,1,0:T(8,128)S(1)} %get-tuple-element.39), channel_id=1, source_target_pairs={{0,8},{8,16},{16,24},{24,32},{32,40},{40,48},{48,56},{56,0},{1,9},... | collective-permute-start | bytes 319496 | tf_op jit(solution)/shard_map/ppermute | solution.py:584
  16.9 5.9 %collective-permute-start.8 = (f32[13,16,128]{2,1,0:T(8,128)S(1)}, f32[13,16,128]{2,1,0:T(8,128)S(1)}, u32[]{:S(2)}, u32[]{:S(2)}) collective-permute-start(f32[13,16,128]{2,1,0:T(8,128)S(1)} %get-tuple-element.40), channel_id=1, source_target_pairs={{8,0},{16,8},{24,16},{32,24},{40,32},{48,40},{56,48},{0,56},{9,1},... | collective-permute-start | bytes 319496 | tf_op jit(solution)/shard_map/ppermute | solution.py:585
  16.9 16.4 %collective-permute-start.1 = (f32[256,128]{1,0:T(8,128)S(1)}, f32[256,128]{1,0:T(8,128)S(1)}, u32[]{:S(2)}, u32[]{:S(2)}) collective-permute-start(f32[256,128]{1,0:T(8,128)S(1)} %get-tuple-element.32), channel_id=1, source_target_pairs={{0,192},{64,128},{128,64},{192,0},{1,193},{65,129},{129,65},{193,1... | collective-permute-start | bytes 393224 | tf_op jit(solution)/shard_map/ppermute | solution.py:589
  16.9 16.4 %collective-permute-start.2 = (f32[256,128]{1,0:T(8,128)S(1)}, f32[256,128]{1,0:T(8,128)S(1)}, u32[]{:S(2)}, u32[]{:S(2)}) collective-permute-start(f32[256,128]{1,0:T(8,128)S(1)} %get-tuple-element.34), channel_id=1, source_target_pairs={{0,64},{64,0},{128,192},{192,128},{1,65},{65,1},{129,193},{193,129... | collective-permute-start | bytes 393224 | tf_op jit(solution)/shard_map/ppermute | solution.py:589
  18.6 4.9 %collective-permute-start.5 = (f32[16,128]{1,0:T(8,128)S(1)}, f32[16,128]{1,0:T(8,128)S(1)}, u32[]{:S(2)}, u32[]{:S(2)}) collective-permute-start(f32[16,128]{1,0:T(8,128)S(1)} %get-tuple-element.37), channel_id=1, source_target_pairs={{0,8},{8,16},{16,24},{24,32},{32,40},{40,48},{48,56},{56,0},{1,9},... | collective-permute-start | bytes 24584 | tf_op jit(solution)/shard_map/ppermute | solution.py:584
  22.8 3.4 %collective-permute-start.6 = (f32[16,128]{1,0:T(8,128)S(1)}, f32[16,128]{1,0:T(8,128)S(1)}, u32[]{:S(2)}, u32[]{:S(2)}) collective-permute-start(f32[16,128]{1,0:T(8,128)S(1)} %get-tuple-element.38), channel_id=1, source_target_pairs={{8,0},{16,8},{24,16},{32,24},{40,32},{48,40},{56,48},{0,56},{9,1},... | collective-permute-start | bytes 24584 | tf_op jit(solution)/shard_map/ppermute | solution.py:585
  27.6 7.0 %collective-permute-start.10 = (f32[12,16,128]{2,1,0:T(8,128)S(1)}, f32[12,16,128]{2,1,0:T(8,128)S(1)}, u32[]{:S(2)}, u32[]{:S(2)}) collective-permute-start(f32[12,16,128]{2,1,0:T(8,128)S(1)} %get-tuple-element.46._after), channel_id=1, source_target_pairs={{0,128},{64,192},{128,0},{192,64},{1,129},{65,193},{129,1},{193,65... | collective-permute-start | bytes 294920 | tf_op jit(solution)/shard_map/ppermute | solution.py:589
  27.7 9.7 %collective-permute-start.11 = (f32[12,16,128]{2,1,0:T(8,128)S(1)}, f32[12,16,128]{2,1,0:T(8,128)S(1)}, u32[]{:S(2)}, u32[]{:S(2)}) collective-permute-start(f32[12,16,128]{2,1,0:T(8,128)S(1)} %get-tuple-element.47), channel_id=1, source_target_pairs={{0,192},{64,128},{128,64},{192,0},{1,193},{65,129},{129,65},{193,1... | collective-permute-start | bytes 294920 | tf_op jit(solution)/shard_map/ppermute | solution.py:589
  28.6 8.8 %collective-permute-start.9 = (f32[12,16,128]{2,1,0:T(8,128)S(1)}, f32[12,16,128]{2,1,0:T(8,128)S(1)}, u32[]{:S(2)}, u32[]{:S(2)}) collective-permute-start(f32[12,16,128]{2,1,0:T(8,128)S(1)} %get-tuple-element.45), channel_id=1, source_target_pairs={{0,64},{64,0},{128,192},{192,128},{1,65},{65,1},{129,193},{193,129... | collective-permute-start | bytes 294920 | tf_op jit(solution)/shard_map/ppermute | solution.py:589
  39.2 11.3 %collective-permute-start.12 = (f32[20,16,128]{2,1,0:T(8,128)S(1)}, f32[20,16,128]{2,1,0:T(8,128)S(1)}, u32[]{:S(2)}, u32[]{:S(2)}) collective-permute-start(f32[20,16,128]{2,1,0:T(8,128)S(1)} %get-tuple-element.51), channel_id=1, source_target_pairs={{0,128},{64,192},{128,0},{192,64},{1,129},{65,193},{129,1},{193,65... | collective-permute-start | bytes 491528 | tf_op jit(solution)/shard_map/ppermute | solution.py:589
  40.4 16.3 %collective-permute-start.13 = (f32[20,16,128]{2,1,0:T(8,128)S(1)}, f32[20,16,128]{2,1,0:T(8,128)S(1)}, u32[]{:S(2)}, u32[]{:S(2)}) collective-permute-start(f32[20,16,128]{2,1,0:T(8,128)S(1)} %get-tuple-element.52), channel_id=1, source_target_pairs={{0,192},{64,128},{128,64},{192,0},{1,193},{65,129},{129,65},{193,1... | collective-permute-start | bytes 491528 | tf_op jit(solution)/shard_map/ppermute | solution.py:589
  41.5 15.1 %collective-permute-start.14 = (f32[20,16,128]{2,1,0:T(8,128)S(1)}, f32[20,16,128]{2,1,0:T(8,128)S(1)}, u32[]{:S(2)}, u32[]{:S(2)}) collective-permute-start(f32[20,16,128]{2,1,0:T(8,128)S(1)} %get-tuple-element.53), channel_id=1, source_target_pairs={{0,64},{64,0},{128,192},{192,128},{1,65},{65,1},{129,193},{193,129... | collective-permute-start | bytes 491528 | tf_op jit(solution)/shard_map/ppermute | solution.py:589
